TPU v7x, 32 devices: a whole 2x2x4 slice. The times are simulated.
32 devices in a mesh: rows: 2 (over y), cols: 16 (over z, x, core).
Axes of the slice: x: 2, y: 2, z: 4, core: 2. Of those that a mesh axis runs over, the one named last changes fastest.
Arguments:
- covariance: float32 [2048, 2048], P('rows', 'cols'), may hold values from -6 to 6
- zonal: float32 [16, 128, 128], P('rows'), may hold values from -0.5 to 0.5
- stencil: float32 [16, 3, 128], P('rows'), may hold values from -0.5 to 1.1, as said below
Outputs:
- lagged: float32 [2048, 2048], P('rows', 'cols')
Inputs may be any that keep to these rules, and one draw needn't show every extreme that they name: `stencil`: component 0 lies in 0.7 to 1.1, components 1 and 2 in -0.5 to 0.5.
All inputs are finite; a program needn't handle non-finite values.
Results may differ from a plain program's by a relative error of at most 0.0003.
Values sent between devices are 32-bit elements; how exact they have to be, the bound alone decides.
No kernel may reach another device: no remote copies, remote signals or barrier semaphores. Data moves between devices by JAX's collectives and lax.ppermute only.
A program may use at most 64 MiB of HBM per device.

v0:
```python
import jax
import jax.numpy as jnp
from jax import lax
from jax.sharding import PartitionSpec as P

STEPS = 3
LAGS = 3


def from_root(value, axis, root):
    mine = lax.axis_index(axis) == root
    return lax.psum(jnp.where(mine, value, jnp.zeros_like(value)), axis)


def with_halo(block, sides, width):
    for axis, dim in sides:
        count = lax.axis_size(axis)
        forward = [(i, i + 1) for i in range(count - 1)]
        backward = [(target, source) for source, target in forward]
        low = lax.ppermute(
            lax.slice_in_dim(block, block.shape[dim] - width, None, axis=dim), axis, forward
        )
        high = lax.ppermute(lax.slice_in_dim(block, 0, width, axis=dim), axis, backward)
        block = jnp.concatenate([low, block, high], axis=dim)
    return block


def rows_local(extended, operator):
    latitudes = operator.shape[0]
    longitudes = operator.shape[2]
    zonal_mats = operator[:, :longitudes]
    weights = operator[:, longitudes:]
    blocks = extended.reshape(latitudes + 2, longitudes, extended.shape[1])
    mixed = (
        weights[:, 0, :, None] * blocks[1:-1]
        + weights[:, 1, :, None] * blocks[2:]
        + weights[:, 2, :, None] * blocks[:-2]
    )
    turned = jnp.einsum("lij,ljc->lic", zonal_mats, mixed, precision=lax.Precision.HIGHEST)
    return turned.reshape(latitudes * longitudes, extended.shape[1])


def cols_local(extended, operator):
    latitudes = operator.shape[0]
    longitudes = operator.shape[2]
    zonal_mats = operator[:, :longitudes]
    weights = operator[:, longitudes:]
    blocks = extended.reshape(extended.shape[0], latitudes + 2, longitudes)
    mixed = (
        weights[None, :, 0, :] * blocks[:, 1:-1]
        + weights[None, :, 1, :] * blocks[:, 2:]
        + weights[None, :, 2, :] * blocks[:, :-2]
    )
    turned = jnp.einsum("rlj,lij->rli", mixed, zonal_mats, precision=lax.Precision.HIGHEST)
    return turned.reshape(extended.shape[0], latitudes * longitudes)


def on_device(covariance, zonal, stencil):
    longitudes = zonal.shape[1]
    lat_rows = zonal.shape[0]
    row_count = lax.axis_size("rows")
    col_count = lax.axis_size("cols")
    ratio = col_count // row_count
    lat_cols = lat_rows // ratio
    operator = jnp.concatenate([zonal, stencil], axis=1)
    col_index = lax.axis_index("cols")
    owner = from_root(operator, "rows", col_index // ratio)
    col_operator = lax.dynamic_slice_in_dim(owner, col_index % ratio * lat_cols, lat_cols, 0)
    rim_width = max(STEPS, LAGS) - 1
    wide_operator = with_halo(operator, (("rows", 0),), rim_width)

    def left_phase(matrix, count):
        extended = with_halo(matrix, (("rows", 0),), count * longitudes)
        for inner in range(count):
            first = rim_width - (count - 1) + inner
            length = lat_rows + 2 * (count - 1 - inner)
            extended = rows_local(extended, wide_operator[first : first + length])
        return extended

    current = left_phase(covariance, STEPS)
    for repeat in range(STEPS):
        right_extended = with_halo(current, (("cols", 1),), longitudes)
        current = cols_local(right_extended, col_operator)
    tile_cols = current.shape[1]
    piece = tile_cols // row_count
    moved = lax.all_to_all(
        lax.all_to_all(current, "rows", split_axis=1, concat_axis=0, tiled=True),
        "cols",
        split_axis=0,
        concat_axis=1,
        tiled=True,
    )
    turned = moved.T.reshape(col_count, piece, tile_cols)
    settled = lax.all_to_all(turned, "rows", split_axis=0, concat_axis=1, tiled=True)
    current = settled.reshape(ratio * row_count * piece, tile_cols)
    current = left_phase(current, LAGS)
    return current


def solution(mesh):
    placed = (P("rows", "cols"), P("rows", None, None), P("rows", None, None))
    return jax.shard_map(
        on_device, mesh=mesh, in_specs=placed, out_specs=P("rows", "cols"), check_vma=False
    )
```

profile of v0, /device:TPU:0, one launch (start us, length us, event | category | flops | bytes accessed | tf_op | source)
XLA Modules:
  0.0 149.4 jit_solution(4234739313666691281)
XLA Ops:
  6.5 1.1 fusion.87
  7.6 1.3 collective-permute-start.3
  8.9 0.0 copy-start.2
  9.0 4.9 %collective-permute-start.2 = (f32[384,128]{1,0:T(8,128)S(1)}, f32[384,128]{1,0:T(8,128)S(1)}, u32[]{:S(2)}, u32[]{:S(2)}) collective-permute-start(f32[384,128]{1,0:T(8,128)S(1)} %get-tuple-element.25), channel_id=1, source_target_pairs={{0,16},{1,17},{2,18},{3,19},{4,20},{5,21},{6,22},{7,23},{8,24},{9,... | collective-permute-start | bytes 589832 | tf_op jit(solution)/shard_map/ppermute | solution.py:20
  14.0 1.3 collective-permute-start
  15.3 1.3 collective-permute-start.1
  16.6 0.9 broadcast_select_fusion
  17.5 0.0 all-reduce.2.cloned.1.call-update
  17.5 3.5 %collective-permute-done = f32[2,131,128]{2,1,0:T(8,128)S(1)} collective-permute-done((f32[2,131,128]{2,1,0:T(8,128)S(1)}, f32[2,131,128]{2,1,0:T(8,128)S(1)}, u32[]{:S(2)}, u32[]{:S(2)}) %collective-permute-start) | collective-permute-done | bytes 134176 | tf_op jit(solution)/shard_map/ppermute | solution.py:20
  21.0 1.3 collective-permute-done.1
  22.4 0.0 copy-start.1
  22.4 0.1 pad_maximum_fusion.1
  22.5 0.9 copy-done.1
  23.5 0.2 fusion.84
  23.7 1.9 %fusion.6 = f32[12,128,128]{2,1,0:T(8,128)S(1)} fusion(f32[12,128,128]{2,1,0:T(8,128)S(1)} %bitcast.116, f32[12,128,128]{2,1,0:T(8,128)S(1)} %bitcast.117, f32[12,128,128]{2,1,0:T(8,128)S(1)} %bitcast.115, f32[12,131,128]{2,1,0:T(8,128)S(1)} %pad_maximum_fusion.1, f32[12,128]{1,0:T(8,128)S(1)} %get-tuple-element.29, f32[12,128]{1,0:T(8,128)S(1)} %get-tuple-element.30, ...), kind=kOutput, calls=%fused_computation.8 | convolution fusion | flops 302972928 | bytes 3956736 | tf_op jit(solution)/shard_map/lij,ljc->lic/dot_general | solution.py:39
  25.6 1.4 fusion.20
  27.0 1.2 fusion.32
  28.2 0.2 copy.24
  28.4 1.3 collective-permute-start.5
  29.7 1.3 collective-permute-start.4
  31.0 19.4 %all-reduce.2.cloned.1.call-done = f32[8,131,128]{2,1,0:T(8,128)} async-done(((f32[8,131,128]{2,1,0:T(8,128)}), f32[8,131,128]{2,1,0:T(8,128)}) %all-reduce.2.cloned.1.call-update) | async-done | bytes 536592 | tf_op jit(solution)/shard_map/psum | solution.py:12
  50.5 0.8 fusion.81
  51.3 1.6 %fusion.44 = f32[128,1024]{1,0:T(8,128)S(1)} fusion(f32[1024,128]{0,1:T(8,128)S(1)} %collective-permute-done.5, f32[1024,128]{0,1:T(8,128)S(1)} %collective-permute-done.4, f32[1024,128]{0,1:T(8,128)S(1)} %copy.24, f32[128]{0:T(128)S(1)} %get-tuple-element.19, f32[128]{0:T(128)S(1)} %get-tuple-element.18, f32[128]{0:T(128)S(1)} %get-tuple-element.17, ...), kind=kOutput, calls=%fused_computation.56 | convolution fusion | flops 201981952 | bytes 2164228 | tf_op jit(solution)/shard_map/rlj,lij->rli/dot_general | solution.py:54
  52.8 1.8 %collective-permute-start.7 = (f32[1024,128]{0,1:T(8,128)S(1)}, f32[1024,128]{0,1:T(8,128)S(1)}, u32[]{:S(2)}, u32[]{:S(2)}) collective-permute-start(f32[1024,128]{0,1:T(8,128)S(1)} %bitcast.120), channel_id=1, source_target_pairs={{0,1},{1,2},{2,3},{3,4},{4,5},{5,6},{6,7},{7,8},{8,9},{9,10},{10,1... | collective-permute-start | bytes 1572872 | tf_op jit(solution)/shard_map/ppermute | solution.py:20
  54.6 1.3 collective-permute-start.6
  55.9 0.2 collective-permute-done.7
  56.1 3.5 %collective-permute-done.6 = f32[1024,128]{0,1:T(8,128)S(1)} collective-permute-done((f32[1024,128]{0,1:T(8,128)S(1)}, f32[1024,128]{0,1:T(8,128)S(1)}, u32[]{:S(2)}, u32[]{:S(2)}) %collective-permute-start.6) | collective-permute-done | bytes 524320 | tf_op jit(solution)/shard_map/ppermute | solution.py:23
  59.6 1.6 %fusion.38 = f32[128,1024]{1,0:T(8,128)S(1)} fusion(f32[128,1024]{1,0:T(8,128)S(1)} %fusion.44, f32[1024,128]{0,1:T(8,128)S(1)} %collective-permute-done.7, f32[1024,128]{0,1:T(8,128)S(1)} %collective-permute-done.6, f32[128]{0:T(128)S(1)} %get-tuple-element.19, f32[128]{0:T(128)S(1)} %get-tuple-element.18, f32[128]{0:T(128)S(1)} %get-tuple-element.17, ...), kind=kOutput, calls=%fused_computation.47 | convolution fusion | flops 201981952 | bytes 2164228 | tf_op jit(solution)/shard_map/rlj,lij->rli/dot_general | solution.py:54
  61.2 10.4 %collective-permute-start.9 = (f32[1024,128]{0,1:T(8,128)S(1)}, f32[1024,128]{0,1:T(8,128)S(1)}, u32[]{:S(2)}, u32[]{:S(2)}) collective-permute-start(f32[1024,128]{0,1:T(8,128)S(1)} %bitcast.118), channel_id=1, source_target_pairs={{0,1},{1,2},{2,3},{3,4},{4,5},{5,6},{6,7},{7,8},{8,9},{9,10},{10,1... | collective-permute-start | bytes 1572872 | tf_op jit(solution)/shard_map/ppermute | solution.py:20
  71.6 1.3 collective-permute-start.8
  72.9 0.2 collective-permute-done.9
  73.1 4.3 %collective-permute-done.8 = f32[1024,128]{0,1:T(8,128)S(1)} collective-permute-done((f32[1024,128]{0,1:T(8,128)S(1)}, f32[1024,128]{0,1:T(8,128)S(1)}, u32[]{:S(2)}, u32[]{:S(2)}) %collective-permute-start.8) | collective-permute-done | bytes 524320 | tf_op jit(solution)/shard_map/ppermute | solution.py:23
  77.4 1.6 %fusion.36 = f32[128,1024]{1,0:T(8,128)S(1)} fusion(f32[128,1024]{1,0:T(8,128)S(1)} %fusion.38, f32[1024,128]{0,1:T(8,128)S(1)} %collective-permute-done.9, f32[1024,128]{0,1:T(8,128)S(1)} %collective-permute-done.8, f32[128]{0:T(128)S(1)} %get-tuple-element.19, f32[128]{0:T(128)S(1)} %get-tuple-element.18, f32[128]{0:T(128)S(1)} %get-tuple-element.17, ...), kind=kOutput, calls=%fused_computation.42 | convolution fusion | flops 201981952 | bytes 2164228 | tf_op jit(solution)/shard_map/rlj,lij->rli/dot_general | solution.py:54
  78.9 9.0 %all_to_all.50 = f32[1024,2,64]{0,2,1:T(8,128)S(1)} all-to-all(f32[1024,2,64]{0,2,1:T(8,128)S(1)} %bitcast.123), channel_id=1, replica_groups=mesh['rows'=2,'cols'=16] {'rows'}, dimensions={1} | all-to-all | bytes 1048576 | tf_op jit(solution)/shard_map/all_to_all | solution.py:87
  87.9 0.4 copy.27
  88.3 0.4 all_to_all.40
  88.8 0.2 copy.28
  88.9 28.3 %all_to_all.51 = f32[16,128,64]{1,2,0:T(8,128)S(1)} all-to-all(f32[16,128,64]{1,2,0:T(8,128)S(1)} %copy.28), channel_id=1, replica_groups=mesh['rows'=2,'cols'=16] {'cols'}, dimensions={0} | all-to-all | bytes 1048576 | tf_op jit(solution)/shard_map/all_to_all | solution.py:86
  117.2 10.8 %all_to_all.52 = f32[16,64,128]{2,1,0:T(8,128)S(1)} all-to-all(f32[16,64,128]{2,1,0:T(8,128)S(1)} %bitcast.126), channel_id=1, replica_groups=mesh['rows'=2,'cols'=16] {'rows'}, dimensions={0} | all-to-all | bytes 1048576 | tf_op jit(solution)/shard_map/all_to_all | solution.py:94
  128.1 1.3 collective-permute-start.11
  129.4 4.6 %collective-permute-start.10 = (f32[384,128]{1,0:T(8,128)S(1)}, f32[384,128]{1,0:T(8,128)S(1)}, u32[]{:S(2)}, u32[]{:S(2)}) collective-permute-start(f32[384,128]{1,0:T(8,128)S(1)} %bitcast.127), channel_id=1, source_target_pairs={{0,16},{1,17},{2,18},{3,19},{4,20},{5,21},{6,22},{7,23},{8,24},{9,... | collective-permute-start | bytes 589832 | tf_op jit(solution)/shard_map/ppermute | solution.py:20
  134.1 2.0 %collective-permute-done.11 = f32[384,128]{1,0:T(8,128)S(1)} collective-permute-done((f32[384,128]{1,0:T(8,128)S(1)}, f32[384,128]{1,0:T(8,128)S(1)}, u32[]{:S(2)}, u32[]{:S(2)}) %collective-permute-start.11) | collective-permute-done | bytes 196640 | tf_op jit(solution)/shard_map/ppermute | solution.py:23
  136.0 1.2 collective-permute-done.10
  137.2 0.1 pad_maximum_fusion
  137.3 0.2 fusion.83
  137.4 1.9 %fusion = f32[12,128,128]{2,1,0:T(8,128)S(1)} fusion(f32[12,128,128]{2,1,0:T(8,128)S(1)} %bitcast.113, f32[12,128,128]{2,1,0:T(8,128)S(1)} %bitcast.114, f32[12,128,128]{2,1,0:T(8,128)S(1)} %bitcast.112, f32[12,131,128]{2,1,0:T(8,128)S(1)} %pad_maximum_fusion.1, f32[12,128]{1,0:T(8,128)S(1)} %get-tuple-element.29, f32[12,128]{1,0:T(8,128)S(1)} %get-tuple-element.30, ...), kind=kOutput, calls=%fused_computation.2 | convolution fusion | flops 302972928 | bytes 3956736 | tf_op jit(solution)/shard_map/lij,ljc->lic/dot_general | solution.py:39
  139.3 1.4 fusion.15
  140.7 1.8 %fusion.27 = f32[8,128,128]{1,2,0:T(8,128)} fusion(f32[8,128,128]{2,1,0:T(8,128)S(1)} %copy-done, f32[10,128,128]{2,1,0:T(8,128)S(1)} %fusion.15, f32[8,128]{1,0:T(8,128)S(1)} %get-tuple-element.27, f32[8,128]{1,0:T(8,128)S(1)} %get-tuple-element.28, f32[8,128]{1,0:T(8,128)S(1)} %get-tuple-element.26), kind=kOutput, calls=%fused_computation.32 | convolution fusion | flops 201981952 | bytes 2633728 | tf_op jit(solution)/shard_map/lij,ljc->lic/dot_general | solution.py:39
  (25 shorter events, 0.3 us)
Async XLA Ops:
  6.5 7.3 %copy-start = (f32[8,128,128]{2,1,0:T(8,128)S(1)}, f32[8,128,128]{2,1,0:T(8,128)}, u32[]{:S(2)}) copy-start(f32[8,128,128]{2,1,0:T(8,128)} %param.4) | copy-start | bytes 1572868
  6.5 43.9 %all-reduce.2.cloned.1.call-start = ((), (), s32[]{:S(2)}) async-start(), calls=%async_computation.3 | async-start | bytes 1114112 | tf_op jit(solution)/shard_map/psum | solution.py:12
  7.6 15.8 %collective-permute-start.3 = (f32[384,128]{1,0:T(8,128)S(1)}, f32[384,128]{1,0:T(8,128)S(1)}, u32[]{:S(2)}, u32[]{:S(2)}) collective-permute-start(f32[384,128]{1,0:T(8,128)S(1)} %get-tuple-element.24), channel_id=1, source_target_pairs={{16,0},{17,1},{18,2},{19,3},{20,4},{21,5},{22,6},{23,7},{24,8},{25... | collective-permute-start | bytes 589832 | tf_op jit(solution)/shard_map/ppermute | solution.py:23
  8.9 5.0 %copy-start.2 = (f32[8,3,128]{2,0,1:T(8,128)S(1)}, f32[8,3,128]{2,0,1:T(8,128)}, u32[]{:S(2)}) copy-start(f32[8,3,128]{2,0,1:T(8,128)} %param.5) | copy-start | bytes 36868
  9.0 13.5 %collective-permute-start.2 = (f32[384,128]{1,0:T(8,128)S(1)}, f32[384,128]{1,0:T(8,128)S(1)}, u32[]{:S(2)}, u32[]{:S(2)}) collective-permute-start(f32[384,128]{1,0:T(8,128)S(1)} %get-tuple-element.25), channel_id=1, source_target_pairs={{0,16},{1,17},{2,18},{3,19},{4,20},{5,21},{6,22},{7,23},{8,24},{9,... | collective-permute-start | bytes 589832 | tf_op jit(solution)/shard_map/ppermute | solution.py:20
  14.0 7.0 %collective-permute-start = (f32[2,131,128]{2,1,0:T(8,128)S(1)}, f32[2,131,128]{2,1,0:T(8,128)S(1)}, u32[]{:S(2)}, u32[]{:S(2)}) collective-permute-start(f32[2,131,128]{2,1,0:T(8,128)S(1)} %get-tuple-element.20), channel_id=1, source_target_pairs={{0,16},{1,17},{2,18},{3,19},{4,20},{5,21},{6,22},{7,23},{8,24},{9,... | collective-permute-start | bytes 402440 | tf_op jit(solution)/shard_map/ppermute | solution.py:20
  15.3 7.0 %collective-permute-start.1 = (f32[2,131,128]{2,1,0:T(8,128)S(1)}, f32[2,131,128]{2,1,0:T(8,128)S(1)}, u32[]{:S(2)}, u32[]{:S(2)}) collective-permute-start(f32[2,131,128]{2,1,0:T(8,128)S(1)} %get-tuple-element.21), channel_id=1, source_target_pairs={{16,0},{17,1},{18,2},{19,3},{20,4},{21,5},{22,6},{23,7},{24,8},{25... | collective-permute-start | bytes 402440 | tf_op jit(solution)/shard_map/ppermute | solution.py:23
  22.4 1.0 copy-start.1
  28.4 22.9 %collective-permute-start.5 = (f32[1024,128]{0,1:T(8,128)S(1)}, f32[1024,128]{0,1:T(8,128)S(1)}, u32[]{:S(2)}, u32[]{:S(2)}) collective-permute-start(f32[1024,128]{0,1:T(8,128)S(1)} %copy.24), channel_id=1, source_target_pairs={{0,1},{1,2},{2,3},{3,4},{4,5},{5,6},{6,7},{7,8},{8,9},{9,10},{10,1... | collective-permute-start | bytes 1572872 | tf_op jit(solution)/shard_map/ppermute | solution.py:20
  29.7 21.5 %collective-permute-start.4 = (f32[1024,128]{0,1:T(8,128)S(1)}, f32[1024,128]{0,1:T(8,128)S(1)}, u32[]{:S(2)}, u32[]{:S(2)}) collective-permute-start(f32[1024,128]{0,1:T(8,128)S(1)} %copy.24), channel_id=1, source_target_pairs={{1,0},{2,1},{3,2},{4,3},{5,4},{6,5},{7,6},{8,7},{9,8},{10,9},{11,1... | collective-permute-start | bytes 1572872 | tf_op jit(solution)/shard_map/ppermute | solution.py:23
  52.8 3.3 %collective-permute-start.7 = (f32[1024,128]{0,1:T(8,128)S(1)}, f32[1024,128]{0,1:T(8,128)S(1)}, u32[]{:S(2)}, u32[]{:S(2)}) collective-permute-start(f32[1024,128]{0,1:T(8,128)S(1)} %bitcast.120), channel_id=1, source_target_pairs={{0,1},{1,2},{2,3},{3,4},{4,5},{5,6},{6,7},{7,8},{8,9},{9,10},{10,1... | collective-permute-start | bytes 1572872 | tf_op jit(solution)/shard_map/ppermute | solution.py:20
  54.6 5.0 %collective-permute-start.6 = (f32[1024,128]{0,1:T(8,128)S(1)}, f32[1024,128]{0,1:T(8,128)S(1)}, u32[]{:S(2)}, u32[]{:S(2)}) collective-permute-start(f32[1024,128]{0,1:T(8,128)S(1)} %bitcast.121), channel_id=1, source_target_pairs={{1,0},{2,1},{3,2},{4,3},{5,4},{6,5},{7,6},{8,7},{9,8},{10,9},{11,1... | collective-permute-start | bytes 1572872 | tf_op jit(solution)/shard_map/ppermute | solution.py:23
  61.2 11.8 %collective-permute-start.9 = (f32[1024,128]{0,1:T(8,128)S(1)}, f32[1024,128]{0,1:T(8,128)S(1)}, u32[]{:S(2)}, u32[]{:S(2)}) collective-permute-start(f32[1024,128]{0,1:T(8,128)S(1)} %bitcast.118), channel_id=1, source_target_pairs={{0,1},{1,2},{2,3},{3,4},{4,5},{5,6},{6,7},{7,8},{8,9},{9,10},{10,1... | collective-permute-start | bytes 1572872 | tf_op jit(solution)/shard_map/ppermute | solution.py:20
  71.6 5.8 %collective-permute-start.8 = (f32[1024,128]{0,1:T(8,128)S(1)}, f32[1024,128]{0,1:T(8,128)S(1)}, u32[]{:S(2)}, u32[]{:S(2)}) collective-permute-start(f32[1024,128]{0,1:T(8,128)S(1)} %bitcast.119), channel_id=1, source_target_pairs={{1,0},{2,1},{3,2},{4,3},{5,4},{6,5},{7,6},{8,7},{9,8},{10,9},{11,1... | collective-permute-start | bytes 1572872 | tf_op jit(solution)/shard_map/ppermute | solution.py:23
  128.1 7.9 %collective-permute-start.11 = (f32[384,128]{1,0:T(8,128)S(1)}, f32[384,128]{1,0:T(8,128)S(1)}, u32[]{:S(2)}, u32[]{:S(2)}) collective-permute-start(f32[384,128]{1,0:T(8,128)S(1)} %bitcast.128), channel_id=1, source_target_pairs={{16,0},{17,1},{18,2},{19,3},{20,4},{21,5},{22,6},{23,7},{24,8},{25... | collective-permute-start | bytes 589832 | tf_op jit(solution)/shard_map/ppermute | solution.py:23
  129.4 7.8 %collective-permute-start.10 = (f32[384,128]{1,0:T(8,128)S(1)}, f32[384,128]{1,0:T(8,128)S(1)}, u32[]{:S(2)}, u32[]{:S(2)}) collective-permute-start(f32[384,128]{1,0:T(8,128)S(1)} %bitcast.127), channel_id=1, source_target_pairs={{0,16},{1,17},{2,18},{3,19},{4,20},{5,21},{6,22},{7,23},{8,24},{9,... | collective-permute-start | bytes 589832 | tf_op jit(solution)/shard_map/ppermute | solution.py:20
Sparse Core Ops, SparseCore 0:
  17.6 32.8 all-reduce.1
where the time goes:
time: 150 us; the launch traced here: 149 us
  blocking collectives  48.1 us (32%)
  waiting for transfers between devices  35.6 us (24%)
  starting transfers between devices  32 us (21%)
  matrix products  14.3 us (10%)
  between operations  13.8 us (9%)
  local copies, waits for them, and re-layouts  4.58 us (3%)
    all_to_all x1, blocking collectives, on_device(): lax.all_to_all(lax.all_to_all(current, 'rows', split_axis=1, concat_axis=...  28.3 us
    ppermute x6, starting transfers between devices, with_halo(): lax.ppermute(lax.slice_in_dim(block, block.shape[dim] - width, None, axis...  24.2 us
    psum x1, waiting for transfers between devices, from_root(): return lax.psum(jnp.where(mine, value, jnp.zeros_like(value)), axis)  19.4 us
    ppermute x6, waiting for transfers between devices, with_halo(): lax.ppermute(lax.slice_in_dim(block, 0, width, axis=dim), axis, backward)  11.1 us
    all_to_all x1, blocking collectives, on_device(): lax.all_to_all(turned, 'rows', split_axis=0, concat_axis=1, tiled=True)  10.8 us
    dot_general x6, matrix products, rows_local(): jnp.einsum('lij,ljc->lic', zonal_mats, mixed, precision=lax.Precision.HIG...  9.57 us
    all_to_all x1, blocking collectives, on_device(): lax.all_to_all(current, 'rows', split_axis=1, concat_axis=0, tiled=True)  8.99 us
    ppermute x6, starting transfers between devices, with_halo(): lax.ppermute(lax.slice_in_dim(block, 0, width, axis=dim), axis, backward)  7.75 us
  transfers between devices with their start and end apart: 13, of which 9 were waited for; matrix products, arithmetic and copies ran while one was open for 5% of the time, Pallas kernels for 0%

commit v1 on v0

v1 whole, which is shorter than its diff:
```python
import functools

import jax
import jax.numpy as jnp
from jax import lax
from jax.experimental import pallas as pl
from jax.experimental.pallas import tpu as pltpu
from jax.sharding import PartitionSpec as P

STEPS = 3
LAGS = 3
VMEM = pl.BlockSpec(memory_space=pltpu.VMEM)
PARAMS = pltpu.CompilerParams(vmem_limit_bytes=48 * 1024 * 1024)
NT = (((1,), (1,)), ((), ()))


def split(value):
    high = value.astype(jnp.bfloat16)
    low = (value - high.astype(jnp.float32)).astype(jnp.bfloat16)
    return high, low


def prepare_operators(zonal_of, lats, ops):
    for lat in range(lats):
        high, low = split(zonal_of(lat))
        ops[lat] = jnp.concatenate([high, high, low], axis=1)


def apply_steps(state, ops, weights, lats, count):
    def one(step, carry):
        before = None
        own = state[0]
        for lat in range(lats):
            after = state[lat + 1] if lat + 1 < lats else None
            mixed = weights[lat, 0:1, :] * own
            if after is not None:
                mixed = mixed + weights[lat, 1:2, :] * after
            if before is not None:
                mixed = mixed + weights[lat, 2:3, :] * before
            high, low = split(mixed)
            state[lat] = lax.dot_general(
                jnp.concatenate([high, low, high], axis=1),
                ops[lat],
                NT,
                preferred_element_type=jnp.float32,
            )
            before, own = own, after
        return carry

    lax.fori_loop(0, count, one, 0)


def cut_kernel(pieces, share, block, zonal, stencil, *outs):
    me = lax.axis_index("rows")
    core = lax.axis_index("cols") % share
    width = block.shape[1] // pieces
    tall = block.shape[0]
    lons = zonal.shape[1]
    for partner in range(pieces):
        target = me ^ partner
        for first in range(0, tall, lons):
            turned = block[first : first + lons, :].T
            for other in range(pieces):

                @pl.when(target == other)
                def _():
                    outs[partner][:, first : first + lons] = turned[other * width : (other + 1) * width]

    packet = outs[pieces]
    count = zonal.shape[0] // share
    for lat in range(count):
        packet[lat * lons : (lat + 1) * lons, :] = zonal[core * count + lat]
        packet[count * lons + 8 * lat : count * lons + 8 * lat + 3, :] = stencil[core * count + lat]


def load_operators(pieces, share, zonal, stencil, packets, ops, weights):
    me = lax.axis_index("rows")
    core = lax.axis_index("cols") % share
    lat_rows, lons = zonal.shape[:2]
    count = lat_rows // share

    def put(lat, matrix, coeffs):
        high, low = split(matrix)
        ops[lat] = jnp.concatenate([high, high, low], axis=1)
        weights[lat, 0:3, :] = coeffs

    for lat in range(lat_rows):
        put(me * lat_rows + lat, zonal[lat], stencil[lat])
    for partner in range(1, pieces):
        for part in range(share):
            packet = packets[(partner - 1) * share + part]
            first = (me ^ partner) * lat_rows + (core ^ part) * count
            for lat in range(count):
                put(
                    first + lat,
                    packet[lat * lons : (lat + 1) * lons, :],
                    packet[count * lons + 8 * lat : count * lons + 8 * lat + 3, :],
                )


def first_kernel(pieces, share, cols, *refs):
    n_packets = (pieces - 1) * share
    blocks = refs[:pieces]
    zonal, stencil = refs[pieces : pieces + 2]
    packets = refs[pieces + 2 : pieces + 2 + n_packets]
    out, state, ops, weights = refs[pieces + 2 + n_packets :]
    me = lax.axis_index("rows")
    lat_rows, lons = zonal.shape[:2]
    lats = pieces * lat_rows
    for partner in range(pieces):
        for lat in range(lat_rows):
            state[(me ^ partner) * lat_rows + lat] = blocks[partner][:, lat * lons : (lat + 1) * lons]
    load_operators(pieces, share, zonal, stencil, packets, ops, weights)
    apply_steps(state, ops, weights, lats, STEPS)
    width = state.shape[1]
    fold = lons // width
    short = width // fold
    for lat in range(lats):
        turned = state[lat].T
        for sub in range(fold):
            index = lat * fold + sub
            target = index % pieces * cols + index // pieces
            out[target] = jnp.concatenate(
                [
                    turned[sub * width + part * short : sub * width + (part + 1) * short]
                    for part in range(fold)
                ],
                axis=1,
            )


def second_kernel(pieces, share, cols, *refs):
    n_packets = (pieces - 1) * share
    moved, zonal, stencil = refs[:3]
    packets = refs[3 : 3 + n_packets]
    outs = refs[3 + n_packets : 3 + n_packets + pieces]
    state, ops, weights = refs[3 + n_packets + pieces :]
    me = lax.axis_index("rows")
    lat_rows, lons = zonal.shape[:2]
    lats = pieces * lat_rows
    width = state.shape[1]
    fold = lons // width
    short = width // fold
    for lat in range(lats):
        got = []
        for sub in range(fold):
            index = lat * fold + sub
            got.append(moved[index % pieces * cols + index // pieces])
        for part in range(fold):
            state[lat, part * short : (part + 1) * short, :] = jnp.concatenate(
                [block[:, part * width : (part + 1) * width] for block in got], axis=1
            )
    load_operators(pieces, share, zonal, stencil, packets, ops, weights)
    apply_steps(state, ops, weights, lats, STEPS + LAGS)
    for partner in range(pieces):
        for lat in range(lat_rows):
            outs[partner][:, lat * lons : (lat + 1) * lons] = state[(me ^ partner) * lat_rows + lat]


def join_kernel(pieces, *refs):
    blocks, out, stack = refs[:pieces], refs[pieces], refs[pieces + 1]
    me = lax.axis_index("rows")
    width, tall = blocks[0].shape
    lons = 128 if tall % 128 == 0 else tall
    for partner in range(pieces):
        stack[me ^ partner] = blocks[partner][...]
    for first in range(0, tall, lons):
        rows = jnp.concatenate([stack[i, :, first : first + lons] for i in range(pieces)], axis=0)
        out[first : first + lons, :] = rows.T


def call(kernel, out_shape, args, scratch=()):
    single = not isinstance(out_shape, (list, tuple))
    return pl.pallas_call(
        kernel,
        out_shape=out_shape,
        in_specs=[VMEM] * len(args),
        out_specs=VMEM if single else [VMEM] * len(out_shape),
        scratch_shapes=list(scratch),
        compiler_params=PARAMS,
    )(*args)


def on_device(covariance, zonal, stencil):
    pieces = lax.axis_size("rows")
    cols = lax.axis_size("cols")
    share = 2
    tall, wide = covariance.shape
    lat_rows, lons = zonal.shape[:2]
    lats = lat_rows * pieces
    width = wide // pieces
    count = lat_rows // share
    f32 = jnp.float32

    def row_swap(value, partner):
        return lax.ppermute(value, "rows", [(i, i ^ partner) for i in range(pieces)])

    def core_swap(value, part):
        return lax.ppermute(value, "cols", [(i, i ^ part) for i in range(cols)])

    strip = jax.ShapeDtypeStruct((width, tall), f32)
    packet_shape = jax.ShapeDtypeStruct((count * (lons + 8), lons), f32)
    cut = call(
        functools.partial(cut_kernel, pieces, share),
        [strip] * pieces + [packet_shape],
        (covariance, zonal, stencil),
    )
    packets = []
    for partner in range(1, pieces):
        direct = row_swap(cut[pieces], partner)
        packets += [direct, core_swap(direct, 1)]
    blocks = [cut[0]] + [row_swap(cut[partner], partner) for partner in range(1, pieces)]
    scratch = [
        pltpu.VMEM((lats, width, lons), f32),
        pltpu.VMEM((lats, lons, 3 * lons), jnp.bfloat16),
        pltpu.VMEM((lats, 8, lons), f32),
    ]
    packed = jax.ShapeDtypeStruct((pieces * cols, width * width // lons, lons), f32)
    sent = call(
        functools.partial(first_kernel, pieces, share, cols),
        packed,
        (*blocks, zonal, stencil, *packets),
        scratch,
    )
    moved = lax.all_to_all(sent, ("rows", "cols"), 0, 0, tiled=True)
    ends = call(
        functools.partial(second_kernel, pieces, share, cols),
        [strip] * pieces,
        (moved, zonal, stencil, *packets),
        scratch,
    )
    blocks = [ends[0]] + [row_swap(ends[partner], partner) for partner in range(1, pieces)]
    return call(
        functools.partial(join_kernel, pieces),
        jax.ShapeDtypeStruct((tall, wide), f32),
        blocks,
        [pltpu.VMEM((pieces, width, tall), f32)],
    )


def solution(mesh):
    placed = (P("rows", "cols"), P("rows", None, None), P("rows", None, None))
    return jax.shard_map(
        on_device, mesh=mesh, in_specs=placed, out_specs=P("rows", "cols"), check_vma=False
    )
```

time: 150 us -> 62.2 us (0.41)
  blocking collectives: 48.1 us -> 21.8 us
  starting transfers between devices: 32 us -> 5.85 us
  waiting for transfers between devices: 35.6 us -> 20.5 us
  matrix products: 14.3 us -> 0 us
  between operations: 13.8 us -> 0.03 us
  Pallas kernels: 0 us -> 11 us
  local copies, waits for them, and re-layouts: 4.58 us -> 2.8 us
    all_to_all x3 -> x1, blocking collectives: 48.1 us -> 21.8 us  [on_device(): moved = lax.all_to_all(sent, ('rows', 'cols'), 0, 0, tiled=True)]
    ppermute x12 -> x4, starting transfers between devices: 32 us -> 5.85 us  [the longest x3 5.85 us: row_swap(): lax.ppermute(value, 'rows', [(i, i ^ partner) for i in range(pieces)])]
    psum x1 -> x0, waiting for transfers between devices: 19.4 us -> none  [from_root(): return lax.psum(jnp.where(mine, value, jnp.zeros_like(value)), axis)]
    dot_general x9 -> x0, matrix products: 14.3 us -> none  [the longest x6 9.57 us: rows_local(): jnp.einsum('lij,ljc->lic', zonal_mats, mixed, precision=lax.Precision.HIG...]
    pallas_call x0 -> x4, Pallas kernels: none -> 11 us  [call(): pl.pallas_call(kernel, out_shape=out_shape, in_specs=[VMEM] * len(args),...]
    ppermute x12 -> x4, waiting for transfers between devices: 16.2 us -> 20.5 us  [the longest x3 20.5 us: row_swap(): lax.ppermute(value, 'rows', [(i, i ^ partner) for i in range(pieces)])]
    unnamed x13 -> x7, local copies, waits for them, and re-layouts: 1.04 us -> 2.8 us
  transfers between devices with their start and end apart: 13 -> 4, of which waited for: 9 -> 3; matrix products, arithmetic and copies ran while one was open for 5% -> 0% of each run, Pallas kernels for 0% -> 0%
where the time goes in v1:
time: 62.2 us; the launch traced here: 62 us
  blocking collectives  21.8 us (35%)
  waiting for transfers between devices  20.5 us (33%)
  Pallas kernels  11 us (18%)
  starting transfers between devices  5.85 us (9%)
  local copies, waits for them, and re-layouts  2.8 us (5%)
    all_to_all x1, blocking collectives, on_device(): moved = lax.all_to_all(sent, ('rows', 'cols'), 0, 0, tiled=True)  21.8 us
    ppermute x3, waiting for transfers between devices, row_swap(): lax.ppermute(value, 'rows', [(i, i ^ partner) for i in range(pieces)])  20.5 us
    pallas_call x4, Pallas kernels, call(): pl.pallas_call(kernel, out_shape=out_shape, in_specs=[VMEM] * len(args),...  11 us
    ppermute x3, starting transfers between devices, row_swap(): lax.ppermute(value, 'rows', [(i, i ^ partner) for i in range(pieces)])  5.85 us
    unnamed x7, local copies, waits for them, and re-layouts  2.8 us
  transfers between devices with their start and end apart: 4, of which 3 were waited for; matrix products, arithmetic and copies ran while one was open for 0% of the time, Pallas kernels for 0%

profile of v1, /device:TPU:0, one launch (start us, length us, event | category | flops | bytes accessed | tf_op | source)
XLA Modules:
  0.0 62.0 jit_solution(16863353571569551696)
XLA Ops:
  0.0 0.7 %copy.4.stencil.refs_3_.refs_2_ = f32[8,3,128]{2,1,0:T(4,128)S(1)} copy(f32[8,3,128]{2,0,1:T(8,128)} %param.5) | data formatting | bytes 24576 | tf_op args[2]
  0.7 0.0 copy-start
  0.7 1.0 %copy-done = f32[8,128,128]{2,1,0:T(8,128)S(1)} copy-done((f32[8,128,128]{2,1,0:T(8,128)S(1)}, f32[8,128,128]{2,1,0:T(8,128)}, u32[]{:S(2)}) %copy-start) | copy-done | bytes 524312
  1.8 0.0 copy-start.2
  1.8 1.0 %copy-done.2 = f32[1024,128]{1,0:T(8,128)S(1)} copy-done((f32[1024,128]{1,0:T(8,128)S(1)}, f32[1024,128]{1,0:T(8,128)}, u32[]{:S(2)}) %copy-start.2) | copy-done | bytes 524312
  2.8 0.0 copy-start.1
  2.8 1.6 %shard_map.37 = (f32[64,1024]{1,0:T(8,128)S(1)}, f32[64,1024]{1,0:T(8,128)S(1)}, f32[544,128]{1,0:T(8,128)S(1)}) custom-call(f32[1024,128]{1,0:T(8,128)S(1)} %copy-done.2, f32[8,128,128]{2,1,0:T(8,128)S(1)} %copy-done, f32[8,3,128]{2,1,0:T(4,128)S(1)} %copy.4.stencil.refs_3_.refs_2_), custom_call_target="tpu_custom_call" | custom-call | tf_op jit(solution)/shard_map/pallas_call | solution.py:174
  4.4 3.0 %collective-permute-start.1 = (f32[544,128]{1,0:T(8,128)S(1)}, f32[544,128]{1,0:T(8,128)S(1)}, u32[]{:S(2)}, u32[]{:S(2)}) collective-permute-start(f32[544,128]{1,0:T(8,128)S(1)} %get-tuple-element.12), channel_id=1, source_target_pairs={{0,16},{16,0},{1,17},{17,1},{2,18},{18,2},{3,19},{19,3},{4,20},{20... | collective-permute-start | bytes 835592 | tf_op jit(solution)/shard_map/ppermute | solution.py:196
  7.5 6.7 %collective-permute-done.1.refs_4_.refs_3_ = f32[544,128]{1,0:T(8,128)S(1)} collective-permute-done((f32[544,128]{1,0:T(8,128)S(1)}, f32[544,128]{1,0:T(8,128)S(1)}, u32[]{:S(2)}, u32[]{:S(2)}) %collective-permute-start.1) | collective-permute-done | bytes 278560 | tf_op jit(solution)/shard_map/ppermute | solution.py:196
  14.1 0.0 collective-permute-start.2
  14.1 1.7 %collective-permute-start = (f32[64,1024]{1,0:T(8,128)S(1)}, f32[64,1024]{1,0:T(8,128)S(1)}, u32[]{:S(2)}, u32[]{:S(2)}) collective-permute-start(f32[64,1024]{1,0:T(8,128)S(1)} %get-tuple-element.11), channel_id=1, source_target_pairs={{0,16},{16,0},{1,17},{17,1},{2,18},{18,2},{3,19},{19,3},{4,20},{20... | collective-permute-start | bytes 786440 | tf_op jit(solution)/shard_map/ppermute | solution.py:196
  15.9 7.0 %collective-permute-done.refs_1_ = f32[64,1024]{1,0:T(8,128)S(1)} collective-permute-done((f32[64,1024]{1,0:T(8,128)S(1)}, f32[64,1024]{1,0:T(8,128)S(1)}, u32[]{:S(2)}, u32[]{:S(2)}) %collective-permute-start) | collective-permute-done | bytes 262176 | tf_op jit(solution)/shard_map/ppermute | solution.py:196
  22.8 0.0 collective-permute-done.2.refs_5_.refs_4_
  22.8 0.0 copy-done.1
  22.8 3.1 %shard_map.38 = f32[32,32,128]{2,1,0:T(8,128)S(1)} custom-call(f32[64,1024]{1,0:T(8,128)S(1)} %get-tuple-element.10.refs_0_, f32[64,1024]{1,0:T(8,128)S(1)} %collective-permute-done.refs_1_, f32[8,128,128]{2,1,0:T(8,128)S(1)} %copy-done.1, f32[8,3,128]{2,1,0:T(4,128)S(1)} %copy.4.stencil.refs_3_.refs_2_, ...), custom_call_target="tpu_custom_call" | custom-call | tf_op jit(solution)/shard_map/pallas_call | solution.py:174
  25.9 21.8 %all_to_all.5.refs_0_ = f32[32,32,128]{2,1,0:T(8,128)S(1)} all-to-all(f32[32,32,128]{2,1,0:T(8,128)S(1)} %shard_map.38), channel_id=1, replica_groups=mesh['rows'=2,'cols'=16] {'rows','cols'}, dimensions={0} | all-to-all | bytes 1048576 | tf_op jit(solution)/shard_map/all_to_all | solution.py:225
  47.8 5.3 %shard_map.39 = (f32[64,1024]{1,0:T(8,128)S(1)}, f32[64,1024]{1,0:T(8,128)S(1)}) custom-call(f32[32,32,128]{2,1,0:T(8,128)S(1)} %all_to_all.5.refs_0_, f32[8,128,128]{2,1,0:T(8,128)S(1)} %copy-done.1, f32[8,3,128]{2,1,0:T(4,128)S(1)} %copy.4.stencil.refs_3_.refs_2_, f32[544,128]{1,0:T(8,128)S(1)} %collective-permute-done.1.refs_4_.refs_3_, ...), custom_call_target="tpu_custom_call" | custom-call | tf_op jit(solution)/shard_map/pallas_call | solution.py:174
  53.0 1.1 %collective-permute-start.3 = (f32[64,1024]{1,0:T(8,128)S(1)}, f32[64,1024]{1,0:T(8,128)S(1)}, u32[]{:S(2)}, u32[]{:S(2)}) collective-permute-start(f32[64,1024]{1,0:T(8,128)S(1)} %get-tuple-element.14), channel_id=1, source_target_pairs={{0,16},{16,0},{1,17},{17,1},{2,18},{18,2},{3,19},{19,3},{4,20},{20... | collective-permute-start | bytes 786440 | tf_op jit(solution)/shard_map/ppermute | solution.py:196
  54.1 6.8 %collective-permute-done.3.refs_1_ = f32[64,1024]{1,0:T(8,128)S(1)} collective-permute-done((f32[64,1024]{1,0:T(8,128)S(1)}, f32[64,1024]{1,0:T(8,128)S(1)}, u32[]{:S(2)}, u32[]{:S(2)}) %collective-permute-start.3) | collective-permute-done | bytes 262176 | tf_op jit(solution)/shard_map/ppermute | solution.py:196
  60.9 1.0 %shard_map.40 = f32[1024,128]{1,0:T(8,128)} custom-call(f32[64,1024]{1,0:T(8,128)S(1)} %get-tuple-element.13.refs_0_, f32[64,1024]{1,0:T(8,128)S(1)} %collective-permute-done.3.refs_1_), custom_call_target="tpu_custom_call" | custom-call | tf_op jit(solution)/shard_map/pallas_call | solution.py:174
Async XLA Ops:
  0.7 1.0 %copy-start = (f32[8,128,128]{2,1,0:T(8,128)S(1)}, f32[8,128,128]{2,1,0:T(8,128)}, u32[]{:S(2)}) copy-start(f32[8,128,128]{2,1,0:T(8,128)} %refs_1_.1) | copy-start | bytes 1572868
  1.8 1.0 %copy-start.2 = (f32[1024,128]{1,0:T(8,128)S(1)}, f32[1024,128]{1,0:T(8,128)}, u32[]{:S(2)}) copy-start(f32[1024,128]{1,0:T(8,128)} %block.1) | copy-start | bytes 1572868
  2.8 20.0 %copy-start.1 = (f32[8,128,128]{2,1,0:T(8,128)S(1)}, f32[8,128,128]{2,1,0:T(8,128)}, u32[]{:S(2)}) copy-start(f32[8,128,128]{2,1,0:T(8,128)} %refs_1_.1) | copy-start | bytes 1572868
  4.4 9.7 %collective-permute-start.1 = (f32[544,128]{1,0:T(8,128)S(1)}, f32[544,128]{1,0:T(8,128)S(1)}, u32[]{:S(2)}, u32[]{:S(2)}) collective-permute-start(f32[544,128]{1,0:T(8,128)S(1)} %get-tuple-element.12), channel_id=1, source_target_pairs={{0,16},{16,0},{1,17},{17,1},{2,18},{18,2},{3,19},{19,3},{4,20},{20... | collective-permute-start | bytes 835592 | tf_op jit(solution)/shard_map/ppermute | solution.py:196
  14.1 8.7 %collective-permute-start.2 = (f32[544,128]{1,0:T(8,128)S(1)}, f32[544,128]{1,0:T(8,128)S(1)}, u32[]{:S(2)}, u32[]{:S(2)}) collective-permute-start(f32[544,128]{1,0:T(8,128)S(1)} %collective-permute-done.1.refs_4_.refs_3_), channel_id=1, source_target_pairs={{0,1},{1,0},{2,3},{3,2},{4,5},{5,4},{6,7},{7,6},{8,9},{9,8},{10,11... | collective-permute-start | bytes 835592 | tf_op jit(solution)/shard_map/ppermute | solution.py:199
  14.1 8.7 %collective-permute-start = (f32[64,1024]{1,0:T(8,128)S(1)}, f32[64,1024]{1,0:T(8,128)S(1)}, u32[]{:S(2)}, u32[]{:S(2)}) collective-permute-start(f32[64,1024]{1,0:T(8,128)S(1)} %get-tuple-element.11), channel_id=1, source_target_pairs={{0,16},{16,0},{1,17},{17,1},{2,18},{18,2},{3,19},{19,3},{4,20},{20... | collective-permute-start | bytes 786440 | tf_op jit(solution)/shard_map/ppermute | solution.py:196
  53.0 7.9 %collective-permute-start.3 = (f32[64,1024]{1,0:T(8,128)S(1)}, f32[64,1024]{1,0:T(8,128)S(1)}, u32[]{:S(2)}, u32[]{:S(2)}) collective-permute-start(f32[64,1024]{1,0:T(8,128)S(1)} %get-tuple-element.14), channel_id=1, source_target_pairs={{0,16},{16,0},{1,17},{17,1},{2,18},{18,2},{3,19},{19,3},{4,20},{20... | collective-permute-start | bytes 786440 | tf_op jit(solution)/shard_map/ppermute | solution.py:196

commit v2 on v0

v2 whole, which is shorter than its diff:
```python
import functools

import jax
import jax.numpy as jnp
from jax import lax
from jax.experimental import pallas as pl
from jax.experimental.pallas import tpu as pltpu
from jax.sharding import PartitionSpec as P

STEPS = 3
LAGS = 3
VMEM = pl.BlockSpec(memory_space=pltpu.VMEM)
HBM = pl.BlockSpec(memory_space=pltpu.HBM)
LIMIT = 32 * 1024 * 1024
F32 = jnp.float32
BF16 = jnp.bfloat16


def split(value):
    high = value.astype(BF16)
    low = (value - high.astype(F32)).astype(BF16)
    return high, low


def call(kernel, out_shape, args, scratch=(), specs=None, flops=0, moved=0):
    single = not isinstance(out_shape, (list, tuple))
    return pl.pallas_call(
        kernel,
        out_shape=out_shape,
        in_specs=specs or [VMEM] * len(args),
        out_specs=VMEM if single else [VMEM] * len(out_shape),
        scratch_shapes=list(scratch),
        compiler_params=pltpu.CompilerParams(vmem_limit_bytes=LIMIT),
        cost_estimate=pl.CostEstimate(flops=flops, bytes_accessed=moved, transcendentals=0),
    )(*args)


def place(pieces, lats, lat):
    if pieces != 2:
        return lat
    return jnp.where(lax.axis_index("rows") == 0, lats - 1 - lat, lat)


def advance(state, ops, weights, first, last, before):
    lats = state.shape[0]
    own = state[first]
    for at in range(first, last):
        after = state[at + 1] if at + 1 < lats else None
        mixed = weights[at, 0:1, :] * own
        if after is not None:
            mixed = mixed + weights[at, 1:2, :] * after
        if before is not None:
            mixed = mixed + weights[at, 2:3, :] * before
        high, low = split(mixed)
        state[at] = jnp.dot(
            jnp.concatenate([high, low, high], axis=1), ops[at], preferred_element_type=F32
        )
        before, own = own, after
    return before


def packet_kernel(share, zonal, stencil, packet, held, sems):
    part = lax.axis_index("cols") % share
    lat_rows, lons = zonal.shape[:2]
    count = lat_rows // share
    copies = [
        pltpu.make_async_copy(
            zonal.at[part * count + i], packet.at[pl.ds(i * lons, lons)], sems.at[i]
        )
        for i in range(count)
    ]
    copies.append(pltpu.make_async_copy(stencil, held, sems.at[count]))
    for copy in copies:
        copy.start()
    copies[-1].wait()
    for i in range(count):
        for k in range(3):
            row = count * lons + 3 * i + k
            packet[row : row + 1, :] = held[k, pl.ds(part * count + i, 1), :]
    for copy in copies[:-1]:
        copy.wait()


def cut_kernel(pieces, block, packet, *refs):
    outs, held, sems = refs[:pieces], refs[pieces], refs[pieces + 1]
    me = lax.axis_index("rows")
    tall, wide = block.shape
    width = wide // pieces
    chunk = min(tall, 128)
    copies = [
        pltpu.make_async_copy(
            block.at[pl.ds(first, chunk)], held.at[pl.ds(first, chunk)], sems.at[first // chunk]
        )
        for first in range(0, tall, chunk)
    ]
    for copy in copies:
        copy.start()
    for first, copy in zip(range(0, tall, chunk), copies):
        copy.wait()
        turned = held[first : first + chunk, :].T
        for piece in range(pieces):
            for partner in range(pieces):

                @pl.when((me ^ partner) == piece)
                def _():
                    outs[partner][:, first : first + chunk] = turned[piece * width : (piece + 1) * width]


def put(ops, weights, at, flipped, matrix, coeffs):
    high, low = split(matrix.T)
    ops[at] = jnp.concatenate([high, high, low], axis=0)
    own, north, south = coeffs
    weights[at, 0:1, :] = own
    weights[at, 1:2, :] = jnp.where(flipped, south, north)
    weights[at, 2:3, :] = jnp.where(flipped, north, south)


def steps(state, ops, weights, count):
    lats = state.shape[0]

    def one(step, carry):
        advance(state, ops, weights, 0, lats, None)
        return carry

    lax.fori_loop(0, count, one, 0, unroll=lats * count <= 128)


def load_kernel(pieces, *refs):
    blocks = refs[:pieces]
    zonal, stencil, state, ops, weights = refs[pieces:]
    me = lax.axis_index("rows")
    lat_rows, lons = zonal.shape[:2]
    lats = pieces * lat_rows
    flipped = place(pieces, lats, 0) != 0
    for lat in range(lat_rows):
        coeffs = [stencil[k, lat : lat + 1, :] for k in range(3)]
        put(ops, weights, lat, flipped, zonal[lat], coeffs)
    for partner in range(pieces):
        for lat in range(lat_rows):
            at = place(pieces, lats, (me ^ partner) * lat_rows + lat)
            state[at] = blocks[partner][:, lat * lons : (lat + 1) * lons]


def first_kernel(pieces, share, cols, *refs):
    n_packets = (pieces - 1) * share
    packets = refs[:n_packets]
    given, own_ops, own_weights, out, ops, weights, state = refs[n_packets:]
    me = lax.axis_index("rows")
    part = lax.axis_index("cols") % share
    lats, width, lons = given.shape
    lat_rows = lats // pieces
    count = lat_rows // share
    flipped = place(pieces, lats, 0) != 0
    for partner in range(1, pieces):
        for other in range(share):
            packet = packets[(partner - 1) * share + other]
            first = (me ^ partner) * lat_rows + (part ^ other) * count
            for i in range(count):
                row = count * lons + 3 * i
                coeffs = [packet[row + k : row + k + 1, :] for k in range(3)]
                matrix = packet[i * lons : (i + 1) * lons, :]
                put(ops, weights, place(pieces, lats, first + i), flipped, matrix, coeffs)
    for lat in range(lat_rows):
        at = place(pieces, lats, me * lat_rows + lat)
        ops[at] = own_ops[lat]
        weights[at] = own_weights[lat]
    for at in range(lats):
        state[at] = given[at]
    steps(state, ops, weights, STEPS)
    fold = lons // width
    short = width // fold
    for at in range(lats):
        lat = place(pieces, lats, at)
        turned = state[at].T
        for sub in range(fold):
            index = lat * fold + sub
            out[index % pieces * cols + index // pieces] = jnp.concatenate(
                [
                    turned[sub * width + i * short : sub * width + (i + 1) * short]
                    for i in range(fold)
                ],
                axis=1,
            )


def second_kernel(pieces, cols, lat_rows, moved, ops, weights, *refs):
    lats, lons = ops.shape[0], ops.shape[2]
    count = STEPS + LAGS
    me = lax.axis_index("rows")
    outs = refs[: pieces - 1]
    if pieces == 2:
        rest, edge, state = refs[1:]
    else:
        rest, state = refs[pieces - 1 :]
    width = state.shape[1]
    fold = lons // width
    short = width // fold
    for at in range(lats):
        lat = place(pieces, lats, at)
        got = []
        for sub in range(fold):
            index = lat * fold + sub
            got.append(moved[index % pieces * cols + index // pieces])
        for i in range(fold):
            state[at, i * short : (i + 1) * short, :] = jnp.concatenate(
                [block[:, i * width : (i + 1) * width] for block in got], axis=1
            )
    if pieces == 2:
        for step in range(count):
            last = min(lats, lat_rows + count - 1 - step)
            edge[step] = advance(state, ops, weights, 0, last, None)
        for at in range(lat_rows, lats):
            rest[at - lat_rows] = state[at]
    else:
        steps(state, ops, weights, count)
        for lat in range(lat_rows):
            rest[:, lat * lons : (lat + 1) * lons] = state[me * lat_rows + lat]
    for partner in range(1, pieces):
        for lat in range(lat_rows):
            at = place(pieces, lats, (me ^ partner) * lat_rows + lat)
            outs[partner - 1][:, lat * lons : (lat + 1) * lons] = state[at]


def rest_kernel(rest, edge, ops, weights, out, state):
    lat_rows = rest.shape[0]
    lats, lons = ops.shape[0], ops.shape[2]
    count = STEPS + LAGS
    me = lax.axis_index("rows")
    for at in range(lat_rows):
        state[lat_rows + at] = rest[at]
    for step in range(count):
        first = min(lats, lat_rows + count - 1 - step)
        if first < lats:
            advance(state, ops, weights, first, lats, edge[step])
    for lat in range(lat_rows):
        out[:, lat * lons : (lat + 1) * lons] = state[place(2, lats, me * lat_rows + lat)]


def join_kernel(pieces, *refs):
    blocks, out, stack, held, sems = refs[:pieces], *refs[pieces:]
    me = lax.axis_index("rows")
    width, tall = blocks[0].shape
    chunk = min(tall, 128)
    for partner in range(pieces):
        stack[me ^ partner] = blocks[partner][...]
    copies = []
    for first in range(0, tall, chunk):
        rows = jnp.concatenate([stack[i, :, first : first + chunk] for i in range(pieces)], axis=0)
        held[first : first + chunk, :] = rows.T
        copies.append(
            pltpu.make_async_copy(
                held.at[pl.ds(first, chunk)], out.at[pl.ds(first, chunk)], sems.at[first // chunk]
            )
        )
        copies[-1].start()
    for copy in copies:
        copy.wait()


def on_device(covariance, zonal, stencil):
    pieces = lax.axis_size("rows")
    cols = lax.axis_size("cols")
    tall, wide = covariance.shape
    lat_rows, lons = zonal.shape[:2]
    lats = lat_rows * pieces
    width = wide // pieces
    share = 4
    count = lat_rows // share
    chunks = tall // min(tall, 128)

    def row_swap(value, partner):
        return lax.ppermute(value, "rows", [(i, i ^ partner) for i in range(pieces)])

    def col_swap(value, partner):
        return lax.ppermute(value, "cols", [(i, i ^ partner) for i in range(cols)])

    coeffs = stencil.transpose(1, 0, 2)
    rows = count * lons + -(-3 * count // 8) * 8
    packet = call(
        functools.partial(packet_kernel, share),
        jax.ShapeDtypeStruct((rows, lons), F32),
        (zonal, coeffs),
        [pltpu.VMEM(coeffs.shape, F32), pltpu.SemaphoreType.DMA((count + 1,))],
        [HBM, HBM],
        moved=rows * lons * 8,
    )
    strip = jax.ShapeDtypeStruct((width, tall), F32)
    cut = call(
        functools.partial(cut_kernel, pieces),
        [strip] * pieces,
        (covariance, packet),
        [pltpu.VMEM((tall, wide), F32), pltpu.SemaphoreType.DMA((chunks,))],
        [HBM, VMEM],
        moved=tall * wide * 8,
    )
    packets = []
    for partner in range(1, pieces):
        direct = row_swap(packet, partner)
        across = col_swap(direct, 2)
        packets += [direct, col_swap(direct, 1), across, col_swap(across, 1)]
    blocks = [cut[0]] + [row_swap(cut[partner], partner) for partner in range(1, pieces)]
    state = pltpu.VMEM((lats, width, lons), F32)

    def operators(number):
        return [
            jax.ShapeDtypeStruct((number, 3 * lons, lons), BF16),
            jax.ShapeDtypeStruct((number, 8, lons), F32),
        ]

    loaded = call(
        functools.partial(load_kernel, pieces),
        [jax.ShapeDtypeStruct((lats, width, lons), F32)] + operators(lat_rows),
        (*blocks, zonal, coeffs),
        flops=10**10,
        moved=10**7,
    )
    sent, ops, weights = call(
        functools.partial(first_kernel, pieces, share, cols),
        [jax.ShapeDtypeStruct((pieces * cols, width * width // lons, lons), F32)] + operators(lats),
        (*packets, *loaded),
        [state],
        flops=STEPS * lats * lons * lons * width * 6,
    )
    moved = lax.all_to_all(sent, ("rows", "cols"), 0, 0, tiled=True)
    if pieces == 2:
        end, rest, edge = call(
            functools.partial(second_kernel, pieces, cols, lat_rows),
            [
                strip,
                jax.ShapeDtypeStruct((lat_rows, width, lons), F32),
                jax.ShapeDtypeStruct((STEPS + LAGS, width, lons), F32),
            ],
            (moved, ops, weights),
            [state],
            flops=(STEPS + LAGS) * lats * lons * lons * width * 6,
        )
        ends = [end]
        mine = call(
            rest_kernel,
            strip,
            (rest, edge, ops, weights),
            [state],
            flops=(STEPS + LAGS) * lat_rows * lons * lons * width * 6,
        )
    else:
        *ends, mine = call(
            functools.partial(second_kernel, pieces, cols, lat_rows),
            [strip] * pieces,
            (moved, ops, weights),
            [state],
            flops=(STEPS + LAGS) * lats * lons * lons * width * 6,
        )
    blocks = [mine] + [row_swap(ends[partner - 1], partner) for partner in range(1, pieces)]
    return pl.pallas_call(
        functools.partial(join_kernel, pieces),
        out_shape=jax.ShapeDtypeStruct((tall, wide), F32),
        in_specs=[VMEM] * pieces,
        out_specs=HBM,
        scratch_shapes=[
            pltpu.VMEM((pieces, width, tall), F32),
            pltpu.VMEM((tall, wide), F32),
            pltpu.SemaphoreType.DMA((chunks,)),
        ],
        compiler_params=pltpu.CompilerParams(vmem_limit_bytes=LIMIT),
    )(*blocks)


def solution(mesh):
    placed = (P("rows", "cols"), P("rows", None, None), P("rows", None, None))
    return jax.shard_map(
        on_device, mesh=mesh, in_specs=placed, out_specs=P("rows", "cols"), check_vma=False
    )
```

time: 150 us -> 49.7 us (0.33)
  blocking collectives: 48.1 us -> 20.6 us
  starting transfers between devices: 32 us -> 5.93 us
  waiting for transfers between devices: 35.6 us -> 11.9 us
  matrix products: 14.3 us -> 0 us
  between operations: 13.8 us -> 0.06 us
  Pallas kernels: 0 us -> 7.03 us
    all_to_all x3 -> x1, blocking collectives: 48.1 us -> 20.6 us  [on_device(): moved = lax.all_to_all(sent, ('rows', 'cols'), 0, 0, tiled=True)]
    ppermute x12 -> x6, starting transfers between devices: 32 us -> 5.93 us  [the longest x3 4.21 us: row_swap(): lax.ppermute(value, 'rows', [(i, i ^ partner) for i in range(pieces)])]
    psum x1 -> x0, waiting for transfers between devices: 19.4 us -> none  [from_root(): return lax.psum(jnp.where(mine, value, jnp.zeros_like(value)), axis)]
    dot_general x9 -> x0, matrix products: 14.3 us -> none  [the longest x6 9.57 us: rows_local(): jnp.einsum('lij,ljc->lic', zonal_mats, mixed, precision=lax.Precision.HIG...]
    pallas_call x0 -> x7, Pallas kernels: none -> 7.03 us  [the longest x6 6.04 us: call(): pl.pallas_call(kernel, out_shape=out_shape, in_specs=specs or [VMEM] * le...]
    ppermute x12 -> x6, waiting for transfers between devices: 16.2 us -> 11.9 us  [the longest x3 8.56 us: row_swap(): lax.ppermute(value, 'rows', [(i, i ^ partner) for i in range(pieces)])]
    unnamed x13 -> x8, local copies, waits for them, and re-layouts: 1.04 us -> 3.83 us
  transfers between devices with their start and end apart: 13 -> 6, of which waited for: 9 -> 4; matrix products, arithmetic and copies ran while one was open for 5% -> 0% of each run, Pallas kernels for 0% -> 6%
where the time goes in v2:
time: 49.7 us; the launch traced here: 49.3 us
  blocking collectives  20.6 us (41%)
  waiting for transfers between devices  11.9 us (24%)
  Pallas kernels  7.03 us (14%)
  starting transfers between devices  5.93 us (12%)
  local copies, waits for them, and re-layouts  3.83 us (8%)
    all_to_all x1, blocking collectives, on_device(): moved = lax.all_to_all(sent, ('rows', 'cols'), 0, 0, tiled=True)  20.6 us
    ppermute x3, waiting for transfers between devices, row_swap(): lax.ppermute(value, 'rows', [(i, i ^ partner) for i in range(pieces)])  8.56 us
    pallas_call x6, Pallas kernels, call(): pl.pallas_call(kernel, out_shape=out_shape, in_specs=specs or [VMEM] * le...  6.04 us
    ppermute x3, starting transfers between devices, row_swap(): lax.ppermute(value, 'rows', [(i, i ^ partner) for i in range(pieces)])  4.21 us
    unnamed x8, local copies, waits for them, and re-layouts  3.83 us
    ppermute x3, waiting for transfers between devices, col_swap(): return lax.ppermute(value, 'cols', [(i, i ^ partner) for i in range(cols)])  3.3 us
    ppermute x3, starting transfers between devices, col_swap(): return lax.ppermute(value, 'cols', [(i, i ^ partner) for i in range(cols)])  1.72 us
  transfers between devices with their start and end apart: 6, of which 4 were waited for; matrix products, arithmetic and copies ran while one was open for 0% of the time, Pallas kernels for 6%

profile of v2, /device:TPU:0, one launch (start us, length us, event | category | flops | bytes accessed | tf_op | source)
XLA Modules:
  0.0 49.3 jit_solution(2523206796348744165)
XLA Ops:
  0.0 0.0 copy-start.1
  0.0 1.0 %copy-done.1 = f32[8,128,128]{2,1,0:T(8,128)S(1)} copy-done((f32[8,128,128]{2,1,0:T(8,128)S(1)}, f32[8,128,128]{2,1,0:T(8,128)}, u32[]{:S(2)}) %copy-start.1) | copy-done | bytes 524312
  1.0 0.0 copy-start.3
  1.0 0.7 %copy-done.3 = f32[8,3,128]{2,0,1:T(8,128)S(1)} copy-done((f32[8,3,128]{2,0,1:T(8,128)S(1)}, f32[8,3,128]{2,0,1:T(8,128)}, u32[]{:S(2)}) %copy-start.3) | copy-done | bytes 12312
  1.8 0.2 shard_map.37.packet
  1.9 3.0 %collective-permute-start = (f32[264,128]{1,0:T(8,128)S(1)}, f32[264,128]{1,0:T(8,128)S(1)}, u32[]{:S(2)}, u32[]{:S(2)}) collective-permute-start(f32[264,128]{1,0:T(8,128)S(1)} %shard_map.37.packet), channel_id=1, source_target_pairs={{0,16},{16,0},{1,17},{17,1},{2,18},{18,2},{3,19},{19,3},{4,20},{20... | collective-permute-start | bytes 405512 | tf_op jit(solution)/shard_map/ppermute | solution.py:272
  5.0 0.0 copy-start
  5.0 1.0 %copy-done = f32[1024,128]{1,0:T(8,128)S(1)} copy-done((f32[1024,128]{1,0:T(8,128)S(1)}, f32[1024,128]{1,0:T(8,128)}, u32[]{:S(2)}) %copy-start) | copy-done | bytes 524312
  6.0 1.5 %shard_map.38 = (f32[64,1024]{1,0:T(8,128)S(1)}, f32[64,1024]{1,0:T(8,128)S(1)}) custom-call(f32[1024,128]{1,0:T(8,128)S(1)} %copy-done, f32[264,128]{1,0:T(8,128)S(1)} %shard_map.37.packet), custom_call_target="tpu_custom_call" | custom-call | bytes 1048576 | tf_op jit(solution)/shard_map/pallas_call | solution.py:27
  7.6 0.1 collective-permute-start.4
  7.7 0.9 %collective-permute-done.refs_0_ = f32[264,128]{1,0:T(8,128)S(1)} collective-permute-done((f32[264,128]{1,0:T(8,128)S(1)}, f32[264,128]{1,0:T(8,128)S(1)}, u32[]{:S(2)}, u32[]{:S(2)}) %collective-permute-start) | collective-permute-done | bytes 135200 | tf_op jit(solution)/shard_map/ppermute | solution.py:272
  8.6 1.7 %collective-permute-start.2 = (f32[264,128]{1,0:T(8,128)S(1)}, f32[264,128]{1,0:T(8,128)S(1)}, u32[]{:S(2)}, u32[]{:S(2)}) collective-permute-start(f32[264,128]{1,0:T(8,128)S(1)} %collective-permute-done.refs_0_), channel_id=1, source_target_pairs={{0,2},{1,3},{2,0},{3,1},{4,6},{5,7},{6,4},{7,5},{8,10},{9,11},{10,... | collective-permute-start | bytes 405512 | tf_op jit(solution)/shard_map/ppermute | solution.py:275
  10.3 0.0 collective-permute-start.1
  10.3 3.3 %collective-permute-done.2.refs_2_ = f32[264,128]{1,0:T(8,128)S(1)} collective-permute-done((f32[264,128]{1,0:T(8,128)S(1)}, f32[264,128]{1,0:T(8,128)S(1)}, u32[]{:S(2)}, u32[]{:S(2)}) %collective-permute-start.2) | collective-permute-done | bytes 135200 | tf_op jit(solution)/shard_map/ppermute | solution.py:275
  13.6 0.0 collective-permute-start.3
  13.6 1.8 %collective-permute-done.4.refs_1_ = f32[64,1024]{1,0:T(8,128)S(1)} collective-permute-done((f32[64,1024]{1,0:T(8,128)S(1)}, f32[64,1024]{1,0:T(8,128)S(1)}, u32[]{:S(2)}, u32[]{:S(2)}) %collective-permute-start.4) | collective-permute-done | bytes 262176 | tf_op jit(solution)/shard_map/ppermute | solution.py:272
  15.4 0.0 copy-start.2
  15.4 1.0 %copy-done.2 = f32[8,128,128]{2,1,0:T(8,128)S(1)} copy-done((f32[8,128,128]{2,1,0:T(8,128)S(1)}, f32[8,128,128]{2,1,0:T(8,128)}, u32[]{:S(2)}) %copy-start.2) | copy-done | bytes 524312
  16.4 0.2 shard_map.39
  16.6 0.0 collective-permute-done.1.refs_1_
  16.7 0.0 collective-permute-done.3.refs_3_
  16.7 1.8 %shard_map.40 = (f32[32,32,128]{2,1,0:T(8,128)S(1)}, bf16[16,384,128]{2,1,0:T(8,128)(2,1)S(1)}, f32[16,8,128]{2,1,0:T(8,128)S(1)}) custom-call(f32[264,128]{1,0:T(8,128)S(1)} %collective-permute-done.refs_0_, f32[264,128]{1,0:T(8,128)S(1)} %collective-permute-done.1.refs_1_, f32[264,128]{1,0:T(8,128)S(1)} %collective-permute-done.2.refs_2_, ...), custom_call_target="tpu_custom_call" | custom-call | flops 301989888 | tf_op jit(solution)/shard_map/pallas_call | solution.py:27
  18.5 20.6 %all_to_all.5.moved = f32[32,32,128]{2,1,0:T(8,128)S(1)} all-to-all(f32[32,32,128]{2,1,0:T(8,128)S(1)} %get-tuple-element.21), channel_id=1, replica_groups=mesh['rows'=2,'cols'=16] {'rows','cols'}, dimensions={0} | all-to-all | bytes 1048576 | tf_op jit(solution)/shard_map/all_to_all | solution.py:324
  39.1 1.3 %shard_map.41 = (f32[64,1024]{1,0:T(8,128)S(1)}, f32[8,64,128]{2,1,0:T(8,128)S(1)}, f32[6,64,128]{2,1,0:T(8,128)S(1)}) custom-call(f32[32,32,128]{2,1,0:T(8,128)S(1)} %all_to_all.5.moved, bf16[16,384,128]{2,1,0:T(8,128)(2,1)S(1)} %get-tuple-element.22.ops, f32[16,8,128]{2,1,0:T(8,128)S(1)} %get-tuple-element.23.weights), custom_call_target="tpu_custom_call" | custom-call | flops 603979776 | tf_op jit(solution)/shard_map/pallas_call | solution.py:27
  40.4 1.1 %collective-permute-start.5 = (f32[64,1024]{1,0:T(8,128)S(1)}, f32[64,1024]{1,0:T(8,128)S(1)}, u32[]{:S(2)}, u32[]{:S(2)}) collective-permute-start(f32[64,1024]{1,0:T(8,128)S(1)} %get-tuple-element.26), channel_id=1, source_target_pairs={{0,16},{16,0},{1,17},{17,1},{2,18},{18,2},{3,19},{19,3},{4,20},{20... | collective-permute-start | bytes 786440 | tf_op jit(solution)/shard_map/ppermute | solution.py:272
  41.5 1.0 %shard_map.42.refs_0_ = f32[64,1024]{1,0:T(8,128)S(1)} custom-call(f32[8,64,128]{2,1,0:T(8,128)S(1)} %get-tuple-element.24.rest, f32[6,64,128]{2,1,0:T(8,128)S(1)} %get-tuple-element.25.edge, bf16[16,384,128]{2,1,0:T(8,128)(2,1)S(1)} %get-tuple-element.22.ops, f32[16,8,128]{2,1,0:T(8,128)S(1)} %get-tuple-element.23.weights), custom_call_target="tpu_custom_call" | custom-call | flops 301989888 | tf_op jit(solution)/shard_map/pallas_call | solution.py:27
  42.5 5.9 %collective-permute-done.5.refs_1_ = f32[64,1024]{1,0:T(8,128)S(1)} collective-permute-done((f32[64,1024]{1,0:T(8,128)S(1)}, f32[64,1024]{1,0:T(8,128)S(1)}, u32[]{:S(2)}, u32[]{:S(2)}) %collective-permute-start.5) | collective-permute-done | bytes 262176 | tf_op jit(solution)/shard_map/ppermute | solution.py:272
  48.3 1.0 %shard_map.43 = f32[1024,128]{1,0:T(8,128)} custom-call(f32[64,1024]{1,0:T(8,128)S(1)} %shard_map.42.refs_0_, f32[64,1024]{1,0:T(8,128)S(1)} %collective-permute-done.5.refs_1_), custom_call_target="tpu_custom_call" | custom-call | tf_op jit(solution)/shard_map/pallas_call | solution.py:354
Async XLA Ops:
  0.0 1.0 %copy-start.1 = (f32[8,128,128]{2,1,0:T(8,128)S(1)}, f32[8,128,128]{2,1,0:T(8,128)}, u32[]{:S(2)}) copy-start(f32[8,128,128]{2,1,0:T(8,128)} %refs_2_.1) | copy-start | bytes 1572868
  1.0 0.7 %copy-start.3 = (f32[8,3,128]{2,0,1:T(8,128)S(1)}, f32[8,3,128]{2,0,1:T(8,128)}, u32[]{:S(2)}) copy-start(f32[8,3,128]{2,0,1:T(8,128)} %param.5) | copy-start | bytes 36868
  1.9 6.6 %collective-permute-start = (f32[264,128]{1,0:T(8,128)S(1)}, f32[264,128]{1,0:T(8,128)S(1)}, u32[]{:S(2)}, u32[]{:S(2)}) collective-permute-start(f32[264,128]{1,0:T(8,128)S(1)} %shard_map.37.packet), channel_id=1, source_target_pairs={{0,16},{16,0},{1,17},{17,1},{2,18},{18,2},{3,19},{19,3},{4,20},{20... | collective-permute-start | bytes 405512 | tf_op jit(solution)/shard_map/ppermute | solution.py:272
  5.0 1.0 %copy-start = (f32[1024,128]{1,0:T(8,128)S(1)}, f32[1024,128]{1,0:T(8,128)}, u32[]{:S(2)}) copy-start(f32[1024,128]{1,0:T(8,128)} %block.1) | copy-start | bytes 1572868
  7.6 7.8 %collective-permute-start.4 = (f32[64,1024]{1,0:T(8,128)S(1)}, f32[64,1024]{1,0:T(8,128)S(1)}, u32[]{:S(2)}, u32[]{:S(2)}) collective-permute-start(f32[64,1024]{1,0:T(8,128)S(1)} %get-tuple-element.17), channel_id=1, source_target_pairs={{0,16},{16,0},{1,17},{17,1},{2,18},{18,2},{3,19},{19,3},{4,20},{20... | collective-permute-start | bytes 786440 | tf_op jit(solution)/shard_map/ppermute | solution.py:272
  8.6 5.0 %collective-permute-start.2 = (f32[264,128]{1,0:T(8,128)S(1)}, f32[264,128]{1,0:T(8,128)S(1)}, u32[]{:S(2)}, u32[]{:S(2)}) collective-permute-start(f32[264,128]{1,0:T(8,128)S(1)} %collective-permute-done.refs_0_), channel_id=1, source_target_pairs={{0,2},{1,3},{2,0},{3,1},{4,6},{5,7},{6,4},{7,5},{8,10},{9,11},{10,... | collective-permute-start | bytes 405512 | tf_op jit(solution)/shard_map/ppermute | solution.py:275
  10.3 6.4 %collective-permute-start.1 = (f32[264,128]{1,0:T(8,128)S(1)}, f32[264,128]{1,0:T(8,128)S(1)}, u32[]{:S(2)}, u32[]{:S(2)}) collective-permute-start(f32[264,128]{1,0:T(8,128)S(1)} %collective-permute-done.refs_0_), channel_id=1, source_target_pairs={{0,1},{1,0},{2,3},{3,2},{4,5},{5,4},{6,7},{7,6},{8,9},{9,8},{10,11... | collective-permute-start | bytes 405512 | tf_op jit(solution)/shard_map/ppermute | solution.py:275
  13.6 3.1 %collective-permute-start.3 = (f32[264,128]{1,0:T(8,128)S(1)}, f32[264,128]{1,0:T(8,128)S(1)}, u32[]{:S(2)}, u32[]{:S(2)}) collective-permute-start(f32[264,128]{1,0:T(8,128)S(1)} %collective-permute-done.2.refs_2_), channel_id=1, source_target_pairs={{0,1},{1,0},{2,3},{3,2},{4,5},{5,4},{6,7},{7,6},{8,9},{9,8},{10,11... | collective-permute-start | bytes 405512 | tf_op jit(solution)/shard_map/ppermute | solution.py:275
  15.4 1.0 %copy-start.2 = (f32[8,128,128]{2,1,0:T(8,128)S(1)}, f32[8,128,128]{2,1,0:T(8,128)}, u32[]{:S(2)}) copy-start(f32[8,128,128]{2,1,0:T(8,128)} %refs_2_.1) | copy-start | bytes 1572868
  40.4 7.9 %collective-permute-start.5 = (f32[64,1024]{1,0:T(8,128)S(1)}, f32[64,1024]{1,0:T(8,128)S(1)}, u32[]{:S(2)}, u32[]{:S(2)}) collective-permute-start(f32[64,1024]{1,0:T(8,128)S(1)} %get-tuple-element.26), channel_id=1, source_target_pairs={{0,16},{16,0},{1,17},{17,1},{2,18},{18,2},{3,19},{19,3},{4,20},{20... | collective-permute-start | bytes 786440 | tf_op jit(solution)/shard_map/ppermute | solution.py:272

commit v3 on v2

--- a/solution.py
+++ b/solution.py
@@ -13,6 +13,7 @@
 HBM = pl.BlockSpec(memory_space=pltpu.HBM)
 LIMIT = 32 * 1024 * 1024
 F32 = jnp.float32
+FLOPS = 10**9
 BF16 = jnp.bfloat16
 
 
@@ -41,69 +42,49 @@
     return jnp.where(lax.axis_index("rows") == 0, lats - 1 - lat, lat)
 
 
-def advance(state, ops, weights, first, last, before):
+def advance(state, ops, weights, first, last, before, beyond=None, shift=0):
     lats = state.shape[0]
     own = state[first]
     for at in range(first, last):
-        after = state[at + 1] if at + 1 < lats else None
-        mixed = weights[at, 0:1, :] * own
+        after = None
+        if at + 1 < lats:
+            after = state[at + 1] if beyond is None or at + 1 < last else beyond
+        mixed = weights[at - shift, 0:1, :] * own
         if after is not None:
-            mixed = mixed + weights[at, 1:2, :] * after
+            mixed = mixed + weights[at - shift, 1:2, :] * after
         if before is not None:
-            mixed = mixed + weights[at, 2:3, :] * before
+            mixed = mixed + weights[at - shift, 2:3, :] * before
         high, low = split(mixed)
         state[at] = jnp.dot(
-            jnp.concatenate([high, low, high], axis=1), ops[at], preferred_element_type=F32
+            jnp.concatenate([high, low, high], axis=1), ops[at - shift], preferred_element_type=F32
         )
         before, own = own, after
     return before
 
 
-def packet_kernel(share, zonal, stencil, packet, held, sems):
+def packet_kernel(share, zonal, stencil, packet, stencil_out, sems):
     part = lax.axis_index("cols") % share
     lat_rows, lons = zonal.shape[:2]
     count = lat_rows // share
-    copies = [
-        pltpu.make_async_copy(
-            zonal.at[part * count + i], packet.at[pl.ds(i * lons, lons)], sems.at[i]
-        )
-        for i in range(count)
-    ]
-    copies.append(pltpu.make_async_copy(stencil, held, sems.at[count]))
+    copies = [pltpu.make_async_copy(stencil, stencil_out, sems.at[count])]
+    for i in range(count):
+        target = packet.at[pl.ds(i * lons, lons)]
+        copies.append(pltpu.make_async_copy(zonal.at[part * count + i], target, sems.at[i]))
     for copy in copies:
         copy.start()
-    copies[-1].wait()
+    copies[0].wait()
     for i in range(count):
         for k in range(3):
             row = count * lons + 3 * i + k
-            packet[row : row + 1, :] = held[k, pl.ds(part * count + i, 1), :]
-    for copy in copies[:-1]:
+            packet[row : row + 1, :] = stencil_out[k, pl.ds(part * count + i, 1), :]
+    for copy in copies[1:]:
         copy.wait()
 
 
-def cut_kernel(pieces, block, packet, *refs):
-    outs, held, sems = refs[:pieces], refs[pieces], refs[pieces + 1]
-    me = lax.axis_index("rows")
-    tall, wide = block.shape
-    width = wide // pieces
-    chunk = min(tall, 128)
-    copies = [
-        pltpu.make_async_copy(
-            block.at[pl.ds(first, chunk)], held.at[pl.ds(first, chunk)], sems.at[first // chunk]
-        )
-        for first in range(0, tall, chunk)
-    ]
-    for copy in copies:
-        copy.start()
-    for first, copy in zip(range(0, tall, chunk), copies):
-        copy.wait()
-        turned = held[first : first + chunk, :].T
-        for piece in range(pieces):
-            for partner in range(pieces):
-
-                @pl.when((me ^ partner) == piece)
-                def _():
-                    outs[partner][:, first : first + chunk] = turned[piece * width : (piece + 1) * width]
+def merge_kernel(*refs):
+    *packets, out = refs
+    for i, packet in enumerate(packets):
+        out[i] = packet[...]
 
 
 def put(ops, weights, at, flipped, matrix, coeffs):
@@ -125,48 +106,99 @@
     lax.fori_loop(0, count, one, 0, unroll=lats * count <= 128)
 
 
-def load_kernel(pieces, *refs):
-    blocks = refs[:pieces]
-    zonal, stencil, state, ops, weights = refs[pieces:]
-    me = lax.axis_index("rows")
-    lat_rows, lons = zonal.shape[:2]
+def cut_kernel(pieces, block, zonal, stencil, *refs):
+    outs, ops, weights = refs[:pieces], *refs[pieces : pieces + 2]
+    held, matrices, sems = refs[pieces + 2 :]
+    me = lax.axis_index("rows")
+    tall, wide = block.shape
+    lat_rows = zonal.shape[0]
     lats = pieces * lat_rows
+    width = wide // pieces
+    chunk = min(tall, 128)
+    starts = range(0, tall, chunk)
+    copies = [
+        pltpu.make_async_copy(
+            block.at[pl.ds(first, chunk)], held.at[pl.ds(first, chunk)], sems.at[first // chunk]
+        )
+        for first in starts
+    ]
+    copies += [
+        pltpu.make_async_copy(zonal.at[lat], matrices.at[lat], sems.at[len(starts) + lat])
+        for lat in range(lat_rows)
+    ]
+    for copy in copies:
+        copy.start()
+    for copy in copies[: len(starts)]:
+        copy.wait()
+    for first in starts:
+        turned = held[first : first + chunk, :].T
+        for partner in range(pieces):
+            piece = turned[:width]
+            for other in range(1, pieces):
+                piece = jnp.where((me ^ partner) == other, turned[other * width : (other + 1) * width], piece)
+            outs[partner][:, first : first + chunk] = piece
+    for copy in copies[len(starts) :]:
+        copy.wait()
     flipped = place(pieces, lats, 0) != 0
     for lat in range(lat_rows):
         coeffs = [stencil[k, lat : lat + 1, :] for k in range(3)]
-        put(ops, weights, lat, flipped, zonal[lat], coeffs)
+        at = place(2, lats, me * lat_rows + lat) - lat_rows if pieces == 2 else lat
+        put(ops, weights, at, flipped, matrices[lat], coeffs)
+
+
+def load_kernel(pieces, lat_rows, *refs):
+    blocks = refs[:pieces]
+    if pieces == 2:
+        own_ops, own_weights, state, edge = refs[pieces:]
+    else:
+        state = refs[pieces]
+    me = lax.axis_index("rows")
+    lats, lons = state.shape[0], state.shape[2]
     for partner in range(pieces):
         for lat in range(lat_rows):
             at = place(pieces, lats, (me ^ partner) * lat_rows + lat)
             state[at] = blocks[partner][:, lat * lons : (lat + 1) * lons]
-
-
-def first_kernel(pieces, share, cols, *refs):
-    n_packets = (pieces - 1) * share
+    if pieces == 2:
+        for step in range(STEPS):
+            first = lat_rows + step
+            edge[step] = state[first]
+            advance(state, own_ops, own_weights, first, lats, state[first - 1], shift=lat_rows)
+
+
+def first_kernel(pieces, cols, hops, *refs):
+    n_packets = 2 * (pieces - 1)
     packets = refs[:n_packets]
-    given, own_ops, own_weights, out, ops, weights, state = refs[n_packets:]
+    own_ops, own_weights, given = refs[n_packets : n_packets + 3]
+    out, ops, weights, state = refs[-4:]
+    share = 2 * len(hops)
     me = lax.axis_index("rows")
     part = lax.axis_index("cols") % share
-    lats, width, lons = given.shape
+    lats, width, lons = state.shape
     lat_rows = lats // pieces
     count = lat_rows // share
     flipped = place(pieces, lats, 0) != 0
-    for partner in range(1, pieces):
-        for other in range(share):
-            packet = packets[(partner - 1) * share + other]
-            first = (me ^ partner) * lat_rows + (part ^ other) * count
-            for i in range(count):
-                row = count * lons + 3 * i
-                coeffs = [packet[row + k : row + k + 1, :] for k in range(3)]
-                matrix = packet[i * lons : (i + 1) * lons, :]
-                put(ops, weights, place(pieces, lats, first + i), flipped, matrix, coeffs)
     for lat in range(lat_rows):
-        at = place(pieces, lats, me * lat_rows + lat)
+        at = lat_rows + lat if pieces == 2 else me * lat_rows + lat
         ops[at] = own_ops[lat]
         weights[at] = own_weights[lat]
+    for partner in range(1, pieces):
+        for core in range(2):
+            packet = packets[2 * (partner - 1) + core]
+            for at, hop in enumerate(hops):
+                for i in range(count):
+                    lat = (me ^ partner) * lat_rows + (part ^ hop ^ core) * count + i
+                    row = count * lons + 3 * i
+                    coeffs = [packet[at, row + k : row + k + 1, :] for k in range(3)]
+                    matrix = packet[at, i * lons : (i + 1) * lons, :]
+                    put(ops, weights, place(pieces, lats, lat), flipped, matrix, coeffs)
     for at in range(lats):
         state[at] = given[at]
-    steps(state, ops, weights, STEPS)
+    if pieces == 2:
+        edge = refs[n_packets + 3]
+        for step in range(STEPS):
+            advance(state, ops, weights, 0, lat_rows + step, None, edge[step])
+    else:
+        steps(state, ops, weights, STEPS)
     fold = lons // width
     short = width // fold
     for at in range(lats):
@@ -264,7 +296,8 @@
     lat_rows, lons = zonal.shape[:2]
     lats = lat_rows * pieces
     width = wide // pieces
-    share = 4
+    hops = (0, 2, 4, 6) if lat_rows % 8 == 0 and cols % 8 == 0 else (0,)
+    share = 2 * len(hops)
     count = lat_rows // share
     chunks = tall // min(tall, 128)
 
@@ -274,32 +307,11 @@
     def col_swap(value, partner):
         return lax.ppermute(value, "cols", [(i, i ^ partner) for i in range(cols)])
 
-    coeffs = stencil.transpose(1, 0, 2)
+    coeffs = pltpu.with_memory_space_constraint(stencil.transpose(1, 0, 2), pltpu.HBM)
+    given = pltpu.with_memory_space_constraint(zonal, pltpu.HBM)
+    block = pltpu.with_memory_space_constraint(covariance, pltpu.HBM)
     rows = count * lons + -(-3 * count // 8) * 8
-    packet = call(
-        functools.partial(packet_kernel, share),
-        jax.ShapeDtypeStruct((rows, lons), F32),
-        (zonal, coeffs),
-        [pltpu.VMEM(coeffs.shape, F32), pltpu.SemaphoreType.DMA((count + 1,))],
-        [HBM, HBM],
-        moved=rows * lons * 8,
-    )
     strip = jax.ShapeDtypeStruct((width, tall), F32)
-    cut = call(
-        functools.partial(cut_kernel, pieces),
-        [strip] * pieces,
-        (covariance, packet),
-        [pltpu.VMEM((tall, wide), F32), pltpu.SemaphoreType.DMA((chunks,))],
-        [HBM, VMEM],
-        moved=tall * wide * 8,
-    )
-    packets = []
-    for partner in range(1, pieces):
-        direct = row_swap(packet, partner)
-        across = col_swap(direct, 2)
-        packets += [direct, col_swap(direct, 1), across, col_swap(across, 1)]
-    blocks = [cut[0]] + [row_swap(cut[partner], partner) for partner in range(1, pieces)]
-    state = pltpu.VMEM((lats, width, lons), F32)
 
     def operators(number):
         return [
@@ -307,17 +319,54 @@
             jax.ShapeDtypeStruct((number, 8, lons), F32),
         ]
 
+    packet, held_coeffs = call(
+        functools.partial(packet_kernel, share),
+        [jax.ShapeDtypeStruct((rows, lons), F32), jax.ShapeDtypeStruct(coeffs.shape, F32)],
+        (given, coeffs),
+        [pltpu.SemaphoreType.DMA((count + 1,))],
+        [HBM, HBM],
+        moved=10**5,
+    )
+    *cut, own_ops, own_weights = call(
+        functools.partial(cut_kernel, pieces),
+        [strip] * pieces + operators(lat_rows),
+        (block, given, held_coeffs),
+        [
+            pltpu.VMEM((tall, wide), F32),
+            pltpu.VMEM(zonal.shape, F32),
+            pltpu.SemaphoreType.DMA((chunks + lat_rows,)),
+        ],
+        [HBM, HBM, VMEM],
+        moved=tall * wide * 8,
+    )
+    packets = []
+    blocks = [cut[0]]
+    for partner in range(1, pieces):
+        direct = row_swap(packet, partner)
+        merged = call(
+            merge_kernel,
+            jax.ShapeDtypeStruct((len(hops), rows, lons), F32),
+            [direct] + [col_swap(direct, hop) for hop in hops[1:]],
+            moved=10**5,
+        )
+        packets += [merged, col_swap(merged, 1)]
+        blocks.append(row_swap(cut[partner], partner))
+    states = [jax.ShapeDtypeStruct((lats, width, lons), F32)]
+    own = [own_ops, own_weights]
+    if pieces == 2:
+        states.append(jax.ShapeDtypeStruct((STEPS, width, lons), F32))
     loaded = call(
-        functools.partial(load_kernel, pieces),
-        [jax.ShapeDtypeStruct((lats, width, lons), F32)] + operators(lat_rows),
-        (*blocks, zonal, coeffs),
-        flops=10**10,
-        moved=10**7,
+        functools.partial(load_kernel, pieces, lat_rows),
+        states,
+        blocks + own if pieces == 2 else blocks,
+        flops=FLOPS,
+        moved=10**6,
     )
+    state = pltpu.VMEM((lats, width, lons), F32)
     sent, ops, weights = call(
-        functools.partial(first_kernel, pieces, share, cols),
+        functools.partial(first_kernel, pieces, cols, hops),
         [jax.ShapeDtypeStruct((pieces * cols, width * width // lons, lons), F32)] + operators(lats),
-        (*packets, *loaded),
+        (*packets, *own, *loaded),
         [state],
         flops=STEPS * lats * lons * lons * width * 6,
     )

time: 49.7 us -> 48 us (0.966)
  local copies, waits for them, and re-layouts: 3.83 us -> 0 us
  starting transfers between devices: 5.93 us -> 7.83 us
  Pallas kernels: 7.03 us -> 7.66 us
    unnamed x8 -> x0, local copies, waits for them, and re-layouts: 3.83 us -> none
    ppermute x3, waiting for transfers between devices: 8.56 us -> 6.44 us  [row_swap(): lax.ppermute(value, 'rows', [(i, i ^ partner) for i in range(pieces)])]
    ppermute x3 -> x4, starting transfers between devices: 1.72 us -> 3.64 us  [col_swap(): return lax.ppermute(value, 'cols', [(i, i ^ partner) for i in range(cols)])]
    ppermute x3 -> x4, waiting for transfers between devices: 3.3 us -> 5.11 us  [col_swap(): return lax.ppermute(value, 'cols', [(i, i ^ partner) for i in range(cols)])]
    pallas_call x6 -> x7, Pallas kernels: 6.04 us -> 6.66 us  [call(): pl.pallas_call(kernel, out_shape=out_shape, in_specs=specs or [VMEM] * le...]
  transfers between devices with their start and end apart: 6 -> 7, of which waited for: 4 -> 6; matrix products, arithmetic and copies ran while one was open for 0% -> 0% of each run, Pallas kernels for 6% -> 7%
where the time goes in v3:
time: 48 us; the launch traced here: 47.7 us
  blocking collectives  20.6 us (43%)
  waiting for transfers between devices  11.5 us (24%)
  starting transfers between devices  7.83 us (16%)
  Pallas kernels  7.66 us (16%)
    all_to_all x1, blocking collectives, on_device(): moved = lax.all_to_all(sent, ('rows', 'cols'), 0, 0, tiled=True)  20.6 us
    pallas_call x7, Pallas kernels, call(): pl.pallas_call(kernel, out_shape=out_shape, in_specs=specs or [VMEM] * le...  6.66 us
    ppermute x3, waiting for transfers between devices, row_swap(): lax.ppermute(value, 'rows', [(i, i ^ partner) for i in range(pieces)])  6.44 us
    ppermute x4, waiting for transfers between devices, col_swap(): return lax.ppermute(value, 'cols', [(i, i ^ partner) for i in range(cols)])  5.11 us
    ppermute x3, starting transfers between devices, row_swap(): lax.ppermute(value, 'rows', [(i, i ^ partner) for i in range(pieces)])  4.18 us
    ppermute x4, starting transfers between devices, col_swap(): return lax.ppermute(value, 'cols', [(i, i ^ partner) for i in range(cols)])  3.64 us
    pallas_call x1, Pallas kernels, on_device(): pl.pallas_call(functools.partial(join_kernel, pieces), out_shape=jax.Shap...  0.99 us
  transfers between devices with their start and end apart: 7, of which 6 were waited for; matrix products, arithmetic and copies ran while one was open for 0% of the time, Pallas kernels for 7%

profile of v3, /device:TPU:0, one launch (start us, length us, event | category | flops | bytes accessed | tf_op | source)
XLA Modules:
  0.0 47.7 jit_solution(2207749412763290760)
XLA Ops:
  0.0 0.9 %shard_map.37 = (f32[136,128]{1,0:T(8,128)S(1)}, f32[3,8,128]{2,1,0:T(8,128)S(1)}) custom-call(f32[8,128,128]{2,1,0:T(8,128)} %zonal.3, f32[3,8,128]{2,1,0:T(8,128)} %bitcast.1), custom_call_target="tpu_custom_call" | custom-call | bytes 100000 | tf_op jit(solution)/shard_map/pallas_call | solution.py:28
  0.9 3.0 %collective-permute-start = (f32[136,128]{1,0:T(8,128)S(1)}, f32[136,128]{1,0:T(8,128)S(1)}, u32[]{:S(2)}, u32[]{:S(2)}) collective-permute-start(f32[136,128]{1,0:T(8,128)S(1)} %get-tuple-element.19), channel_id=1, source_target_pairs={{0,16},{16,0},{1,17},{17,1},{2,18},{18,2},{3,19},{19,3},{4,20},{20... | collective-permute-start | bytes 208904 | tf_op jit(solution)/shard_map/ppermute | solution.py:305
  3.9 1.6 %shard_map.39 = (f32[64,1024]{1,0:T(8,128)S(1)}, f32[64,1024]{1,0:T(8,128)S(1)}, bf16[8,384,128]{2,1,0:T(8,128)(2,1)S(1)}, f32[8,8,128]{2,1,0:T(8,128)S(1)}) custom-call(f32[1024,128]{1,0:T(8,128)} %block.1, f32[8,128,128]{2,1,0:T(8,128)} %zonal.3, f32[3,8,128]{2,1,0:T(8,128)S(1)} %get-tuple-element.20.stencil), custom_call_target="tpu_custom_call" | custom-call | bytes 1048576 | tf_op jit(solution)/shard_map/pallas_call | solution.py:28
  5.5 0.1 collective-permute-start.5
  5.6 0.6 %collective-permute-done.refs_0_ = f32[136,128]{1,0:T(8,128)S(1)} collective-permute-done((f32[136,128]{1,0:T(8,128)S(1)}, f32[136,128]{1,0:T(8,128)S(1)}, u32[]{:S(2)}, u32[]{:S(2)}) %collective-permute-start) | collective-permute-done | bytes 69664 | tf_op jit(solution)/shard_map/ppermute | solution.py:305
  6.2 3.0 %collective-permute-start.3 = (f32[136,128]{1,0:T(8,128)S(1)}, f32[136,128]{1,0:T(8,128)S(1)}, u32[]{:S(2)}, u32[]{:S(2)}) collective-permute-start(f32[136,128]{1,0:T(8,128)S(1)} %collective-permute-done.refs_0_), channel_id=1, source_target_pairs={{0,6},{1,7},{2,4},{3,5},{4,2},{5,3},{6,0},{7,1},{8,14},{9,15},{10,... | collective-permute-start | bytes 208904 | tf_op jit(solution)/shard_map/ppermute | solution.py:308
  9.2 0.4 collective-permute-start.2
  9.7 0.1 collective-permute-start.1
  9.8 2.0 %collective-permute-done.3.refs_3_ = f32[136,128]{1,0:T(8,128)S(1)} collective-permute-done((f32[136,128]{1,0:T(8,128)S(1)}, f32[136,128]{1,0:T(8,128)S(1)}, u32[]{:S(2)}, u32[]{:S(2)}) %collective-permute-start.3) | collective-permute-done | bytes 69664 | tf_op jit(solution)/shard_map/ppermute | solution.py:308
  11.7 1.8 %collective-permute-done.2.refs_2_ = f32[136,128]{1,0:T(8,128)S(1)} collective-permute-done((f32[136,128]{1,0:T(8,128)S(1)}, f32[136,128]{1,0:T(8,128)S(1)}, u32[]{:S(2)}, u32[]{:S(2)}) %collective-permute-start.2) | collective-permute-done | bytes 69664 | tf_op jit(solution)/shard_map/ppermute | solution.py:308
  13.5 0.4 collective-permute-done.1.refs_1_
  14.0 0.1 collective-permute-start.4
  14.1 0.0 collective-permute-done.5.refs_1_
  14.1 0.6 %shard_map.40 = (f32[16,64,128]{2,1,0:T(8,128)S(1)}, f32[3,64,128]{2,1,0:T(8,128)S(1)}) custom-call(f32[64,1024]{1,0:T(8,128)S(1)} %get-tuple-element.23.refs_0_, f32[64,1024]{1,0:T(8,128)S(1)} %collective-permute-done.5.refs_1_, bf16[8,384,128]{2,1,0:T(8,128)(2,1)S(1)} %get-tuple-element.21.refs_2_, f32[8,8,128]{2,1,0:T(8,128)S(1)} %get-tuple-element.22.refs_3_), custom_call_target="tpu_custom_call" | custom-call | flops 1000000000 | bytes 1000000 | tf_op jit(solution)/shard_map/pallas_call | solution.py:28
  14.7 0.9 %collective-permute-done.4.refs_1_ = f32[4,136,128]{2,1,0:T(8,128)S(1)} collective-permute-done((f32[4,136,128]{2,1,0:T(8,128)S(1)}, f32[4,136,128]{2,1,0:T(8,128)S(1)}, u32[]{:S(2)}, u32[]{:S(2)}) %collective-permute-start.4) | collective-permute-done | bytes 278560 | tf_op jit(solution)/shard_map/ppermute | solution.py:308
  15.6 1.2 %shard_map.41 = (f32[32,32,128]{2,1,0:T(8,128)S(1)}, bf16[16,384,128]{2,1,0:T(8,128)(2,1)S(1)}, f32[16,8,128]{2,1,0:T(8,128)S(1)}) custom-call(f32[4,136,128]{2,1,0:T(8,128)S(1)} %shard_map.38.refs_0_, f32[4,136,128]{2,1,0:T(8,128)S(1)} %collective-permute-done.4.refs_1_, bf16[8,384,128]{2,1,0:T(8,128)(2,1)S(1)} %get-tuple-element.21.refs_2_, ...), custom_call_target="tpu_custom_call" | custom-call | flops 301989888 | tf_op jit(solution)/shard_map/pallas_call | solution.py:28
  16.8 20.6 %all_to_all.5.moved = f32[32,32,128]{2,1,0:T(8,128)S(1)} all-to-all(f32[32,32,128]{2,1,0:T(8,128)S(1)} %get-tuple-element.27), channel_id=1, replica_groups=mesh['rows'=2,'cols'=16] {'rows','cols'}, dimensions={0} | all-to-all | bytes 1048576 | tf_op jit(solution)/shard_map/all_to_all | solution.py:373
  37.5 1.3 %shard_map.42 = (f32[64,1024]{1,0:T(8,128)S(1)}, f32[8,64,128]{2,1,0:T(8,128)S(1)}, f32[6,64,128]{2,1,0:T(8,128)S(1)}) custom-call(f32[32,32,128]{2,1,0:T(8,128)S(1)} %all_to_all.5.moved, bf16[16,384,128]{2,1,0:T(8,128)(2,1)S(1)} %get-tuple-element.28.ops, f32[16,8,128]{2,1,0:T(8,128)S(1)} %get-tuple-element.29.weights), custom_call_target="tpu_custom_call" | custom-call | flops 603979776 | tf_op jit(solution)/shard_map/pallas_call | solution.py:28
  38.8 1.1 %collective-permute-start.6 = (f32[64,1024]{1,0:T(8,128)S(1)}, f32[64,1024]{1,0:T(8,128)S(1)}, u32[]{:S(2)}, u32[]{:S(2)}) collective-permute-start(f32[64,1024]{1,0:T(8,128)S(1)} %get-tuple-element.32), channel_id=1, source_target_pairs={{0,16},{16,0},{1,17},{17,1},{2,18},{18,2},{3,19},{19,3},{4,20},{20... | collective-permute-start | bytes 786440 | tf_op jit(solution)/shard_map/ppermute | solution.py:305
  39.9 1.0 %shard_map.43.refs_0_ = f32[64,1024]{1,0:T(8,128)S(1)} custom-call(f32[8,64,128]{2,1,0:T(8,128)S(1)} %get-tuple-element.30.rest, f32[6,64,128]{2,1,0:T(8,128)S(1)} %get-tuple-element.31.edge, bf16[16,384,128]{2,1,0:T(8,128)(2,1)S(1)} %get-tuple-element.28.ops, f32[16,8,128]{2,1,0:T(8,128)S(1)} %get-tuple-element.29.weights), custom_call_target="tpu_custom_call" | custom-call | flops 301989888 | tf_op jit(solution)/shard_map/pallas_call | solution.py:28
  40.9 5.9 %collective-permute-done.6.refs_1_ = f32[64,1024]{1,0:T(8,128)S(1)} collective-permute-done((f32[64,1024]{1,0:T(8,128)S(1)}, f32[64,1024]{1,0:T(8,128)S(1)}, u32[]{:S(2)}, u32[]{:S(2)}) %collective-permute-start.6) | collective-permute-done | bytes 262176 | tf_op jit(solution)/shard_map/ppermute | solution.py:305
  46.7 1.0 %shard_map.44 = f32[1024,128]{1,0:T(8,128)} custom-call(f32[64,1024]{1,0:T(8,128)S(1)} %shard_map.43.refs_0_, f32[64,1024]{1,0:T(8,128)S(1)} %collective-permute-done.6.refs_1_), custom_call_target="tpu_custom_call" | custom-call | tf_op jit(solution)/shard_map/pallas_call | solution.py:403
  (1 shorter events, 0.0 us)
Async XLA Ops:
  0.9 5.3 %collective-permute-start = (f32[136,128]{1,0:T(8,128)S(1)}, f32[136,128]{1,0:T(8,128)S(1)}, u32[]{:S(2)}, u32[]{:S(2)}) collective-permute-start(f32[136,128]{1,0:T(8,128)S(1)} %get-tuple-element.19), channel_id=1, source_target_pairs={{0,16},{16,0},{1,17},{17,1},{2,18},{18,2},{3,19},{19,3},{4,20},{20... | collective-permute-start | bytes 208904 | tf_op jit(solution)/shard_map/ppermute | solution.py:305
  5.5 8.5 %collective-permute-start.5 = (f32[64,1024]{1,0:T(8,128)S(1)}, f32[64,1024]{1,0:T(8,128)S(1)}, u32[]{:S(2)}, u32[]{:S(2)}) collective-permute-start(f32[64,1024]{1,0:T(8,128)S(1)} %get-tuple-element.24), channel_id=1, source_target_pairs={{0,16},{16,0},{1,17},{17,1},{2,18},{18,2},{3,19},{19,3},{4,20},{20... | collective-permute-start | bytes 786440 | tf_op jit(solution)/shard_map/ppermute | solution.py:305
  6.2 5.5 %collective-permute-start.3 = (f32[136,128]{1,0:T(8,128)S(1)}, f32[136,128]{1,0:T(8,128)S(1)}, u32[]{:S(2)}, u32[]{:S(2)}) collective-permute-start(f32[136,128]{1,0:T(8,128)S(1)} %collective-permute-done.refs_0_), channel_id=1, source_target_pairs={{0,6},{1,7},{2,4},{3,5},{4,2},{5,3},{6,0},{7,1},{8,14},{9,15},{10,... | collective-permute-start | bytes 208904 | tf_op jit(solution)/shard_map/ppermute | solution.py:308
  9.2 4.3 %collective-permute-start.2 = (f32[136,128]{1,0:T(8,128)S(1)}, f32[136,128]{1,0:T(8,128)S(1)}, u32[]{:S(2)}, u32[]{:S(2)}) collective-permute-start(f32[136,128]{1,0:T(8,128)S(1)} %collective-permute-done.refs_0_), channel_id=1, source_target_pairs={{0,4},{1,5},{2,6},{3,7},{4,0},{5,1},{6,2},{7,3},{8,12},{9,13},{10,... | collective-permute-start | bytes 208904 | tf_op jit(solution)/shard_map/ppermute | solution.py:308
  9.7 4.3 %collective-permute-start.1 = (f32[136,128]{1,0:T(8,128)S(1)}, f32[136,128]{1,0:T(8,128)S(1)}, u32[]{:S(2)}, u32[]{:S(2)}) collective-permute-start(f32[136,128]{1,0:T(8,128)S(1)} %collective-permute-done.refs_0_), channel_id=1, source_target_pairs={{0,2},{1,3},{2,0},{3,1},{4,6},{5,7},{6,4},{7,5},{8,10},{9,11},{10,... | collective-permute-start | bytes 208904 | tf_op jit(solution)/shard_map/ppermute | solution.py:308
  14.0 1.6 %collective-permute-start.4 = (f32[4,136,128]{2,1,0:T(8,128)S(1)}, f32[4,136,128]{2,1,0:T(8,128)S(1)}, u32[]{:S(2)}, u32[]{:S(2)}) collective-permute-start(f32[4,136,128]{2,1,0:T(8,128)S(1)} %shard_map.38.refs_0_), channel_id=1, source_target_pairs={{0,1},{1,0},{2,3},{3,2},{4,5},{5,4},{6,7},{7,6},{8,9},{9,8},{10,11... | collective-permute-start | bytes 835592 | tf_op jit(solution)/shard_map/ppermute | solution.py:308
  38.8 7.9 %collective-permute-start.6 = (f32[64,1024]{1,0:T(8,128)S(1)}, f32[64,1024]{1,0:T(8,128)S(1)}, u32[]{:S(2)}, u32[]{:S(2)}) collective-permute-start(f32[64,1024]{1,0:T(8,128)S(1)} %get-tuple-element.32), channel_id=1, source_target_pairs={{0,16},{16,0},{1,17},{17,1},{2,18},{18,2},{3,19},{19,3},{4,20},{20... | collective-permute-start | bytes 786440 | tf_op jit(solution)/shard_map/ppermute | solution.py:305

commit v4 on v3

--- a/solution.py
+++ b/solution.py
@@ -215,16 +215,8 @@
             )
 
 
-def second_kernel(pieces, cols, lat_rows, moved, ops, weights, *refs):
-    lats, lons = ops.shape[0], ops.shape[2]
-    count = STEPS + LAGS
-    me = lax.axis_index("rows")
-    outs = refs[: pieces - 1]
-    if pieces == 2:
-        rest, edge, state = refs[1:]
-    else:
-        rest, state = refs[pieces - 1 :]
-    width = state.shape[1]
+def unpack(pieces, cols, moved, state):
+    lats, width, lons = state.shape
     fold = lons // width
     short = width // fold
     for at in range(lats):
@@ -237,56 +229,90 @@
             state[at, i * short : (i + 1) * short, :] = jnp.concatenate(
                 [block[:, i * width : (i + 1) * width] for block in got], axis=1
             )
+
+
+def second_kernel(pieces, cols, lat_rows, moved, ops, weights, *refs):
+    *outs, state = refs
+    lons = ops.shape[2]
+    me = lax.axis_index("rows")
+    unpack(pieces, cols, moved, state)
+    steps(state, ops, weights, STEPS + LAGS)
+    for partner in range(pieces):
+        for lat in range(lat_rows):
+            outs[partner][:, lat * lons : (lat + 1) * lons] = state[(me ^ partner) * lat_rows + lat]
+
+
+def stage_kernel(cols, low, high, groups, *refs):
+    count = STEPS + LAGS
+    state = refs[-1]
+    lats, width, lons = state.shape
+    if low == 0:
+        moved, ops, weights = refs[:3]
+        outs = refs[3:-1]
+        unpack(2, cols, moved, state)
+    else:
+        rest, edge, ops, weights = refs[:4]
+        outs = refs[4:-1]
+        for at in range(low, lats):
+            state[at] = rest[at - low]
+    for step in range(count):
+        further = count - 1 - step
+        first = low + further if low else 0
+        last = min(lats, high + further) if high < lats else lats
+        if first < last:
+            before = advance(state, ops, weights, first, last, edge[step] if low else None)
+            if high < lats:
+                outs[-1][step] = before
+    if high < lats:
+        for at in range(high, lats):
+            outs[-2][at - high] = state[at]
+    flipped = place(2, lats, 0) != 0
+    for out, (start, stop) in zip(outs, groups):
+        for i in range(stop - start):
+            out[:, i * lons : (i + 1) * lons] = state[jnp.where(flipped, stop - 1 - i, start + i)]
+
+
+def join_kernel(pieces, lons, start, stop, *refs):
+    stack, held, sems = refs[-3:]
+    blocks, out = refs[:pieces], refs[-4]
+    me = lax.axis_index("rows")
+    base = 0
     if pieces == 2:
-        for step in range(count):
-            last = min(lats, lat_rows + count - 1 - step)
-            edge[step] = advance(state, ops, weights, 0, last, None)
-        for at in range(lat_rows, lats):
-            rest[at - lat_rows] = state[at]
-    else:
-        steps(state, ops, weights, count)
-        for lat in range(lat_rows):
-            rest[:, lat * lons : (lat + 1) * lons] = state[me * lat_rows + lat]
-    for partner in range(1, pieces):
-        for lat in range(lat_rows):
-            at = place(pieces, lats, (me ^ partner) * lat_rows + lat)
-            outs[partner - 1][:, lat * lons : (lat + 1) * lons] = state[at]
-
-
-def rest_kernel(rest, edge, ops, weights, out, state):
-    lat_rows = rest.shape[0]
-    lats, lons = ops.shape[0], ops.shape[2]
-    count = STEPS + LAGS
-    me = lax.axis_index("rows")
-    for at in range(lat_rows):
-        state[lat_rows + at] = rest[at]
-    for step in range(count):
-        first = min(lats, lat_rows + count - 1 - step)
-        if first < lats:
-            advance(state, ops, weights, first, lats, edge[step])
-    for lat in range(lat_rows):
-        out[:, lat * lons : (lat + 1) * lons] = state[place(2, lats, me * lat_rows + lat)]
-
-
-def join_kernel(pieces, *refs):
-    blocks, out, stack, held, sems = refs[:pieces], *refs[pieces:]
-    me = lax.axis_index("rows")
-    width, tall = blocks[0].shape
-    chunk = min(tall, 128)
+        lat_rows = out.shape[0] // lons
+        base = pl.multiple_of(jnp.where(me == 0, start, lat_rows - stop) * lons, lons)
     for partner in range(pieces):
         stack[me ^ partner] = blocks[partner][...]
     copies = []
-    for first in range(0, tall, chunk):
-        rows = jnp.concatenate([stack[i, :, first : first + chunk] for i in range(pieces)], axis=0)
-        held[first : first + chunk, :] = rows.T
+    for at in range(stop - start):
+        first = at * lons
+        rows = jnp.concatenate([stack[i, :, first : first + lons] for i in range(pieces)], axis=0)
+        held[first : first + lons, :] = rows.T
         copies.append(
             pltpu.make_async_copy(
-                held.at[pl.ds(first, chunk)], out.at[pl.ds(first, chunk)], sems.at[first // chunk]
+                held.at[pl.ds(first, lons)], out.at[pl.ds(base + first, lons)], sems.at[at]
             )
         )
         copies[-1].start()
     for copy in copies:
         copy.wait()
+
+
+def join(pieces, lons, start, stop, shape, blocks, given=None):
+    width = blocks[0].shape[0]
+    size = stop - start
+    return pl.pallas_call(
+        functools.partial(join_kernel, pieces, lons, start, stop),
+        out_shape=jax.ShapeDtypeStruct(shape, F32),
+        in_specs=[VMEM] * pieces + ([] if given is None else [HBM]),
+        out_specs=HBM,
+        scratch_shapes=[
+            pltpu.VMEM((pieces, width, size * lons), F32),
+            pltpu.VMEM((size * lons, shape[1]), F32),
+            pltpu.SemaphoreType.DMA((size,)),
+        ],
+        input_output_aliases={} if given is None else {pieces: 0},
+        compiler_params=pltpu.CompilerParams(vmem_limit_bytes=LIMIT),
+    )(*blocks, *([] if given is None else [given]))
 
 
 def on_device(covariance, zonal, stencil):
@@ -371,47 +397,49 @@
         flops=STEPS * lats * lons * lons * width * 6,
     )
     moved = lax.all_to_all(sent, ("rows", "cols"), 0, 0, tiled=True)
-    if pieces == 2:
-        end, rest, edge = call(
-            functools.partial(second_kernel, pieces, cols, lat_rows),
-            [
-                strip,
-                jax.ShapeDtypeStruct((lat_rows, width, lons), F32),
-                jax.ShapeDtypeStruct((STEPS + LAGS, width, lons), F32),
-            ],
-            (moved, ops, weights),
-            [state],
-            flops=(STEPS + LAGS) * lats * lons * lons * width * 6,
-        )
-        ends = [end]
-        mine = call(
-            rest_kernel,
-            strip,
-            (rest, edge, ops, weights),
-            [state],
-            flops=(STEPS + LAGS) * lat_rows * lons * lons * width * 6,
-        )
-    else:
-        *ends, mine = call(
+    if pieces != 2:
+        mine, *ends = call(
             functools.partial(second_kernel, pieces, cols, lat_rows),
             [strip] * pieces,
             (moved, ops, weights),
             [state],
             flops=(STEPS + LAGS) * lats * lons * lons * width * 6,
         )
-    blocks = [mine] + [row_swap(ends[partner - 1], partner) for partner in range(1, pieces)]
-    return pl.pallas_call(
-        functools.partial(join_kernel, pieces),
-        out_shape=jax.ShapeDtypeStruct((tall, wide), F32),
-        in_specs=[VMEM] * pieces,
-        out_specs=HBM,
-        scratch_shapes=[
-            pltpu.VMEM((pieces, width, tall), F32),
-            pltpu.VMEM((tall, wide), F32),
-            pltpu.SemaphoreType.DMA((chunks,)),
-        ],
-        compiler_params=pltpu.CompilerParams(vmem_limit_bytes=LIMIT),
-    )(*blocks)
+        blocks = [mine] + [row_swap(ends[partner - 1], partner) for partner in range(1, pieces)]
+        return join(pieces, lons, 0, lat_rows, (tall, wide), blocks)
+
+    def group(start, stop):
+        return jax.ShapeDtypeStruct((width, (stop - start) * lons), F32)
+
+    cuts = [0, lat_rows // 2, lat_rows] if lat_rows % 2 == 0 else [0, lat_rows]
+    given = (moved,)
+    got = []
+    for low, high in zip(cuts, cuts[1:]):
+        end, rest, edge = call(
+            functools.partial(stage_kernel, cols, low, high, ((low, high),)),
+            [
+                group(low, high),
+                jax.ShapeDtypeStruct((lats - high, width, lons), F32),
+                jax.ShapeDtypeStruct((STEPS + LAGS, width, lons), F32),
+            ],
+            (*given, ops, weights),
+            [state],
+            flops=10**7,
+        )
+        got.append(row_swap(end, 1))
+        given = (rest, edge)
+    mirror = [(lats - high, lats - low) for low, high in zip(cuts, cuts[1:])]
+    mine = call(
+        functools.partial(stage_kernel, cols, lat_rows, lats, mirror),
+        [group(*span) for span in mirror],
+        (*given, ops, weights),
+        [state],
+        flops=10**7,
+    )
+    out = None
+    for low, high, own, other in zip(cuts, cuts[1:], mine, got):
+        out = join(2, lons, low, high, (tall, wide), [own, other], out)
+    return out
 
 
 def solution(mesh):

time: 48 us -> 47.6 us (level)
  waiting for transfers between devices: 11.5 us -> 8.72 us
  Pallas kernels: 7.66 us -> 8.99 us
  starting transfers between devices: 7.83 us -> 8.91 us
    ppermute x3 -> x4, waiting for transfers between devices: 6.44 us -> 3.61 us  [row_swap(): lax.ppermute(value, 'rows', [(i, i ^ partner) for i in range(pieces)])]
    ppermute x3 -> x4, starting transfers between devices: 4.18 us -> 5.27 us  [row_swap(): lax.ppermute(value, 'rows', [(i, i ^ partner) for i in range(pieces)])]
    pallas_call x1 -> x2, Pallas kernels: 0.99 us -> 1.71 us  [join(): pl.pallas_call(functools.partial(join_kernel, pieces, lons, start, stop),...]
    pallas_call x7 -> x8, Pallas kernels: 6.66 us -> 7.28 us  [call(): pl.pallas_call(kernel, out_shape=out_shape, in_specs=specs or [VMEM] * le...]
  transfers between devices with their start and end apart: 7 -> 8, of which waited for: 6 -> 7; matrix products, arithmetic and copies ran while one was open for 0% -> 0% of each run, Pallas kernels for 7% -> 10%
where the time goes in v4:
time: 47.6 us; the launch traced here: 47.3 us
  blocking collectives  20.6 us (43%)
  Pallas kernels  8.99 us (19%)
  starting transfers between devices  8.91 us (19%)
  waiting for transfers between devices  8.72 us (18%)
    all_to_all x1, blocking collectives, on_device(): moved = lax.all_to_all(sent, ('rows', 'cols'), 0, 0, tiled=True)  20.6 us
    pallas_call x8, Pallas kernels, call(): pl.pallas_call(kernel, out_shape=out_shape, in_specs=specs or [VMEM] * le...  7.28 us
    ppermute x4, starting transfers between devices, row_swap(): lax.ppermute(value, 'rows', [(i, i ^ partner) for i in range(pieces)])  5.27 us
    ppermute x4, waiting for transfers between devices, col_swap(): return lax.ppermute(value, 'cols', [(i, i ^ partner) for i in range(cols)])  5.11 us
    ppermute x4, starting transfers between devices, col_swap(): return lax.ppermute(value, 'cols', [(i, i ^ partner) for i in range(cols)])  3.64 us
    ppermute x4, waiting for transfers between devices, row_swap(): lax.ppermute(value, 'rows', [(i, i ^ partner) for i in range(pieces)])  3.61 us
    pallas_call x2, Pallas kernels, join(): pl.pallas_call(functools.partial(join_kernel, pieces, lons, start, stop),...  1.71 us
  transfers between devices with their start and end apart: 8, of which 7 were waited for; matrix products, arithmetic and copies ran while one was open for 0% of the time, Pallas kernels for 10%

profile of v4, /device:TPU:0, one launch (start us, length us, event | category | flops | bytes accessed | tf_op | source)
XLA Modules:
  0.0 47.3 jit_solution(15200359452428488490)
XLA Ops:
  0.0 0.9 %shard_map.37 = (f32[136,128]{1,0:T(8,128)S(1)}, f32[3,8,128]{2,1,0:T(8,128)S(1)}) custom-call(f32[8,128,128]{2,1,0:T(8,128)} %zonal.3, f32[3,8,128]{2,1,0:T(8,128)} %bitcast.1), custom_call_target="tpu_custom_call" | custom-call | bytes 100000 | tf_op jit(solution)/shard_map/pallas_call | solution.py:28
  0.9 3.0 %collective-permute-start = (f32[136,128]{1,0:T(8,128)S(1)}, f32[136,128]{1,0:T(8,128)S(1)}, u32[]{:S(2)}, u32[]{:S(2)}) collective-permute-start(f32[136,128]{1,0:T(8,128)S(1)} %get-tuple-element.24), channel_id=1, source_target_pairs={{0,16},{16,0},{1,17},{17,1},{2,18},{18,2},{3,19},{19,3},{4,20},{20... | collective-permute-start | bytes 208904 | tf_op jit(solution)/shard_map/ppermute | solution.py:331
  3.9 1.6 %shard_map.39 = (f32[64,1024]{1,0:T(8,128)S(1)}, f32[64,1024]{1,0:T(8,128)S(1)}, bf16[8,384,128]{2,1,0:T(8,128)(2,1)S(1)}, f32[8,8,128]{2,1,0:T(8,128)S(1)}) custom-call(f32[1024,128]{1,0:T(8,128)} %block.1, f32[8,128,128]{2,1,0:T(8,128)} %zonal.3, f32[3,8,128]{2,1,0:T(8,128)S(1)} %get-tuple-element.25.stencil), custom_call_target="tpu_custom_call" | custom-call | bytes 1048576 | tf_op jit(solution)/shard_map/pallas_call | solution.py:28
  5.5 0.1 collective-permute-start.5
  5.6 0.6 %collective-permute-done.refs_0_ = f32[136,128]{1,0:T(8,128)S(1)} collective-permute-done((f32[136,128]{1,0:T(8,128)S(1)}, f32[136,128]{1,0:T(8,128)S(1)}, u32[]{:S(2)}, u32[]{:S(2)}) %collective-permute-start) | collective-permute-done | bytes 69664 | tf_op jit(solution)/shard_map/ppermute | solution.py:331
  6.2 3.0 %collective-permute-start.3 = (f32[136,128]{1,0:T(8,128)S(1)}, f32[136,128]{1,0:T(8,128)S(1)}, u32[]{:S(2)}, u32[]{:S(2)}) collective-permute-start(f32[136,128]{1,0:T(8,128)S(1)} %collective-permute-done.refs_0_), channel_id=1, source_target_pairs={{0,6},{1,7},{2,4},{3,5},{4,2},{5,3},{6,0},{7,1},{8,14},{9,15},{10,... | collective-permute-start | bytes 208904 | tf_op jit(solution)/shard_map/ppermute | solution.py:334
  9.2 0.4 collective-permute-start.2
  9.7 0.1 collective-permute-start.1
  9.8 2.0 %collective-permute-done.3.refs_3_ = f32[136,128]{1,0:T(8,128)S(1)} collective-permute-done((f32[136,128]{1,0:T(8,128)S(1)}, f32[136,128]{1,0:T(8,128)S(1)}, u32[]{:S(2)}, u32[]{:S(2)}) %collective-permute-start.3) | collective-permute-done | bytes 69664 | tf_op jit(solution)/shard_map/ppermute | solution.py:334
  11.7 1.8 %collective-permute-done.2.refs_2_ = f32[136,128]{1,0:T(8,128)S(1)} collective-permute-done((f32[136,128]{1,0:T(8,128)S(1)}, f32[136,128]{1,0:T(8,128)S(1)}, u32[]{:S(2)}, u32[]{:S(2)}) %collective-permute-start.2) | collective-permute-done | bytes 69664 | tf_op jit(solution)/shard_map/ppermute | solution.py:334
  13.5 0.4 collective-permute-done.1.refs_1_
  14.0 0.1 collective-permute-start.4
  14.1 0.0 collective-permute-done.5.refs_1_
  14.1 0.6 %shard_map.40 = (f32[16,64,128]{2,1,0:T(8,128)S(1)}, f32[3,64,128]{2,1,0:T(8,128)S(1)}) custom-call(f32[64,1024]{1,0:T(8,128)S(1)} %get-tuple-element.28.refs_0_, f32[64,1024]{1,0:T(8,128)S(1)} %collective-permute-done.5.refs_1_, bf16[8,384,128]{2,1,0:T(8,128)(2,1)S(1)} %get-tuple-element.26.refs_2_, f32[8,8,128]{2,1,0:T(8,128)S(1)} %get-tuple-element.27.refs_3_), custom_call_target="tpu_custom_call" | custom-call | flops 1000000000 | bytes 1000000 | tf_op jit(solution)/shard_map/pallas_call | solution.py:28
  14.7 0.9 %collective-permute-done.4.refs_1_ = f32[4,136,128]{2,1,0:T(8,128)S(1)} collective-permute-done((f32[4,136,128]{2,1,0:T(8,128)S(1)}, f32[4,136,128]{2,1,0:T(8,128)S(1)}, u32[]{:S(2)}, u32[]{:S(2)}) %collective-permute-start.4) | collective-permute-done | bytes 278560 | tf_op jit(solution)/shard_map/ppermute | solution.py:334
  15.6 1.2 %shard_map.41 = (f32[32,32,128]{2,1,0:T(8,128)S(1)}, bf16[16,384,128]{2,1,0:T(8,128)(2,1)S(1)}, f32[16,8,128]{2,1,0:T(8,128)S(1)}) custom-call(f32[4,136,128]{2,1,0:T(8,128)S(1)} %shard_map.38.refs_0_, f32[4,136,128]{2,1,0:T(8,128)S(1)} %collective-permute-done.4.refs_1_, bf16[8,384,128]{2,1,0:T(8,128)(2,1)S(1)} %get-tuple-element.26.refs_2_, ...), custom_call_target="tpu_custom_call" | custom-call | flops 301989888 | tf_op jit(solution)/shard_map/pallas_call | solution.py:28
  16.8 20.6 %all_to_all.5.refs_0_ = f32[32,32,128]{2,1,0:T(8,128)S(1)} all-to-all(f32[32,32,128]{2,1,0:T(8,128)S(1)} %get-tuple-element.32), channel_id=1, replica_groups=mesh['rows'=2,'cols'=16] {'rows','cols'}, dimensions={0} | all-to-all | bytes 1048576 | tf_op jit(solution)/shard_map/all_to_all | solution.py:399
  37.5 1.1 %shard_map.42 = (f32[64,512]{1,0:T(8,128)S(1)}, f32[12,64,128]{2,1,0:T(8,128)S(1)}, f32[6,64,128]{2,1,0:T(8,128)S(1)}) custom-call(f32[32,32,128]{2,1,0:T(8,128)S(1)} %all_to_all.5.refs_0_, bf16[16,384,128]{2,1,0:T(8,128)(2,1)S(1)} %get-tuple-element.33.refs_1_.refs_2_, f32[16,8,128]{2,1,0:T(8,128)S(1)} %get-tuple-element.34.refs_2_.refs_3_), custom_call_target="tpu_custom_call" | custom-call | flops 10000000 | tf_op jit(solution)/shard_map/pallas_call | solution.py:28
  38.6 1.1 %collective-permute-start.7 = (f32[64,512]{1,0:T(8,128)S(1)}, f32[64,512]{1,0:T(8,128)S(1)}, u32[]{:S(2)}, u32[]{:S(2)}) collective-permute-start(f32[64,512]{1,0:T(8,128)S(1)} %get-tuple-element.42), channel_id=1, source_target_pairs={{0,16},{16,0},{1,17},{17,1},{2,18},{18,2},{3,19},{19,3},{4,20},{20... | collective-permute-start | bytes 393224 | tf_op jit(solution)/shard_map/ppermute | solution.py:331
  39.6 0.9 %shard_map.43 = (f32[64,512]{1,0:T(8,128)S(1)}, f32[8,64,128]{2,1,0:T(8,128)S(1)}, f32[6,64,128]{2,1,0:T(8,128)S(1)}) custom-call(f32[12,64,128]{2,1,0:T(8,128)S(1)} %get-tuple-element.35.refs_0_, f32[6,64,128]{2,1,0:T(8,128)S(1)} %get-tuple-element.36.refs_1_, bf16[16,384,128]{2,1,0:T(8,128)(2,1)S(1)} %get-tuple-element.33.refs_1_.refs_2_, ...), custom_call_target="tpu_custom_call" | custom-call | flops 10000000 | tf_op jit(solution)/shard_map/pallas_call | solution.py:28
  40.5 1.1 %collective-permute-start.6 = (f32[64,512]{1,0:T(8,128)S(1)}, f32[64,512]{1,0:T(8,128)S(1)}, u32[]{:S(2)}, u32[]{:S(2)}) collective-permute-start(f32[64,512]{1,0:T(8,128)S(1)} %get-tuple-element.40), channel_id=1, source_target_pairs={{0,16},{16,0},{1,17},{17,1},{2,18},{18,2},{3,19},{19,3},{4,20},{20... | collective-permute-start | bytes 393224 | tf_op jit(solution)/shard_map/ppermute | solution.py:331
  41.6 1.0 %shard_map.44 = (f32[64,512]{1,0:T(8,128)S(1)}, f32[64,512]{1,0:T(8,128)S(1)}) custom-call(f32[8,64,128]{2,1,0:T(8,128)S(1)} %get-tuple-element.37.refs_0_, f32[6,64,128]{2,1,0:T(8,128)S(1)} %get-tuple-element.38.refs_1_, bf16[16,384,128]{2,1,0:T(8,128)(2,1)S(1)} %get-tuple-element.33.refs_1_.refs_2_, f32[16,8,128]{2,1,0:T(8,128)S(1)} %get-tuple-element.34.refs_2_.refs_3_), custom_call_target="tpu_custom_call" | custom-call | flops 10000000 | tf_op jit(solution)/shard_map/pallas_call | solution.py:28
  42.6 1.9 %collective-permute-done.7.refs_1_ = f32[64,512]{1,0:T(8,128)S(1)} collective-permute-done((f32[64,512]{1,0:T(8,128)S(1)}, f32[64,512]{1,0:T(8,128)S(1)}, u32[]{:S(2)}, u32[]{:S(2)}) %collective-permute-start.7) | collective-permute-done | bytes 131104 | tf_op jit(solution)/shard_map/ppermute | solution.py:331
  44.5 0.9 %shard_map.45.refs_2_ = f32[1024,128]{1,0:T(8,128)} custom-call(f32[64,512]{1,0:T(8,128)S(1)} %get-tuple-element.41.refs_0_, f32[64,512]{1,0:T(8,128)S(1)} %collective-permute-done.7.refs_1_), custom_call_target="tpu_custom_call" | custom-call | tf_op jit(solution)/shard_map/pallas_call | solution.py:303
  45.3 1.2 %collective-permute-done.6.refs_1_ = f32[64,512]{1,0:T(8,128)S(1)} collective-permute-done((f32[64,512]{1,0:T(8,128)S(1)}, f32[64,512]{1,0:T(8,128)S(1)}, u32[]{:S(2)}, u32[]{:S(2)}) %collective-permute-start.6) | collective-permute-done | bytes 131104 | tf_op jit(solution)/shard_map/ppermute | solution.py:331
  46.5 0.9 %shard_map.46 = f32[1024,128]{1,0:T(8,128)} custom-call(f32[64,512]{1,0:T(8,128)S(1)} %get-tuple-element.39.refs_0_, f32[64,512]{1,0:T(8,128)S(1)} %collective-permute-done.6.refs_1_, f32[1024,128]{1,0:T(8,128)} %shard_map.45.refs_2_), custom_call_target="tpu_custom_call", output_to_operand_aliasing={{}: (2, {})} | custom-call | tf_op jit(solution)/shard_map/pallas_call | solution.py:303
  (1 shorter events, 0.0 us)
Async XLA Ops:
  0.9 5.3 %collective-permute-start = (f32[136,128]{1,0:T(8,128)S(1)}, f32[136,128]{1,0:T(8,128)S(1)}, u32[]{:S(2)}, u32[]{:S(2)}) collective-permute-start(f32[136,128]{1,0:T(8,128)S(1)} %get-tuple-element.24), channel_id=1, source_target_pairs={{0,16},{16,0},{1,17},{17,1},{2,18},{18,2},{3,19},{19,3},{4,20},{20... | collective-permute-start | bytes 208904 | tf_op jit(solution)/shard_map/ppermute | solution.py:331
  5.5 8.5 %collective-permute-start.5 = (f32[64,1024]{1,0:T(8,128)S(1)}, f32[64,1024]{1,0:T(8,128)S(1)}, u32[]{:S(2)}, u32[]{:S(2)}) collective-permute-start(f32[64,1024]{1,0:T(8,128)S(1)} %get-tuple-element.29), channel_id=1, source_target_pairs={{0,16},{16,0},{1,17},{17,1},{2,18},{18,2},{3,19},{19,3},{4,20},{20... | collective-permute-start | bytes 786440 | tf_op jit(solution)/shard_map/ppermute | solution.py:331
  6.2 5.5 %collective-permute-start.3 = (f32[136,128]{1,0:T(8,128)S(1)}, f32[136,128]{1,0:T(8,128)S(1)}, u32[]{:S(2)}, u32[]{:S(2)}) collective-permute-start(f32[136,128]{1,0:T(8,128)S(1)} %collective-permute-done.refs_0_), channel_id=1, source_target_pairs={{0,6},{1,7},{2,4},{3,5},{4,2},{5,3},{6,0},{7,1},{8,14},{9,15},{10,... | collective-permute-start | bytes 208904 | tf_op jit(solution)/shard_map/ppermute | solution.py:334
  9.2 4.3 %collective-permute-start.2 = (f32[136,128]{1,0:T(8,128)S(1)}, f32[136,128]{1,0:T(8,128)S(1)}, u32[]{:S(2)}, u32[]{:S(2)}) collective-permute-start(f32[136,128]{1,0:T(8,128)S(1)} %collective-permute-done.refs_0_), channel_id=1, source_target_pairs={{0,4},{1,5},{2,6},{3,7},{4,0},{5,1},{6,2},{7,3},{8,12},{9,13},{10,... | collective-permute-start | bytes 208904 | tf_op jit(solution)/shard_map/ppermute | solution.py:334
  9.7 4.3 %collective-permute-start.1 = (f32[136,128]{1,0:T(8,128)S(1)}, f32[136,128]{1,0:T(8,128)S(1)}, u32[]{:S(2)}, u32[]{:S(2)}) collective-permute-start(f32[136,128]{1,0:T(8,128)S(1)} %collective-permute-done.refs_0_), channel_id=1, source_target_pairs={{0,2},{1,3},{2,0},{3,1},{4,6},{5,7},{6,4},{7,5},{8,10},{9,11},{10,... | collective-permute-start | bytes 208904 | tf_op jit(solution)/shard_map/ppermute | solution.py:334
  14.0 1.6 %collective-permute-start.4 = (f32[4,136,128]{2,1,0:T(8,128)S(1)}, f32[4,136,128]{2,1,0:T(8,128)S(1)}, u32[]{:S(2)}, u32[]{:S(2)}) collective-permute-start(f32[4,136,128]{2,1,0:T(8,128)S(1)} %shard_map.38.refs_0_), channel_id=1, source_target_pairs={{0,1},{1,0},{2,3},{3,2},{4,5},{5,4},{6,7},{7,6},{8,9},{9,8},{10,11... | collective-permute-start | bytes 835592 | tf_op jit(solution)/shard_map/ppermute | solution.py:334
  38.6 5.9 %collective-permute-start.7 = (f32[64,512]{1,0:T(8,128)S(1)}, f32[64,512]{1,0:T(8,128)S(1)}, u32[]{:S(2)}, u32[]{:S(2)}) collective-permute-start(f32[64,512]{1,0:T(8,128)S(1)} %get-tuple-element.42), channel_id=1, source_target_pairs={{0,16},{16,0},{1,17},{17,1},{2,18},{18,2},{3,19},{19,3},{4,20},{20... | collective-permute-start | bytes 393224 | tf_op jit(solution)/shard_map/ppermute | solution.py:331
  40.5 6.0 %collective-permute-start.6 = (f32[64,512]{1,0:T(8,128)S(1)}, f32[64,512]{1,0:T(8,128)S(1)}, u32[]{:S(2)}, u32[]{:S(2)}) collective-permute-start(f32[64,512]{1,0:T(8,128)S(1)} %get-tuple-element.40), channel_id=1, source_target_pairs={{0,16},{16,0},{1,17},{17,1},{2,18},{18,2},{3,19},{19,3},{4,20},{20... | collective-permute-start | bytes 393224 | tf_op jit(solution)/shard_map/ppermute | solution.py:331

commit v5 on v4

--- a/solution.py
+++ b/solution.py
@@ -13,7 +13,8 @@
 HBM = pl.BlockSpec(memory_space=pltpu.HBM)
 LIMIT = 32 * 1024 * 1024
 F32 = jnp.float32
-FLOPS = 10**9
+FLOPS = 5 * 10**8
+LATE = 10**9
 BF16 = jnp.bfloat16
 
 
@@ -81,14 +82,17 @@
         copy.wait()
 
 
-def merge_kernel(*refs):
+def merge_kernel(count, *refs):
     *packets, out = refs
-    for i, packet in enumerate(packets):
-        out[i] = packet[...]
-
-
-def put(ops, weights, at, flipped, matrix, coeffs):
-    high, low = split(matrix.T)
+    lons = out.shape[2]
+    for at, packet in enumerate(packets):
+        for i in range(count):
+            out[at, i * lons : (i + 1) * lons, :] = packet[i * lons : (i + 1) * lons, :].T
+        out[at, count * lons :, :] = packet[count * lons :, :]
+
+
+def put(ops, weights, at, flipped, turned, coeffs):
+    high, low = split(turned)
     ops[at] = jnp.concatenate([high, high, low], axis=0)
     own, north, south = coeffs
     weights[at, 0:1, :] = own
@@ -143,7 +147,7 @@
     for lat in range(lat_rows):
         coeffs = [stencil[k, lat : lat + 1, :] for k in range(3)]
         at = place(2, lats, me * lat_rows + lat) - lat_rows if pieces == 2 else lat
-        put(ops, weights, at, flipped, matrices[lat], coeffs)
+        put(ops, weights, at, flipped, matrices[lat].T, coeffs)
 
 
 def load_kernel(pieces, lat_rows, *refs):
@@ -166,7 +170,7 @@
 
 
 def first_kernel(pieces, cols, hops, *refs):
-    n_packets = 2 * (pieces - 1)
+    n_packets = (2 if len(hops) == 1 else 4) * (pieces - 1)
     packets = refs[:n_packets]
     own_ops, own_weights, given = refs[n_packets : n_packets + 3]
     out, ops, weights, state = refs[-4:]
@@ -181,16 +185,19 @@
         at = lat_rows + lat if pieces == 2 else me * lat_rows + lat
         ops[at] = own_ops[lat]
         weights[at] = own_weights[lat]
+    early = hops[:1] + hops[2:]
+    late = hops[1:2]
     for partner in range(1, pieces):
-        for core in range(2):
-            packet = packets[2 * (partner - 1) + core]
-            for at, hop in enumerate(hops):
-                for i in range(count):
-                    lat = (me ^ partner) * lat_rows + (part ^ hop ^ core) * count + i
-                    row = count * lons + 3 * i
-                    coeffs = [packet[at, row + k : row + k + 1, :] for k in range(3)]
-                    matrix = packet[at, i * lons : (i + 1) * lons, :]
-                    put(ops, weights, place(pieces, lats, lat), flipped, matrix, coeffs)
+        for group, of_group in enumerate([early, late] if late else [early]):
+            for core in range(2):
+                packet = packets[(n_packets // (pieces - 1)) * (partner - 1) + 2 * group + core]
+                for at, hop in enumerate(of_group):
+                    for i in range(count):
+                        lat = (me ^ partner) * lat_rows + (part ^ hop ^ core) * count + i
+                        row = count * lons + 3 * i
+                        coeffs = [packet[at, row + k : row + k + 1, :] for k in range(3)]
+                        turned = packet[at, i * lons : (i + 1) * lons, :]
+                        put(ops, weights, place(pieces, lats, lat), flipped, turned, coeffs)
     for at in range(lats):
         state[at] = given[at]
     if pieces == 2:
@@ -369,13 +376,17 @@
     blocks = [cut[0]]
     for partner in range(1, pieces):
         direct = row_swap(packet, partner)
-        merged = call(
-            merge_kernel,
-            jax.ShapeDtypeStruct((len(hops), rows, lons), F32),
-            [direct] + [col_swap(direct, hop) for hop in hops[1:]],
-            moved=10**5,
-        )
-        packets += [merged, col_swap(merged, 1)]
+        across = [col_swap(direct, hop) for hop in hops[1:]]
+        for group, flops in (([direct] + across[1:], 0), (across[:1], LATE)):
+            if group:
+                merged = call(
+                    functools.partial(merge_kernel, count),
+                    jax.ShapeDtypeStruct((len(group), rows, lons), F32),
+                    group,
+                    flops=flops,
+                    moved=10**5,
+                )
+                packets += [merged, col_swap(merged, 1)]
         blocks.append(row_swap(cut[partner], partner))
     states = [jax.ShapeDtypeStruct((lats, width, lons), F32)]
     own = [own_ops, own_weights]

time: 47.6 us -> 47.2 us (level)
  waiting for transfers between devices: 8.72 us -> 7.96 us
    ppermute x4 -> x5, waiting for transfers between devices: 5.11 us -> 4.35 us  [col_swap(): return lax.ppermute(value, 'cols', [(i, i ^ partner) for i in range(cols)])]
    ppermute x4 -> x5, starting transfers between devices: 3.64 us -> 3.97 us  [col_swap(): return lax.ppermute(value, 'cols', [(i, i ^ partner) for i in range(cols)])]
    pallas_call x8 -> x9, Pallas kernels: 7.28 us -> 7.34 us  [call(): pl.pallas_call(kernel, out_shape=out_shape, in_specs=specs or [VMEM] * le...]
  transfers between devices with their start and end apart: 8 -> 9, of which waited for: 7 -> 7; matrix products, arithmetic and copies ran while one was open for 0% -> 0% of each run, Pallas kernels for 10% -> 11%
where the time goes in v5:
time: 47.2 us; the launch traced here: 47 us
  blocking collectives  20.6 us (44%)
  starting transfers between devices  9.23 us (20%)
  Pallas kernels  9.05 us (19%)
  waiting for transfers between devices  7.96 us (17%)
    all_to_all x1, blocking collectives, on_device(): moved = lax.all_to_all(sent, ('rows', 'cols'), 0, 0, tiled=True)  20.6 us
    pallas_call x9, Pallas kernels, call(): pl.pallas_call(kernel, out_shape=out_shape, in_specs=specs or [VMEM] * le...  7.34 us
    ppermute x4, starting transfers between devices, row_swap(): lax.ppermute(value, 'rows', [(i, i ^ partner) for i in range(pieces)])  5.27 us
    ppermute x5, waiting for transfers between devices, col_swap(): return lax.ppermute(value, 'cols', [(i, i ^ partner) for i in range(cols)])  4.35 us
    ppermute x5, starting transfers between devices, col_swap(): return lax.ppermute(value, 'cols', [(i, i ^ partner) for i in range(cols)])  3.97 us
    ppermute x4, waiting for transfers between devices, row_swap(): lax.ppermute(value, 'rows', [(i, i ^ partner) for i in range(pieces)])  3.61 us
    pallas_call x2, Pallas kernels, join(): pl.pallas_call(functools.partial(join_kernel, pieces, lons, start, stop),...  1.71 us
  transfers between devices with their start and end apart: 9, of which 7 were waited for; matrix products, arithmetic and copies ran while one was open for 0% of the time, Pallas kernels for 11%

profile of v5, /device:TPU:0, one launch (start us, length us, event | category | flops | bytes accessed | tf_op | source)
XLA Modules:
  0.0 47.0 jit_solution(14338192153254180745)
XLA Ops:
  0.0 0.9 %shard_map.37 = (f32[136,128]{1,0:T(8,128)S(1)}, f32[3,8,128]{2,1,0:T(8,128)S(1)}) custom-call(f32[8,128,128]{2,1,0:T(8,128)} %zonal.3, f32[3,8,128]{2,1,0:T(8,128)} %bitcast.1), custom_call_target="tpu_custom_call" | custom-call | bytes 100000 | tf_op jit(solution)/shard_map/pallas_call | solution.py:29
  0.9 3.0 %collective-permute-start = (f32[136,128]{1,0:T(8,128)S(1)}, f32[136,128]{1,0:T(8,128)S(1)}, u32[]{:S(2)}, u32[]{:S(2)}) collective-permute-start(f32[136,128]{1,0:T(8,128)S(1)} %get-tuple-element.24), channel_id=1, source_target_pairs={{0,16},{16,0},{1,17},{17,1},{2,18},{18,2},{3,19},{19,3},{4,20},{20... | collective-permute-start | bytes 208904 | tf_op jit(solution)/shard_map/ppermute | solution.py:338
  3.9 1.6 %shard_map.40 = (f32[64,1024]{1,0:T(8,128)S(1)}, f32[64,1024]{1,0:T(8,128)S(1)}, bf16[8,384,128]{2,1,0:T(8,128)(2,1)S(1)}, f32[8,8,128]{2,1,0:T(8,128)S(1)}) custom-call(f32[1024,128]{1,0:T(8,128)} %block.1, f32[8,128,128]{2,1,0:T(8,128)} %zonal.3, f32[3,8,128]{2,1,0:T(8,128)S(1)} %get-tuple-element.25.stencil), custom_call_target="tpu_custom_call" | custom-call | bytes 1048576 | tf_op jit(solution)/shard_map/pallas_call | solution.py:29
  5.5 0.1 collective-permute-start.6
  5.6 0.6 %collective-permute-done.refs_0_ = f32[136,128]{1,0:T(8,128)S(1)} collective-permute-done((f32[136,128]{1,0:T(8,128)S(1)}, f32[136,128]{1,0:T(8,128)S(1)}, u32[]{:S(2)}, u32[]{:S(2)}) %collective-permute-start) | collective-permute-done | bytes 69664 | tf_op jit(solution)/shard_map/ppermute | solution.py:338
  6.2 3.0 %collective-permute-start.2 = (f32[136,128]{1,0:T(8,128)S(1)}, f32[136,128]{1,0:T(8,128)S(1)}, u32[]{:S(2)}, u32[]{:S(2)}) collective-permute-start(f32[136,128]{1,0:T(8,128)S(1)} %collective-permute-done.refs_0_), channel_id=1, source_target_pairs={{0,6},{1,7},{2,4},{3,5},{4,2},{5,3},{6,0},{7,1},{8,14},{9,15},{10,... | collective-permute-start | bytes 208904 | tf_op jit(solution)/shard_map/ppermute | solution.py:341
  9.2 0.4 collective-permute-start.1
  9.7 0.1 collective-permute-start.4
  9.8 2.0 %collective-permute-done.2.refs_2_ = f32[136,128]{1,0:T(8,128)S(1)} collective-permute-done((f32[136,128]{1,0:T(8,128)S(1)}, f32[136,128]{1,0:T(8,128)S(1)}, u32[]{:S(2)}, u32[]{:S(2)}) %collective-permute-start.2) | collective-permute-done | bytes 69664 | tf_op jit(solution)/shard_map/ppermute | solution.py:341
  11.7 1.8 %collective-permute-done.1.refs_1_ = f32[136,128]{1,0:T(8,128)S(1)} collective-permute-done((f32[136,128]{1,0:T(8,128)S(1)}, f32[136,128]{1,0:T(8,128)S(1)}, u32[]{:S(2)}, u32[]{:S(2)}) %collective-permute-start.1) | collective-permute-done | bytes 69664 | tf_op jit(solution)/shard_map/ppermute | solution.py:341
  13.5 0.1 shard_map.38.refs_0_
  13.7 0.1 collective-permute-start.3
  13.7 0.2 collective-permute-done.4.refs_0_
  14.0 0.1 shard_map.39.refs_2_
  14.1 0.3 collective-permute-start.5
  14.4 0.0 collective-permute-done.6.refs_1_
  14.4 0.6 %shard_map.41 = (f32[16,64,128]{2,1,0:T(8,128)S(1)}, f32[3,64,128]{2,1,0:T(8,128)S(1)}) custom-call(f32[64,1024]{1,0:T(8,128)S(1)} %get-tuple-element.28.refs_0_, f32[64,1024]{1,0:T(8,128)S(1)} %collective-permute-done.6.refs_1_, bf16[8,384,128]{2,1,0:T(8,128)(2,1)S(1)} %get-tuple-element.26.refs_2_.refs_4_, f32[8,8,128]{2,1,0:T(8,128)S(1)} %get-tuple-element.27.refs_3_.refs_5_), custom_call_target="tpu_custom_call" | custom-call | flops 500000000 | bytes 1000000 | tf_op jit(solution)/shard_map/pallas_call | solution.py:29
  15.0 0.4 collective-permute-done.5.refs_3_
  15.4 0.0 collective-permute-done.3.refs_1_
  15.4 1.1 %shard_map.42 = (f32[32,32,128]{2,1,0:T(8,128)S(1)}, bf16[16,384,128]{2,1,0:T(8,128)(2,1)S(1)}, f32[16,8,128]{2,1,0:T(8,128)S(1)}) custom-call(f32[3,136,128]{2,1,0:T(8,128)S(1)} %shard_map.38.refs_0_, f32[3,136,128]{2,1,0:T(8,128)S(1)} %collective-permute-done.3.refs_1_, f32[1,136,128]{2,1,0:T(8,128)S(1)} %shard_map.39.refs_2_, ...), custom_call_target="tpu_custom_call" | custom-call | flops 301989888 | tf_op jit(solution)/shard_map/pallas_call | solution.py:29
  16.5 20.6 %all_to_all.5.refs_0_ = f32[32,32,128]{2,1,0:T(8,128)S(1)} all-to-all(f32[32,32,128]{2,1,0:T(8,128)S(1)} %get-tuple-element.32), channel_id=1, replica_groups=mesh['rows'=2,'cols'=16] {'rows','cols'}, dimensions={0} | all-to-all | bytes 1048576 | tf_op jit(solution)/shard_map/all_to_all | solution.py:410
  37.1 1.1 %shard_map.43 = (f32[64,512]{1,0:T(8,128)S(1)}, f32[12,64,128]{2,1,0:T(8,128)S(1)}, f32[6,64,128]{2,1,0:T(8,128)S(1)}) custom-call(f32[32,32,128]{2,1,0:T(8,128)S(1)} %all_to_all.5.refs_0_, bf16[16,384,128]{2,1,0:T(8,128)(2,1)S(1)} %get-tuple-element.33.refs_1_.refs_2_, f32[16,8,128]{2,1,0:T(8,128)S(1)} %get-tuple-element.34.refs_2_.refs_3_), custom_call_target="tpu_custom_call" | custom-call | flops 10000000 | tf_op jit(solution)/shard_map/pallas_call | solution.py:29
  38.2 1.1 %collective-permute-start.8 = (f32[64,512]{1,0:T(8,128)S(1)}, f32[64,512]{1,0:T(8,128)S(1)}, u32[]{:S(2)}, u32[]{:S(2)}) collective-permute-start(f32[64,512]{1,0:T(8,128)S(1)} %get-tuple-element.42), channel_id=1, source_target_pairs={{0,16},{16,0},{1,17},{17,1},{2,18},{18,2},{3,19},{19,3},{4,20},{20... | collective-permute-start | bytes 393224 | tf_op jit(solution)/shard_map/ppermute | solution.py:338
  39.3 0.9 %shard_map.44 = (f32[64,512]{1,0:T(8,128)S(1)}, f32[8,64,128]{2,1,0:T(8,128)S(1)}, f32[6,64,128]{2,1,0:T(8,128)S(1)}) custom-call(f32[12,64,128]{2,1,0:T(8,128)S(1)} %get-tuple-element.35.refs_0_, f32[6,64,128]{2,1,0:T(8,128)S(1)} %get-tuple-element.36.refs_1_, bf16[16,384,128]{2,1,0:T(8,128)(2,1)S(1)} %get-tuple-element.33.refs_1_.refs_2_, ...), custom_call_target="tpu_custom_call" | custom-call | flops 10000000 | tf_op jit(solution)/shard_map/pallas_call | solution.py:29
  40.2 1.1 %collective-permute-start.7 = (f32[64,512]{1,0:T(8,128)S(1)}, f32[64,512]{1,0:T(8,128)S(1)}, u32[]{:S(2)}, u32[]{:S(2)}) collective-permute-start(f32[64,512]{1,0:T(8,128)S(1)} %get-tuple-element.40), channel_id=1, source_target_pairs={{0,16},{16,0},{1,17},{17,1},{2,18},{18,2},{3,19},{19,3},{4,20},{20... | collective-permute-start | bytes 393224 | tf_op jit(solution)/shard_map/ppermute | solution.py:338
  41.2 1.0 %shard_map.45 = (f32[64,512]{1,0:T(8,128)S(1)}, f32[64,512]{1,0:T(8,128)S(1)}) custom-call(f32[8,64,128]{2,1,0:T(8,128)S(1)} %get-tuple-element.37.refs_0_, f32[6,64,128]{2,1,0:T(8,128)S(1)} %get-tuple-element.38.refs_1_, bf16[16,384,128]{2,1,0:T(8,128)(2,1)S(1)} %get-tuple-element.33.refs_1_.refs_2_, f32[16,8,128]{2,1,0:T(8,128)S(1)} %get-tuple-element.34.refs_2_.refs_3_), custom_call_target="tpu_custom_call" | custom-call | flops 10000000 | tf_op jit(solution)/shard_map/pallas_call | solution.py:29
  42.2 1.9 %collective-permute-done.8.refs_1_ = f32[64,512]{1,0:T(8,128)S(1)} collective-permute-done((f32[64,512]{1,0:T(8,128)S(1)}, f32[64,512]{1,0:T(8,128)S(1)}, u32[]{:S(2)}, u32[]{:S(2)}) %collective-permute-start.8) | collective-permute-done | bytes 131104 | tf_op jit(solution)/shard_map/ppermute | solution.py:338
  44.1 0.9 %shard_map.46.refs_2_ = f32[1024,128]{1,0:T(8,128)} custom-call(f32[64,512]{1,0:T(8,128)S(1)} %get-tuple-element.41.refs_0_, f32[64,512]{1,0:T(8,128)S(1)} %collective-permute-done.8.refs_1_), custom_call_target="tpu_custom_call" | custom-call | tf_op jit(solution)/shard_map/pallas_call | solution.py:310
  44.9 1.2 %collective-permute-done.7.refs_1_ = f32[64,512]{1,0:T(8,128)S(1)} collective-permute-done((f32[64,512]{1,0:T(8,128)S(1)}, f32[64,512]{1,0:T(8,128)S(1)}, u32[]{:S(2)}, u32[]{:S(2)}) %collective-permute-start.7) | collective-permute-done | bytes 131104 | tf_op jit(solution)/shard_map/ppermute | solution.py:338
  46.1 0.9 %shard_map.47 = f32[1024,128]{1,0:T(8,128)} custom-call(f32[64,512]{1,0:T(8,128)S(1)} %get-tuple-element.39.refs_0_, f32[64,512]{1,0:T(8,128)S(1)} %collective-permute-done.7.refs_1_, f32[1024,128]{1,0:T(8,128)} %shard_map.46.refs_2_), custom_call_target="tpu_custom_call", output_to_operand_aliasing={{}: (2, {})} | custom-call | tf_op jit(solution)/shard_map/pallas_call | solution.py:310
Async XLA Ops:
  0.9 5.3 %collective-permute-start = (f32[136,128]{1,0:T(8,128)S(1)}, f32[136,128]{1,0:T(8,128)S(1)}, u32[]{:S(2)}, u32[]{:S(2)}) collective-permute-start(f32[136,128]{1,0:T(8,128)S(1)} %get-tuple-element.24), channel_id=1, source_target_pairs={{0,16},{16,0},{1,17},{17,1},{2,18},{18,2},{3,19},{19,3},{4,20},{20... | collective-permute-start | bytes 208904 | tf_op jit(solution)/shard_map/ppermute | solution.py:338
  5.5 8.8 %collective-permute-start.6 = (f32[64,1024]{1,0:T(8,128)S(1)}, f32[64,1024]{1,0:T(8,128)S(1)}, u32[]{:S(2)}, u32[]{:S(2)}) collective-permute-start(f32[64,1024]{1,0:T(8,128)S(1)} %get-tuple-element.29), channel_id=1, source_target_pairs={{0,16},{16,0},{1,17},{17,1},{2,18},{18,2},{3,19},{19,3},{4,20},{20... | collective-permute-start | bytes 786440 | tf_op jit(solution)/shard_map/ppermute | solution.py:338
  6.2 5.5 %collective-permute-start.2 = (f32[136,128]{1,0:T(8,128)S(1)}, f32[136,128]{1,0:T(8,128)S(1)}, u32[]{:S(2)}, u32[]{:S(2)}) collective-permute-start(f32[136,128]{1,0:T(8,128)S(1)} %collective-permute-done.refs_0_), channel_id=1, source_target_pairs={{0,6},{1,7},{2,4},{3,5},{4,2},{5,3},{6,0},{7,1},{8,14},{9,15},{10,... | collective-permute-start | bytes 208904 | tf_op jit(solution)/shard_map/ppermute | solution.py:341
  9.2 4.3 %collective-permute-start.1 = (f32[136,128]{1,0:T(8,128)S(1)}, f32[136,128]{1,0:T(8,128)S(1)}, u32[]{:S(2)}, u32[]{:S(2)}) collective-permute-start(f32[136,128]{1,0:T(8,128)S(1)} %collective-permute-done.refs_0_), channel_id=1, source_target_pairs={{0,4},{1,5},{2,6},{3,7},{4,0},{5,1},{6,2},{7,3},{8,12},{9,13},{10,... | collective-permute-start | bytes 208904 | tf_op jit(solution)/shard_map/ppermute | solution.py:341
  9.7 4.3 %collective-permute-start.4 = (f32[136,128]{1,0:T(8,128)S(1)}, f32[136,128]{1,0:T(8,128)S(1)}, u32[]{:S(2)}, u32[]{:S(2)}) collective-permute-start(f32[136,128]{1,0:T(8,128)S(1)} %collective-permute-done.refs_0_), channel_id=1, source_target_pairs={{0,2},{1,3},{2,0},{3,1},{4,6},{5,7},{6,4},{7,5},{8,10},{9,11},{10,... | collective-permute-start | bytes 208904 | tf_op jit(solution)/shard_map/ppermute | solution.py:341
  13.7 1.7 %collective-permute-start.3 = (f32[3,136,128]{2,1,0:T(8,128)S(1)}, f32[3,136,128]{2,1,0:T(8,128)S(1)}, u32[]{:S(2)}, u32[]{:S(2)}) collective-permute-start(f32[3,136,128]{2,1,0:T(8,128)S(1)} %shard_map.38.refs_0_), channel_id=1, source_target_pairs={{0,1},{1,0},{2,3},{3,2},{4,5},{5,4},{6,7},{7,6},{8,9},{9,8},{10,11... | collective-permute-start | bytes 626696 | tf_op jit(solution)/shard_map/ppermute | solution.py:341
  14.1 1.3 %collective-permute-start.5 = (f32[1,136,128]{2,1,0:T(8,128)S(1)}, f32[1,136,128]{2,1,0:T(8,128)S(1)}, u32[]{:S(2)}, u32[]{:S(2)}) collective-permute-start(f32[1,136,128]{2,1,0:T(8,128)S(1)} %shard_map.39.refs_2_), channel_id=1, source_target_pairs={{0,1},{1,0},{2,3},{3,2},{4,5},{5,4},{6,7},{7,6},{8,9},{9,8},{10,11... | collective-permute-start | bytes 208904 | tf_op jit(solution)/shard_map/ppermute | solution.py:341
  38.2 5.9 %collective-permute-start.8 = (f32[64,512]{1,0:T(8,128)S(1)}, f32[64,512]{1,0:T(8,128)S(1)}, u32[]{:S(2)}, u32[]{:S(2)}) collective-permute-start(f32[64,512]{1,0:T(8,128)S(1)} %get-tuple-element.42), channel_id=1, source_target_pairs={{0,16},{16,0},{1,17},{17,1},{2,18},{18,2},{3,19},{19,3},{4,20},{20... | collective-permute-start | bytes 393224 | tf_op jit(solution)/shard_map/ppermute | solution.py:338
  40.2 5.9 %collective-permute-start.7 = (f32[64,512]{1,0:T(8,128)S(1)}, f32[64,512]{1,0:T(8,128)S(1)}, u32[]{:S(2)}, u32[]{:S(2)}) collective-permute-start(f32[64,512]{1,0:T(8,128)S(1)} %get-tuple-element.40), channel_id=1, source_target_pairs={{0,16},{16,0},{1,17},{17,1},{2,18},{18,2},{3,19},{19,3},{4,20},{20... | collective-permute-start | bytes 393224 | tf_op jit(solution)/shard_map/ppermute | solution.py:338

commit v6 on v5

--- a/solution.py
+++ b/solution.py
@@ -329,7 +329,7 @@
     lat_rows, lons = zonal.shape[:2]
     lats = lat_rows * pieces
     width = wide // pieces
-    hops = (0, 2, 4, 6) if lat_rows % 8 == 0 and cols % 8 == 0 else (0,)
+    hops = (0, 6, 2, 4) if lat_rows % 8 == 0 and cols % 8 == 0 else (0,)
     share = 2 * len(hops)
     count = lat_rows // share
     chunks = tall // min(tall, 128)

time: 47.2 us -> 47.2 us (level)
  waiting for transfers between devices: 7.96 us -> 9.22 us
  blocking collectives: 20.6 us -> 19.6 us
    ppermute x5, waiting for transfers between devices: 4.35 us -> 5.61 us  [col_swap(): return lax.ppermute(value, 'cols', [(i, i ^ partner) for i in range(cols)])]
    all_to_all x1, blocking collectives: 20.6 us -> 19.6 us  [on_device(): moved = lax.all_to_all(sent, ('rows', 'cols'), 0, 0, tiled=True)]
where the time goes in v6:
time: 47.2 us; the launch traced here: 47 us
  blocking collectives  19.6 us (42%)
  waiting for transfers between devices  9.22 us (20%)
  Pallas kernels  9.06 us (19%)
  starting transfers between devices  8.98 us (19%)
    all_to_all x1, blocking collectives, on_device(): moved = lax.all_to_all(sent, ('rows', 'cols'), 0, 0, tiled=True)  19.6 us
    pallas_call x9, Pallas kernels, call(): pl.pallas_call(kernel, out_shape=out_shape, in_specs=specs or [VMEM] * le...  7.35 us
    ppermute x5, waiting for transfers between devices, col_swap(): return lax.ppermute(value, 'cols', [(i, i ^ partner) for i in range(cols)])  5.61 us
    ppermute x4, starting transfers between devices, row_swap(): lax.ppermute(value, 'rows', [(i, i ^ partner) for i in range(pieces)])  5.27 us
    ppermute x5, starting transfers between devices, col_swap(): return lax.ppermute(value, 'cols', [(i, i ^ partner) for i in range(cols)])  3.71 us
    ppermute x4, waiting for transfers between devices, row_swap(): lax.ppermute(value, 'rows', [(i, i ^ partner) for i in range(pieces)])  3.61 us
    pallas_call x2, Pallas kernels, join(): pl.pallas_call(functools.partial(join_kernel, pieces, lons, start, stop),...  1.71 us
  transfers between devices with their start and end apart: 9, of which 7 were waited for; matrix products, arithmetic and copies ran while one was open for 0% of the time, Pallas kernels for 11%

profile of v6, /device:TPU:0, one launch (start us, length us, event | category | flops | bytes accessed | tf_op | source)
XLA Modules:
  0.0 47.0 jit_solution(16921385684638165715)
XLA Ops:
  0.0 0.9 %shard_map.37 = (f32[136,128]{1,0:T(8,128)S(1)}, f32[3,8,128]{2,1,0:T(8,128)S(1)}) custom-call(f32[8,128,128]{2,1,0:T(8,128)} %zonal.3, f32[3,8,128]{2,1,0:T(8,128)} %bitcast.1), custom_call_target="tpu_custom_call" | custom-call | bytes 100000 | tf_op jit(solution)/shard_map/pallas_call | solution.py:29
  0.9 3.0 %collective-permute-start = (f32[136,128]{1,0:T(8,128)S(1)}, f32[136,128]{1,0:T(8,128)S(1)}, u32[]{:S(2)}, u32[]{:S(2)}) collective-permute-start(f32[136,128]{1,0:T(8,128)S(1)} %get-tuple-element.24), channel_id=1, source_target_pairs={{0,16},{16,0},{1,17},{17,1},{2,18},{18,2},{3,19},{19,3},{4,20},{20... | collective-permute-start | bytes 208904 | tf_op jit(solution)/shard_map/ppermute | solution.py:338
  3.9 1.6 %shard_map.40 = (f32[64,1024]{1,0:T(8,128)S(1)}, f32[64,1024]{1,0:T(8,128)S(1)}, bf16[8,384,128]{2,1,0:T(8,128)(2,1)S(1)}, f32[8,8,128]{2,1,0:T(8,128)S(1)}) custom-call(f32[1024,128]{1,0:T(8,128)} %block.1, f32[8,128,128]{2,1,0:T(8,128)} %zonal.3, f32[3,8,128]{2,1,0:T(8,128)S(1)} %get-tuple-element.25.stencil), custom_call_target="tpu_custom_call" | custom-call | bytes 1048576 | tf_op jit(solution)/shard_map/pallas_call | solution.py:29
  5.5 0.1 collective-permute-start.6
  5.6 0.6 %collective-permute-done.refs_0_ = f32[136,128]{1,0:T(8,128)S(1)} collective-permute-done((f32[136,128]{1,0:T(8,128)S(1)}, f32[136,128]{1,0:T(8,128)S(1)}, u32[]{:S(2)}, u32[]{:S(2)}) %collective-permute-start) | collective-permute-done | bytes 69664 | tf_op jit(solution)/shard_map/ppermute | solution.py:338
  6.2 2.1 %collective-permute-start.2 = (f32[136,128]{1,0:T(8,128)S(1)}, f32[136,128]{1,0:T(8,128)S(1)}, u32[]{:S(2)}, u32[]{:S(2)}) collective-permute-start(f32[136,128]{1,0:T(8,128)S(1)} %collective-permute-done.refs_0_), channel_id=1, source_target_pairs={{0,4},{1,5},{2,6},{3,7},{4,0},{5,1},{6,2},{7,3},{8,12},{9,13},{10,... | collective-permute-start | bytes 208904 | tf_op jit(solution)/shard_map/ppermute | solution.py:341
  8.3 1.5 %collective-permute-start.1 = (f32[136,128]{1,0:T(8,128)S(1)}, f32[136,128]{1,0:T(8,128)S(1)}, u32[]{:S(2)}, u32[]{:S(2)}) collective-permute-start(f32[136,128]{1,0:T(8,128)S(1)} %collective-permute-done.refs_0_), channel_id=1, source_target_pairs={{0,2},{1,3},{2,0},{3,1},{4,6},{5,7},{6,4},{7,5},{8,10},{9,11},{10,... | collective-permute-start | bytes 208904 | tf_op jit(solution)/shard_map/ppermute | solution.py:341
  9.8 0.0 collective-permute-start.4
  9.8 0.9 %collective-permute-done.2.refs_2_ = f32[136,128]{1,0:T(8,128)S(1)} collective-permute-done((f32[136,128]{1,0:T(8,128)S(1)}, f32[136,128]{1,0:T(8,128)S(1)}, u32[]{:S(2)}, u32[]{:S(2)}) %collective-permute-start.2) | collective-permute-done | bytes 69664 | tf_op jit(solution)/shard_map/ppermute | solution.py:341
  10.7 2.4 %collective-permute-done.1.refs_1_ = f32[136,128]{1,0:T(8,128)S(1)} collective-permute-done((f32[136,128]{1,0:T(8,128)S(1)}, f32[136,128]{1,0:T(8,128)S(1)}, u32[]{:S(2)}, u32[]{:S(2)}) %collective-permute-start.1) | collective-permute-done | bytes 69664 | tf_op jit(solution)/shard_map/ppermute | solution.py:341
  13.1 0.1 shard_map.38.refs_0_
  13.2 0.1 collective-permute-start.3
  13.3 1.7 %collective-permute-done.4.refs_0_ = f32[136,128]{1,0:T(8,128)S(1)} collective-permute-done((f32[136,128]{1,0:T(8,128)S(1)}, f32[136,128]{1,0:T(8,128)S(1)}, u32[]{:S(2)}, u32[]{:S(2)}) %collective-permute-start.4) | collective-permute-done | bytes 69664 | tf_op jit(solution)/shard_map/ppermute | solution.py:341
  15.0 0.1 shard_map.39.refs_2_
  15.1 0.1 collective-permute-start.5
  15.2 0.0 collective-permute-done.6.refs_1_
  15.2 0.6 %shard_map.41 = (f32[16,64,128]{2,1,0:T(8,128)S(1)}, f32[3,64,128]{2,1,0:T(8,128)S(1)}) custom-call(f32[64,1024]{1,0:T(8,128)S(1)} %get-tuple-element.28.refs_0_, f32[64,1024]{1,0:T(8,128)S(1)} %collective-permute-done.6.refs_1_, bf16[8,384,128]{2,1,0:T(8,128)(2,1)S(1)} %get-tuple-element.26.refs_2_.refs_4_, f32[8,8,128]{2,1,0:T(8,128)S(1)} %get-tuple-element.27.refs_3_.refs_5_), custom_call_target="tpu_custom_call" | custom-call | flops 500000000 | bytes 1000000 | tf_op jit(solution)/shard_map/pallas_call | solution.py:29
  15.8 0.6 %collective-permute-done.5.refs_3_ = f32[1,136,128]{2,1,0:T(8,128)S(1)} collective-permute-done((f32[1,136,128]{2,1,0:T(8,128)S(1)}, f32[1,136,128]{2,1,0:T(8,128)S(1)}, u32[]{:S(2)}, u32[]{:S(2)}) %collective-permute-start.5) | collective-permute-done | bytes 69664 | tf_op jit(solution)/shard_map/ppermute | solution.py:341
  16.4 0.0 collective-permute-done.3.refs_1_
  16.4 1.1 %shard_map.42 = (f32[32,32,128]{2,1,0:T(8,128)S(1)}, bf16[16,384,128]{2,1,0:T(8,128)(2,1)S(1)}, f32[16,8,128]{2,1,0:T(8,128)S(1)}) custom-call(f32[3,136,128]{2,1,0:T(8,128)S(1)} %shard_map.38.refs_0_, f32[3,136,128]{2,1,0:T(8,128)S(1)} %collective-permute-done.3.refs_1_, f32[1,136,128]{2,1,0:T(8,128)S(1)} %shard_map.39.refs_2_, ...), custom_call_target="tpu_custom_call" | custom-call | flops 301989888 | tf_op jit(solution)/shard_map/pallas_call | solution.py:29
  17.5 19.6 %all_to_all.5.refs_0_ = f32[32,32,128]{2,1,0:T(8,128)S(1)} all-to-all(f32[32,32,128]{2,1,0:T(8,128)S(1)} %get-tuple-element.32), channel_id=1, replica_groups=mesh['rows'=2,'cols'=16] {'rows','cols'}, dimensions={0} | all-to-all | bytes 1048576 | tf_op jit(solution)/shard_map/all_to_all | solution.py:410
  37.1 1.1 %shard_map.43 = (f32[64,512]{1,0:T(8,128)S(1)}, f32[12,64,128]{2,1,0:T(8,128)S(1)}, f32[6,64,128]{2,1,0:T(8,128)S(1)}) custom-call(f32[32,32,128]{2,1,0:T(8,128)S(1)} %all_to_all.5.refs_0_, bf16[16,384,128]{2,1,0:T(8,128)(2,1)S(1)} %get-tuple-element.33.refs_1_.refs_2_, f32[16,8,128]{2,1,0:T(8,128)S(1)} %get-tuple-element.34.refs_2_.refs_3_), custom_call_target="tpu_custom_call" | custom-call | flops 10000000 | tf_op jit(solution)/shard_map/pallas_call | solution.py:29
  38.2 1.1 %collective-permute-start.8 = (f32[64,512]{1,0:T(8,128)S(1)}, f32[64,512]{1,0:T(8,128)S(1)}, u32[]{:S(2)}, u32[]{:S(2)}) collective-permute-start(f32[64,512]{1,0:T(8,128)S(1)} %get-tuple-element.42), channel_id=1, source_target_pairs={{0,16},{16,0},{1,17},{17,1},{2,18},{18,2},{3,19},{19,3},{4,20},{20... | collective-permute-start | bytes 393224 | tf_op jit(solution)/shard_map/ppermute | solution.py:338
  39.3 0.9 %shard_map.44 = (f32[64,512]{1,0:T(8,128)S(1)}, f32[8,64,128]{2,1,0:T(8,128)S(1)}, f32[6,64,128]{2,1,0:T(8,128)S(1)}) custom-call(f32[12,64,128]{2,1,0:T(8,128)S(1)} %get-tuple-element.35.refs_0_, f32[6,64,128]{2,1,0:T(8,128)S(1)} %get-tuple-element.36.refs_1_, bf16[16,384,128]{2,1,0:T(8,128)(2,1)S(1)} %get-tuple-element.33.refs_1_.refs_2_, ...), custom_call_target="tpu_custom_call" | custom-call | flops 10000000 | tf_op jit(solution)/shard_map/pallas_call | solution.py:29
  40.2 1.1 %collective-permute-start.7 = (f32[64,512]{1,0:T(8,128)S(1)}, f32[64,512]{1,0:T(8,128)S(1)}, u32[]{:S(2)}, u32[]{:S(2)}) collective-permute-start(f32[64,512]{1,0:T(8,128)S(1)} %get-tuple-element.40), channel_id=1, source_target_pairs={{0,16},{16,0},{1,17},{17,1},{2,18},{18,2},{3,19},{19,3},{4,20},{20... | collective-permute-start | bytes 393224 | tf_op jit(solution)/shard_map/ppermute | solution.py:338
  41.3 1.0 %shard_map.45 = (f32[64,512]{1,0:T(8,128)S(1)}, f32[64,512]{1,0:T(8,128)S(1)}) custom-call(f32[8,64,128]{2,1,0:T(8,128)S(1)} %get-tuple-element.37.refs_0_, f32[6,64,128]{2,1,0:T(8,128)S(1)} %get-tuple-element.38.refs_1_, bf16[16,384,128]{2,1,0:T(8,128)(2,1)S(1)} %get-tuple-element.33.refs_1_.refs_2_, f32[16,8,128]{2,1,0:T(8,128)S(1)} %get-tuple-element.34.refs_2_.refs_3_), custom_call_target="tpu_custom_call" | custom-call | flops 10000000 | tf_op jit(solution)/shard_map/pallas_call | solution.py:29
  42.2 1.9 %collective-permute-done.8.refs_1_ = f32[64,512]{1,0:T(8,128)S(1)} collective-permute-done((f32[64,512]{1,0:T(8,128)S(1)}, f32[64,512]{1,0:T(8,128)S(1)}, u32[]{:S(2)}, u32[]{:S(2)}) %collective-permute-start.8) | collective-permute-done | bytes 131104 | tf_op jit(solution)/shard_map/ppermute | solution.py:338
  44.1 0.9 %shard_map.46.refs_2_ = f32[1024,128]{1,0:T(8,128)} custom-call(f32[64,512]{1,0:T(8,128)S(1)} %get-tuple-element.41.refs_0_, f32[64,512]{1,0:T(8,128)S(1)} %collective-permute-done.8.refs_1_), custom_call_target="tpu_custom_call" | custom-call | tf_op jit(solution)/shard_map/pallas_call | solution.py:310
  45.0 1.2 %collective-permute-done.7.refs_1_ = f32[64,512]{1,0:T(8,128)S(1)} collective-permute-done((f32[64,512]{1,0:T(8,128)S(1)}, f32[64,512]{1,0:T(8,128)S(1)}, u32[]{:S(2)}, u32[]{:S(2)}) %collective-permute-start.7) | collective-permute-done | bytes 131104 | tf_op jit(solution)/shard_map/ppermute | solution.py:338
  46.1 0.9 %shard_map.47 = f32[1024,128]{1,0:T(8,128)} custom-call(f32[64,512]{1,0:T(8,128)S(1)} %get-tuple-element.39.refs_0_, f32[64,512]{1,0:T(8,128)S(1)} %collective-permute-done.7.refs_1_, f32[1024,128]{1,0:T(8,128)} %shard_map.46.refs_2_), custom_call_target="tpu_custom_call", output_to_operand_aliasing={{}: (2, {})} | custom-call | tf_op jit(solution)/shard_map/pallas_call | solution.py:310
Async XLA Ops:
  0.9 5.3 %collective-permute-start = (f32[136,128]{1,0:T(8,128)S(1)}, f32[136,128]{1,0:T(8,128)S(1)}, u32[]{:S(2)}, u32[]{:S(2)}) collective-permute-start(f32[136,128]{1,0:T(8,128)S(1)} %get-tuple-element.24), channel_id=1, source_target_pairs={{0,16},{16,0},{1,17},{17,1},{2,18},{18,2},{3,19},{19,3},{4,20},{20... | collective-permute-start | bytes 208904 | tf_op jit(solution)/shard_map/ppermute | solution.py:338
  5.5 9.6 %collective-permute-start.6 = (f32[64,1024]{1,0:T(8,128)S(1)}, f32[64,1024]{1,0:T(8,128)S(1)}, u32[]{:S(2)}, u32[]{:S(2)}) collective-permute-start(f32[64,1024]{1,0:T(8,128)S(1)} %get-tuple-element.29), channel_id=1, source_target_pairs={{0,16},{16,0},{1,17},{17,1},{2,18},{18,2},{3,19},{19,3},{4,20},{20... | collective-permute-start | bytes 786440 | tf_op jit(solution)/shard_map/ppermute | solution.py:338
  6.2 4.5 %collective-permute-start.2 = (f32[136,128]{1,0:T(8,128)S(1)}, f32[136,128]{1,0:T(8,128)S(1)}, u32[]{:S(2)}, u32[]{:S(2)}) collective-permute-start(f32[136,128]{1,0:T(8,128)S(1)} %collective-permute-done.refs_0_), channel_id=1, source_target_pairs={{0,4},{1,5},{2,6},{3,7},{4,0},{5,1},{6,2},{7,3},{8,12},{9,13},{10,... | collective-permute-start | bytes 208904 | tf_op jit(solution)/shard_map/ppermute | solution.py:341
  8.3 4.8 %collective-permute-start.1 = (f32[136,128]{1,0:T(8,128)S(1)}, f32[136,128]{1,0:T(8,128)S(1)}, u32[]{:S(2)}, u32[]{:S(2)}) collective-permute-start(f32[136,128]{1,0:T(8,128)S(1)} %collective-permute-done.refs_0_), channel_id=1, source_target_pairs={{0,2},{1,3},{2,0},{3,1},{4,6},{5,7},{6,4},{7,5},{8,10},{9,11},{10,... | collective-permute-start | bytes 208904 | tf_op jit(solution)/shard_map/ppermute | solution.py:341
  9.8 5.2 %collective-permute-start.4 = (f32[136,128]{1,0:T(8,128)S(1)}, f32[136,128]{1,0:T(8,128)S(1)}, u32[]{:S(2)}, u32[]{:S(2)}) collective-permute-start(f32[136,128]{1,0:T(8,128)S(1)} %collective-permute-done.refs_0_), channel_id=1, source_target_pairs={{0,6},{1,7},{2,4},{3,5},{4,2},{5,3},{6,0},{7,1},{8,14},{9,15},{10,... | collective-permute-start | bytes 208904 | tf_op jit(solution)/shard_map/ppermute | solution.py:341
  13.2 3.2 %collective-permute-start.3 = (f32[3,136,128]{2,1,0:T(8,128)S(1)}, f32[3,136,128]{2,1,0:T(8,128)S(1)}, u32[]{:S(2)}, u32[]{:S(2)}) collective-permute-start(f32[3,136,128]{2,1,0:T(8,128)S(1)} %shard_map.38.refs_0_), channel_id=1, source_target_pairs={{0,1},{1,0},{2,3},{3,2},{4,5},{5,4},{6,7},{7,6},{8,9},{9,8},{10,11... | collective-permute-start | bytes 626696 | tf_op jit(solution)/shard_map/ppermute | solution.py:341
  15.1 1.3 %collective-permute-start.5 = (f32[1,136,128]{2,1,0:T(8,128)S(1)}, f32[1,136,128]{2,1,0:T(8,128)S(1)}, u32[]{:S(2)}, u32[]{:S(2)}) collective-permute-start(f32[1,136,128]{2,1,0:T(8,128)S(1)} %shard_map.39.refs_2_), channel_id=1, source_target_pairs={{0,1},{1,0},{2,3},{3,2},{4,5},{5,4},{6,7},{7,6},{8,9},{9,8},{10,11... | collective-permute-start | bytes 208904 | tf_op jit(solution)/shard_map/ppermute | solution.py:341
  38.2 5.9 %collective-permute-start.8 = (f32[64,512]{1,0:T(8,128)S(1)}, f32[64,512]{1,0:T(8,128)S(1)}, u32[]{:S(2)}, u32[]{:S(2)}) collective-permute-start(f32[64,512]{1,0:T(8,128)S(1)} %get-tuple-element.42), channel_id=1, source_target_pairs={{0,16},{16,0},{1,17},{17,1},{2,18},{18,2},{3,19},{19,3},{4,20},{20... | collective-permute-start | bytes 393224 | tf_op jit(solution)/shard_map/ppermute | solution.py:338
  40.2 6.0 %collective-permute-start.7 = (f32[64,512]{1,0:T(8,128)S(1)}, f32[64,512]{1,0:T(8,128)S(1)}, u32[]{:S(2)}, u32[]{:S(2)}) collective-permute-start(f32[64,512]{1,0:T(8,128)S(1)} %get-tuple-element.40), channel_id=1, source_target_pairs={{0,16},{16,0},{1,17},{17,1},{2,18},{18,2},{3,19},{19,3},{4,20},{20... | collective-permute-start | bytes 393224 | tf_op jit(solution)/shard_map/ppermute | solution.py:338

commit v7 on v5

--- a/solution.py
+++ b/solution.py
@@ -280,19 +280,24 @@
 
 
 def join_kernel(pieces, lons, start, stop, *refs):
-    stack, held, sems = refs[-3:]
-    blocks, out = refs[:pieces], refs[-4]
+    held, sems = refs[-2:]
+    blocks, out = refs[:pieces], refs[-3]
     me = lax.axis_index("rows")
     base = 0
     if pieces == 2:
         lat_rows = out.shape[0] // lons
         base = pl.multiple_of(jnp.where(me == 0, start, lat_rows - stop) * lons, lons)
-    for partner in range(pieces):
-        stack[me ^ partner] = blocks[partner][...]
     copies = []
     for at in range(stop - start):
         first = at * lons
-        rows = jnp.concatenate([stack[i, :, first : first + lons] for i in range(pieces)], axis=0)
+        found = [block[:, first : first + lons] for block in blocks]
+        parts = []
+        for i in range(pieces):
+            part = found[0]
+            for partner in range(1, pieces):
+                part = jnp.where((me ^ partner) == i, found[partner], part)
+            parts.append(part)
+        rows = jnp.concatenate(parts, axis=0)
         held[first : first + lons, :] = rows.T
         copies.append(
             pltpu.make_async_copy(
@@ -305,7 +310,6 @@
 
 
 def join(pieces, lons, start, stop, shape, blocks, given=None):
-    width = blocks[0].shape[0]
     size = stop - start
     return pl.pallas_call(
         functools.partial(join_kernel, pieces, lons, start, stop),
@@ -313,7 +317,6 @@
         in_specs=[VMEM] * pieces + ([] if given is None else [HBM]),
         out_specs=HBM,
         scratch_shapes=[
-            pltpu.VMEM((pieces, width, size * lons), F32),
             pltpu.VMEM((size * lons, shape[1]), F32),
             pltpu.SemaphoreType.DMA((size,)),
         ],

time: 47.2 us -> 47.2 us (level)
  no operation moved by 1% of the time
where the time goes in v7:
time: 47.2 us; the launch traced here: 46.9 us
  blocking collectives  20.6 us (44%)
  starting transfers between devices  9.23 us (20%)
  Pallas kernels  9.02 us (19%)
  waiting for transfers between devices  7.98 us (17%)
    all_to_all x1, blocking collectives, on_device(): moved = lax.all_to_all(sent, ('rows', 'cols'), 0, 0, tiled=True)  20.6 us
    pallas_call x9, Pallas kernels, call(): pl.pallas_call(kernel, out_shape=out_shape, in_specs=specs or [VMEM] * le...  7.34 us
    ppermute x4, starting transfers between devices, row_swap(): lax.ppermute(value, 'rows', [(i, i ^ partner) for i in range(pieces)])  5.27 us
    ppermute x5, waiting for transfers between devices, col_swap(): return lax.ppermute(value, 'cols', [(i, i ^ partner) for i in range(cols)])  4.35 us
    ppermute x5, starting transfers between devices, col_swap(): return lax.ppermute(value, 'cols', [(i, i ^ partner) for i in range(cols)])  3.97 us
    ppermute x4, waiting for transfers between devices, row_swap(): lax.ppermute(value, 'rows', [(i, i ^ partner) for i in range(pieces)])  3.62 us
    pallas_call x2, Pallas kernels, join(): pl.pallas_call(functools.partial(join_kernel, pieces, lons, start, stop),...  1.68 us
  transfers between devices with their start and end apart: 9, of which 7 were waited for; matrix products, arithmetic and copies ran while one was open for 0% of the time, Pallas kernels for 11%

profile of v7, /device:TPU:0, one launch (start us, length us, event | category | flops | bytes accessed | tf_op | source)
XLA Modules:
  0.0 46.9 jit_solution(5831304183350451812)
XLA Ops:
  0.0 0.9 %shard_map.37 = (f32[136,128]{1,0:T(8,128)S(1)}, f32[3,8,128]{2,1,0:T(8,128)S(1)}) custom-call(f32[8,128,128]{2,1,0:T(8,128)} %zonal.3, f32[3,8,128]{2,1,0:T(8,128)} %bitcast.1), custom_call_target="tpu_custom_call" | custom-call | bytes 100000 | tf_op jit(solution)/shard_map/pallas_call | solution.py:29
  0.9 3.0 %collective-permute-start = (f32[136,128]{1,0:T(8,128)S(1)}, f32[136,128]{1,0:T(8,128)S(1)}, u32[]{:S(2)}, u32[]{:S(2)}) collective-permute-start(f32[136,128]{1,0:T(8,128)S(1)} %get-tuple-element.24), channel_id=1, source_target_pairs={{0,16},{16,0},{1,17},{17,1},{2,18},{18,2},{3,19},{19,3},{4,20},{20... | collective-permute-start | bytes 208904 | tf_op jit(solution)/shard_map/ppermute | solution.py:341
  3.9 1.6 %shard_map.40 = (f32[64,1024]{1,0:T(8,128)S(1)}, f32[64,1024]{1,0:T(8,128)S(1)}, bf16[8,384,128]{2,1,0:T(8,128)(2,1)S(1)}, f32[8,8,128]{2,1,0:T(8,128)S(1)}) custom-call(f32[1024,128]{1,0:T(8,128)} %block.1, f32[8,128,128]{2,1,0:T(8,128)} %zonal.3, f32[3,8,128]{2,1,0:T(8,128)S(1)} %get-tuple-element.25.stencil), custom_call_target="tpu_custom_call" | custom-call | bytes 1048576 | tf_op jit(solution)/shard_map/pallas_call | solution.py:29
  5.5 0.1 collective-permute-start.6
  5.6 0.6 %collective-permute-done.refs_0_ = f32[136,128]{1,0:T(8,128)S(1)} collective-permute-done((f32[136,128]{1,0:T(8,128)S(1)}, f32[136,128]{1,0:T(8,128)S(1)}, u32[]{:S(2)}, u32[]{:S(2)}) %collective-permute-start) | collective-permute-done | bytes 69664 | tf_op jit(solution)/shard_map/ppermute | solution.py:341
  6.2 3.0 %collective-permute-start.2 = (f32[136,128]{1,0:T(8,128)S(1)}, f32[136,128]{1,0:T(8,128)S(1)}, u32[]{:S(2)}, u32[]{:S(2)}) collective-permute-start(f32[136,128]{1,0:T(8,128)S(1)} %collective-permute-done.refs_0_), channel_id=1, source_target_pairs={{0,6},{1,7},{2,4},{3,5},{4,2},{5,3},{6,0},{7,1},{8,14},{9,15},{10,... | collective-permute-start | bytes 208904 | tf_op jit(solution)/shard_map/ppermute | solution.py:344
  9.2 0.4 collective-permute-start.1
  9.7 0.1 collective-permute-start.4
  9.8 2.0 %collective-permute-done.2.refs_2_ = f32[136,128]{1,0:T(8,128)S(1)} collective-permute-done((f32[136,128]{1,0:T(8,128)S(1)}, f32[136,128]{1,0:T(8,128)S(1)}, u32[]{:S(2)}, u32[]{:S(2)}) %collective-permute-start.2) | collective-permute-done | bytes 69664 | tf_op jit(solution)/shard_map/ppermute | solution.py:344
  11.7 1.8 %collective-permute-done.1.refs_1_ = f32[136,128]{1,0:T(8,128)S(1)} collective-permute-done((f32[136,128]{1,0:T(8,128)S(1)}, f32[136,128]{1,0:T(8,128)S(1)}, u32[]{:S(2)}, u32[]{:S(2)}) %collective-permute-start.1) | collective-permute-done | bytes 69664 | tf_op jit(solution)/shard_map/ppermute | solution.py:344
  13.5 0.1 shard_map.38.refs_0_
  13.7 0.1 collective-permute-start.3
  13.7 0.2 collective-permute-done.4.refs_0_
  14.0 0.1 shard_map.39.refs_2_
  14.1 0.3 collective-permute-start.5
  14.4 0.0 collective-permute-done.6.refs_1_
  14.4 0.6 %shard_map.41 = (f32[16,64,128]{2,1,0:T(8,128)S(1)}, f32[3,64,128]{2,1,0:T(8,128)S(1)}) custom-call(f32[64,1024]{1,0:T(8,128)S(1)} %get-tuple-element.28.refs_0_, f32[64,1024]{1,0:T(8,128)S(1)} %collective-permute-done.6.refs_1_, bf16[8,384,128]{2,1,0:T(8,128)(2,1)S(1)} %get-tuple-element.26.refs_2_.refs_4_, f32[8,8,128]{2,1,0:T(8,128)S(1)} %get-tuple-element.27.refs_3_.refs_5_), custom_call_target="tpu_custom_call" | custom-call | flops 500000000 | bytes 1000000 | tf_op jit(solution)/shard_map/pallas_call | solution.py:29
  15.0 0.4 collective-permute-done.5.refs_3_
  15.4 0.0 collective-permute-done.3.refs_1_
  15.4 1.1 %shard_map.42 = (f32[32,32,128]{2,1,0:T(8,128)S(1)}, bf16[16,384,128]{2,1,0:T(8,128)(2,1)S(1)}, f32[16,8,128]{2,1,0:T(8,128)S(1)}) custom-call(f32[3,136,128]{2,1,0:T(8,128)S(1)} %shard_map.38.refs_0_, f32[3,136,128]{2,1,0:T(8,128)S(1)} %collective-permute-done.3.refs_1_, f32[1,136,128]{2,1,0:T(8,128)S(1)} %shard_map.39.refs_2_, ...), custom_call_target="tpu_custom_call" | custom-call | flops 301989888 | tf_op jit(solution)/shard_map/pallas_call | solution.py:29
  16.5 20.6 %all_to_all.5.refs_0_ = f32[32,32,128]{2,1,0:T(8,128)S(1)} all-to-all(f32[32,32,128]{2,1,0:T(8,128)S(1)} %get-tuple-element.32), channel_id=1, replica_groups=mesh['rows'=2,'cols'=16] {'rows','cols'}, dimensions={0} | all-to-all | bytes 1048576 | tf_op jit(solution)/shard_map/all_to_all | solution.py:413
  37.1 1.1 %shard_map.43 = (f32[64,512]{1,0:T(8,128)S(1)}, f32[12,64,128]{2,1,0:T(8,128)S(1)}, f32[6,64,128]{2,1,0:T(8,128)S(1)}) custom-call(f32[32,32,128]{2,1,0:T(8,128)S(1)} %all_to_all.5.refs_0_, bf16[16,384,128]{2,1,0:T(8,128)(2,1)S(1)} %get-tuple-element.33.refs_1_.refs_2_, f32[16,8,128]{2,1,0:T(8,128)S(1)} %get-tuple-element.34.refs_2_.refs_3_), custom_call_target="tpu_custom_call" | custom-call | flops 10000000 | tf_op jit(solution)/shard_map/pallas_call | solution.py:29
  38.2 1.1 %collective-permute-start.8 = (f32[64,512]{1,0:T(8,128)S(1)}, f32[64,512]{1,0:T(8,128)S(1)}, u32[]{:S(2)}, u32[]{:S(2)}) collective-permute-start(f32[64,512]{1,0:T(8,128)S(1)} %get-tuple-element.42), channel_id=1, source_target_pairs={{0,16},{16,0},{1,17},{17,1},{2,18},{18,2},{3,19},{19,3},{4,20},{20... | collective-permute-start | bytes 393224 | tf_op jit(solution)/shard_map/ppermute | solution.py:341
  39.3 0.9 %shard_map.44 = (f32[64,512]{1,0:T(8,128)S(1)}, f32[8,64,128]{2,1,0:T(8,128)S(1)}, f32[6,64,128]{2,1,0:T(8,128)S(1)}) custom-call(f32[12,64,128]{2,1,0:T(8,128)S(1)} %get-tuple-element.35.refs_0_, f32[6,64,128]{2,1,0:T(8,128)S(1)} %get-tuple-element.36.refs_1_, bf16[16,384,128]{2,1,0:T(8,128)(2,1)S(1)} %get-tuple-element.33.refs_1_.refs_2_, ...), custom_call_target="tpu_custom_call" | custom-call | flops 10000000 | tf_op jit(solution)/shard_map/pallas_call | solution.py:29
  40.2 1.1 %collective-permute-start.7 = (f32[64,512]{1,0:T(8,128)S(1)}, f32[64,512]{1,0:T(8,128)S(1)}, u32[]{:S(2)}, u32[]{:S(2)}) collective-permute-start(f32[64,512]{1,0:T(8,128)S(1)} %get-tuple-element.40), channel_id=1, source_target_pairs={{0,16},{16,0},{1,17},{17,1},{2,18},{18,2},{3,19},{19,3},{4,20},{20... | collective-permute-start | bytes 393224 | tf_op jit(solution)/shard_map/ppermute | solution.py:341
  41.2 1.0 %shard_map.45 = (f32[64,512]{1,0:T(8,128)S(1)}, f32[64,512]{1,0:T(8,128)S(1)}) custom-call(f32[8,64,128]{2,1,0:T(8,128)S(1)} %get-tuple-element.37.refs_0_, f32[6,64,128]{2,1,0:T(8,128)S(1)} %get-tuple-element.38.refs_1_, bf16[16,384,128]{2,1,0:T(8,128)(2,1)S(1)} %get-tuple-element.33.refs_1_.refs_2_, f32[16,8,128]{2,1,0:T(8,128)S(1)} %get-tuple-element.34.refs_2_.refs_3_), custom_call_target="tpu_custom_call" | custom-call | flops 10000000 | tf_op jit(solution)/shard_map/pallas_call | solution.py:29
  42.2 1.9 %collective-permute-done.8.refs_1_ = f32[64,512]{1,0:T(8,128)S(1)} collective-permute-done((f32[64,512]{1,0:T(8,128)S(1)}, f32[64,512]{1,0:T(8,128)S(1)}, u32[]{:S(2)}, u32[]{:S(2)}) %collective-permute-start.8) | collective-permute-done | bytes 131104 | tf_op jit(solution)/shard_map/ppermute | solution.py:341
  44.1 0.8 %shard_map.46.refs_2_ = f32[1024,128]{1,0:T(8,128)} custom-call(f32[64,512]{1,0:T(8,128)S(1)} %get-tuple-element.41.refs_0_, f32[64,512]{1,0:T(8,128)S(1)} %collective-permute-done.8.refs_1_), custom_call_target="tpu_custom_call" | custom-call | tf_op jit(solution)/shard_map/pallas_call | solution.py:314
  44.9 1.2 %collective-permute-done.7.refs_1_ = f32[64,512]{1,0:T(8,128)S(1)} collective-permute-done((f32[64,512]{1,0:T(8,128)S(1)}, f32[64,512]{1,0:T(8,128)S(1)}, u32[]{:S(2)}, u32[]{:S(2)}) %collective-permute-start.7) | collective-permute-done | bytes 131104 | tf_op jit(solution)/shard_map/ppermute | solution.py:341
  46.1 0.8 %shard_map.47 = f32[1024,128]{1,0:T(8,128)} custom-call(f32[64,512]{1,0:T(8,128)S(1)} %get-tuple-element.39.refs_0_, f32[64,512]{1,0:T(8,128)S(1)} %collective-permute-done.7.refs_1_, f32[1024,128]{1,0:T(8,128)} %shard_map.46.refs_2_), custom_call_target="tpu_custom_call", output_to_operand_aliasing={{}: (2, {})} | custom-call | tf_op jit(solution)/shard_map/pallas_call | solution.py:314
Async XLA Ops:
  0.9 5.3 %collective-permute-start = (f32[136,128]{1,0:T(8,128)S(1)}, f32[136,128]{1,0:T(8,128)S(1)}, u32[]{:S(2)}, u32[]{:S(2)}) collective-permute-start(f32[136,128]{1,0:T(8,128)S(1)} %get-tuple-element.24), channel_id=1, source_target_pairs={{0,16},{16,0},{1,17},{17,1},{2,18},{18,2},{3,19},{19,3},{4,20},{20... | collective-permute-start | bytes 208904 | tf_op jit(solution)/shard_map/ppermute | solution.py:341
  5.5 8.8 %collective-permute-start.6 = (f32[64,1024]{1,0:T(8,128)S(1)}, f32[64,1024]{1,0:T(8,128)S(1)}, u32[]{:S(2)}, u32[]{:S(2)}) collective-permute-start(f32[64,1024]{1,0:T(8,128)S(1)} %get-tuple-element.29), channel_id=1, source_target_pairs={{0,16},{16,0},{1,17},{17,1},{2,18},{18,2},{3,19},{19,3},{4,20},{20... | collective-permute-start | bytes 786440 | tf_op jit(solution)/shard_map/ppermute | solution.py:341
  6.2 5.5 %collective-permute-start.2 = (f32[136,128]{1,0:T(8,128)S(1)}, f32[136,128]{1,0:T(8,128)S(1)}, u32[]{:S(2)}, u32[]{:S(2)}) collective-permute-start(f32[136,128]{1,0:T(8,128)S(1)} %collective-permute-done.refs_0_), channel_id=1, source_target_pairs={{0,6},{1,7},{2,4},{3,5},{4,2},{5,3},{6,0},{7,1},{8,14},{9,15},{10,... | collective-permute-start | bytes 208904 | tf_op jit(solution)/shard_map/ppermute | solution.py:344
  9.2 4.3 %collective-permute-start.1 = (f32[136,128]{1,0:T(8,128)S(1)}, f32[136,128]{1,0:T(8,128)S(1)}, u32[]{:S(2)}, u32[]{:S(2)}) collective-permute-start(f32[136,128]{1,0:T(8,128)S(1)} %collective-permute-done.refs_0_), channel_id=1, source_target_pairs={{0,4},{1,5},{2,6},{3,7},{4,0},{5,1},{6,2},{7,3},{8,12},{9,13},{10,... | collective-permute-start | bytes 208904 | tf_op jit(solution)/shard_map/ppermute | solution.py:344
  9.7 4.3 %collective-permute-start.4 = (f32[136,128]{1,0:T(8,128)S(1)}, f32[136,128]{1,0:T(8,128)S(1)}, u32[]{:S(2)}, u32[]{:S(2)}) collective-permute-start(f32[136,128]{1,0:T(8,128)S(1)} %collective-permute-done.refs_0_), channel_id=1, source_target_pairs={{0,2},{1,3},{2,0},{3,1},{4,6},{5,7},{6,4},{7,5},{8,10},{9,11},{10,... | collective-permute-start | bytes 208904 | tf_op jit(solution)/shard_map/ppermute | solution.py:344
  13.7 1.7 %collective-permute-start.3 = (f32[3,136,128]{2,1,0:T(8,128)S(1)}, f32[3,136,128]{2,1,0:T(8,128)S(1)}, u32[]{:S(2)}, u32[]{:S(2)}) collective-permute-start(f32[3,136,128]{2,1,0:T(8,128)S(1)} %shard_map.38.refs_0_), channel_id=1, source_target_pairs={{0,1},{1,0},{2,3},{3,2},{4,5},{5,4},{6,7},{7,6},{8,9},{9,8},{10,11... | collective-permute-start | bytes 626696 | tf_op jit(solution)/shard_map/ppermute | solution.py:344
  14.1 1.3 %collective-permute-start.5 = (f32[1,136,128]{2,1,0:T(8,128)S(1)}, f32[1,136,128]{2,1,0:T(8,128)S(1)}, u32[]{:S(2)}, u32[]{:S(2)}) collective-permute-start(f32[1,136,128]{2,1,0:T(8,128)S(1)} %shard_map.39.refs_2_), channel_id=1, source_target_pairs={{0,1},{1,0},{2,3},{3,2},{4,5},{5,4},{6,7},{7,6},{8,9},{9,8},{10,11... | collective-permute-start | bytes 208904 | tf_op jit(solution)/shard_map/ppermute | solution.py:344
  38.2 5.9 %collective-permute-start.8 = (f32[64,512]{1,0:T(8,128)S(1)}, f32[64,512]{1,0:T(8,128)S(1)}, u32[]{:S(2)}, u32[]{:S(2)}) collective-permute-start(f32[64,512]{1,0:T(8,128)S(1)} %get-tuple-element.42), channel_id=1, source_target_pairs={{0,16},{16,0},{1,17},{17,1},{2,18},{18,2},{3,19},{19,3},{4,20},{20... | collective-permute-start | bytes 393224 | tf_op jit(solution)/shard_map/ppermute | solution.py:341
  40.2 5.9 %collective-permute-start.7 = (f32[64,512]{1,0:T(8,128)S(1)}, f32[64,512]{1,0:T(8,128)S(1)}, u32[]{:S(2)}, u32[]{:S(2)}) collective-permute-start(f32[64,512]{1,0:T(8,128)S(1)} %get-tuple-element.40), channel_id=1, source_target_pairs={{0,16},{16,0},{1,17},{17,1},{2,18},{18,2},{3,19},{19,3},{4,20},{20... | collective-permute-start | bytes 393224 | tf_op jit(solution)/shard_map/ppermute | solution.py:341
